TPU v7x, 32 devices: a whole 2x2x4 slice. The times are simulated.
32 devices in a mesh: frame: 4 (over x, core), patch: 8 (over z, y).
Axes of the slice: x: 2, y: 2, z: 4, core: 2. Of those that a mesh axis runs over, the one named last changes fastest.
Arguments:
- tokens: bfloat16 [16, 256, 1152], P(None, ('frame', 'patch')), may hold values from -6 to 6
- image_mask: int32 [16, 256], P(None, ('frame', 'patch')), may hold values from 0 to 1, as said below
- sample_index: int32 [16, 256], P(None, ('frame', 'patch')), may hold values from 0 to 31, as said below
- condition: bfloat16 [32, 1152], replicated, may hold values from -6 to 6
- ada_weight: bfloat16 [1152, 6912], P('patch'), may hold values from -0.1875 to 0.1875
- ada_bias: bfloat16 [6912], replicated, may hold values from -1.75 to 1.75
- qkv_weight: bfloat16 [1152, 3456], P('patch'), may hold values from -0.1875 to 0.1875
- qkv_bias: bfloat16 [2304], replicated, may hold values from -1.75 to 1.75
- proj_weight: bfloat16 [1152, 1152], P('patch'), may hold values from -0.375 to 0.375
- proj_bias: bfloat16 [1152], replicated, may hold values from -1.75 to 1.75
- fc1_weight: bfloat16 [1152, 4608], P('patch'), may hold values from -0.1875 to 0.1875
- fc1_bias: bfloat16 [4608], replicated, may hold values from -1.75 to 1.75
- fc2_weight: bfloat16 [4608, 1152], P('patch'), may hold values from -0.09375 to 0.09375
- fc2_bias: bfloat16 [1152], replicated, may hold values from -1.75 to 1.75
- cotangent: bfloat16 [16, 256, 1152], P(None, ('frame', 'patch')), may hold values from -6 to 6
Outputs:
- output: bfloat16 [16, 256, 1152], P(None, ('frame', 'patch'))
- input_grad: float32 [16, 256, 1152], P(None, ('frame', 'patch'))
- condition_grad: float32 [32, 1152], P(None, 'patch')
- ada_weight_grad: float32 [1152, 6912], P('patch')
- ada_bias_grad: float32 [6912], replicated
- qkv_weight_grad: float32 [1152, 3456], P('patch', 'frame')
- qkv_bias_grad: float32 [2304], replicated
- proj_weight_grad: float32 [1152, 1152], P('patch', 'frame')
- proj_bias_grad: float32 [1152], replicated
- fc1_weight_grad: float32 [1152, 4608], P('patch', 'frame')
- fc1_bias_grad: float32 [4608], replicated
- fc2_weight_grad: float32 [4608, 1152], P('patch', 'frame')
- fc2_bias_grad: float32 [1152], replicated
Inputs may be any that keep to these rules, and one draw needn't show every extreme that they name: `image_mask`: all 16 tokens of a patch column share the mask; at least one column is an image column. `sample_index`: all tokens of a clip column carry one index below 16; in an image column the token at frame slot f carries 16 + f.
All inputs are finite; a program needn't handle non-finite values.
Results may differ from a plain program's by a relative error of at most 0.018.
Values may be sent and summed in bfloat16 or wider, within the bound.
No kernel may reach another device: no remote copies, remote signals or barrier semaphores. Data moves between devices by JAX's collectives and lax.ppermute only.
A program may use at most 192 MiB of HBM per device.

v0:
```python
import functools

import jax
import jax.numpy as jnp
from jax import lax
from jax.experimental import pallas as pl
from jax.experimental.pallas import tpu as pltpu
from jax.sharding import Mesh, PartitionSpec as P

HEAD_DIM = 72
EPSILON = 1e-06
SCORE_SCALE = HEAD_DIM**-0.5
GELU_C = 0.7978845608028654
GELU_A = 0.044715
VMEM_BYTES = 56 * 1024 * 1024
(AT_F, AT_Y, AT_Z, AT_P, AT_G) = range(5)
AT_PART, AT_SLOT, AT_SHARD, AT_PIECE, TABLE = 8, 16, 24, 32, 40
BF = jnp.bfloat16
F32 = jnp.float32


def mm(a, b, ca=1, cb=0):
    return lax.dot_general(a, b, (((ca,), (cb,)), ((), ())), preferred_element_type=F32)


def normalize(values):
    centred = values - jnp.mean(values, axis=-1, keepdims=True)
    inverse = lax.rsqrt(jnp.mean(centred * centred, axis=-1, keepdims=True) + EPSILON)
    return centred * inverse, inverse


def normalize_back(grad_normed, normed, inverse):
    return inverse * (
        grad_normed
        - jnp.mean(grad_normed, axis=-1, keepdims=True)
        - normed * jnp.mean(grad_normed * normed, axis=-1, keepdims=True)
    )


def stack_rows(pieces):
    if pieces[0].shape[0] % 16 == 0:
        return jnp.concatenate(pieces, axis=0)
    return jnp.concatenate([piece.astype(F32) for piece in pieces], axis=0).astype(pieces[0].dtype)


def softmax_prob(queries, key_rows, same_column):
    grid = mm(queries, key_rows, 1, 1) * SCORE_SCALE
    grid = jnp.where(same_column, grid, -1e30)
    expanded = jnp.exp(grid - jnp.max(grid, axis=-1, keepdims=True))
    return expanded / jnp.sum(expanded, axis=-1, keepdims=True)


def column_mask(tokens_per_part, columns):
    rows = lax.broadcasted_iota(jnp.int32, (tokens_per_part, tokens_per_part), 0)
    cols = lax.broadcasted_iota(jnp.int32, (tokens_per_part, tokens_per_part), 1)
    return lax.rem(rows, columns) == lax.rem(cols, columns)


def slab_attention(refs, order, size):
    pieces = []
    for ref, swapped in zip(refs, order):
        piece = ref[...]
        if swapped:
            piece = jnp.concatenate([piece[:, size:], piece[:, :size]], axis=1)
        pieces.append(piece)
    return stack_rows(pieces)


def general_attend_kernel(d, width, columns, tok_ref, sel_ref, mod_ref, w_ref, bias_ref, out_ref, qkv_ref):
    normed, _ = normalize(tok_ref[...].astype(F32))
    sel = sel_ref[...]
    shift = mm(sel, mod_ref[:, 0:d])
    scale = mm(sel, mod_ref[:, d : 2 * d])
    attn_in = (normed * (1.0 + scale) + shift).astype(BF)
    qkv = (mm(attn_in, w_ref[...]) + bias_ref[...]).astype(BF)
    qkv_ref[...] = qkv
    size = tok_ref.shape[0] // 2
    same = column_mask(size, columns)
    for half in range(2):
        rows = slice(half * size, (half + 1) * size)
        parts = []
        for head in range(width // HEAD_DIM):
            q, k, v = (
                qkv[rows, t * width + head * HEAD_DIM : t * width + (head + 1) * HEAD_DIM]
                for t in range(3)
            )
            prob = softmax_prob(q, k, same)
            parts.append(mm(prob.astype(BF), v).T)
        out_ref[:, rows] = jnp.concatenate(parts, axis=0).astype(BF)


def general_mlp_kernel(d, order, *refs):
    n = len(order)
    slots = refs[:n]
    (tok_ref, cot_ref, sel_ref, selt_ref, mod_ref, proj_ref, projb_ref, fc1_ref, fc1b_ref, fc2_ref, fc2b_ref) = refs[n : n + 11]
    (b2_ref, gm_ref, fc1g_ref, fc2g_ref, fc1bg_ref, fc2bg_ref, modg_ref, after_ref, branch_ref, fc1a, fc2a) = refs[n + 11 :]
    step = pl.program_id(0)
    size = tok_ref.shape[0] // 2
    sel = sel_ref[...]
    selt = selt_ref[...]

    def mod(block):
        return mm(sel, mod_ref[:, block * d : (block + 1) * d])

    attn_t = slab_attention(slots, order, size)
    branch_one = mm(attn_t, proj_ref[...], 0, 0) + projb_ref[...]
    after_one = tok_ref[...].astype(F32) + mod(2) * branch_one

    @pl.when(step == 0)
    def _():
        after_ref[...] = after_one[:size]
        branch_ref[...] = branch_one[:size]
        fc1a[...] = jnp.zeros_like(fc1a)
        fc2a[...] = jnp.zeros_like(fc2a)
        fc1bg_ref[...] = jnp.zeros_like(fc1bg_ref)
        fc2bg_ref[...] = jnp.zeros_like(fc2bg_ref)
        modg_ref[...] = jnp.zeros_like(modg_ref)

    normed, _ = normalize(after_one)
    mlp_in = (normed * (1.0 + mod(4)) + mod(3)).astype(BF)
    pre = mm(mlp_in, fc1_ref[...]) + fc1b_ref[...]
    square = pre * pre
    tanh = jnp.tanh(GELU_C * pre * (1.0 + GELU_A * square))
    hidden = (0.5 * pre * (1.0 + tanh)).astype(BF)
    slope = 0.5 * (1.0 + tanh) + 0.5 * pre * (1.0 - tanh * tanh) * GELU_C * (1.0 + 3.0 * GELU_A * square)
    branch_two = mm(hidden, fc2_ref[...]) + fc2b_ref[...]
    b2_ref[...] = branch_two.astype(BF).reshape(b2_ref.shape)
    grad_two = cot_ref[...].astype(F32)
    grad_branch = mod(5) * grad_two
    gb2 = grad_branch.astype(BF)
    fc2bg_ref[...] += jnp.sum(gb2.astype(F32), axis=0, keepdims=True)
    fc2a[...] += mm(hidden, gb2, 0, 0)
    grad_pre = (mm(gb2, fc2_ref[...], 1, 1) * slope).astype(BF)
    fc1bg_ref[...] += jnp.sum(grad_pre.astype(F32), axis=0, keepdims=True)
    fc1a[...] += mm(mlp_in, grad_pre, 0, 0)
    grad_in = mm(grad_pre, fc1_ref[...], 1, 1)
    gm_ref[...] = grad_in.astype(BF).reshape(gm_ref.shape)
    modg_ref[0] += mm(selt, grad_in.astype(BF))
    modg_ref[1] += mm(selt, (grad_in * normed).astype(BF))
    modg_ref[2] += mm(selt, (grad_two * branch_two).astype(BF))

    @pl.when(step == pl.num_programs(0) - 1)
    def _():
        fc1g_ref[...] = fc1a[...].astype(BF)
        fc2g_ref[...] = fc2a[...].astype(BF)


def general_middle_kernel(d, n_parts, count, place_ref, *refs):
    grads = refs[:count]
    (after_ref, branch_ref, cot_ref, sel_ref, selt_ref, mod_ref, proj_ref) = refs[count : count + 7]
    (ex_ref, one_ref, modg_ref, pbias_ref) = refs[count + 7 :]
    sel = sel_ref[...]
    grad_in = grads[0][...].astype(F32)
    for ref in grads[1:]:
        grad_in = grad_in + ref[...].astype(F32)
    normed, inverse = normalize(after_ref[...])
    scale = mm(sel, mod_ref[:, 4 * d : 5 * d])
    gate = mm(sel, mod_ref[:, 2 * d : 3 * d])
    grad_one = cot_ref[...].astype(F32) + normalize_back(grad_in * (1.0 + scale), normed, inverse)
    one_ref[...] = grad_one
    modg_ref[...] = mm(selt_ref[...], (grad_one * branch_ref[...]).astype(BF))
    gb1 = (gate * grad_one).astype(BF)
    gb1_wide = gb1.astype(F32)
    pbias_ref[...] = jnp.sum(gb1_wide, axis=0, keepdims=True)
    width = d // n_parts
    grad_attn = mm(proj_ref[...], gb1, 1, 1)
    gb1_t = gb1_wide.T
    for part in range(n_parts):
        rows = slice(part * width, (part + 1) * width)
        ex_ref[part, 0] = grad_attn[rows].astype(BF)
        ex_ref[place_ref[part], 1] = gb1_t[rows].astype(BF)


def general_attend_back_kernel(d, width, columns, order, place_ref, *refs):
    n = len(order)
    slots = refs[:n]
    (ga_ref, tok_ref, sel_ref, selt_ref, mod_ref, w_ref, qkv_ref) = refs[n : n + 7]
    (gin_ref, qkvg_ref, projg_ref, bias_ref, modg_ref, qkva, proja) = refs[n + 7 :]
    step = pl.program_id(0)
    size = tok_ref.shape[0] // 2

    @pl.when(step == 0)
    def _():
        qkva[...] = jnp.zeros_like(qkva)
        proja[...] = jnp.zeros_like(proja)
        bias_ref[...] = jnp.zeros_like(bias_ref)
        modg_ref[...] = jnp.zeros_like(modg_ref)

    qkv = qkv_ref[...]
    same = column_mask(size, columns)
    heads = width // HEAD_DIM
    halves = []
    for half in range(2):
        rows = slice(half * size, (half + 1) * size)
        grad_mixed = ga_ref[half, 0].astype(F32).T
        pieces = [None] * (3 * heads)
        for head in range(heads):
            q, k, v = (
                qkv[rows, t * width + head * HEAD_DIM : t * width + (head + 1) * HEAD_DIM]
                for t in range(3)
            )
            grad = grad_mixed[:, head * HEAD_DIM : (head + 1) * HEAD_DIM].astype(BF)
            prob = softmax_prob(q, k, same)
            grad_prob = mm(grad, v, 1, 1)
            delta = jnp.sum(prob * grad_prob, axis=-1, keepdims=True)
            grad_score = (prob * (grad_prob - delta) * SCORE_SCALE).astype(BF)
            pieces[head] = mm(grad_score, k)
            pieces[heads + head] = mm(grad_score, q, 0, 0)
            pieces[2 * heads + head] = mm(prob.astype(BF), grad, 0, 0)
        halves.append(jnp.concatenate(pieces, axis=1))
    grad_qkv = jnp.concatenate(halves, axis=0).astype(BF)
    bias_ref[...] += jnp.sum(grad_qkv.astype(F32), axis=0, keepdims=True)

    sel = sel_ref[...]
    selt = selt_ref[...]
    normed, _ = normalize(tok_ref[...].astype(F32))
    shift = mm(sel, mod_ref[:, 0:d])
    scale = mm(sel, mod_ref[:, d : 2 * d])
    attn_in = (normed * (1.0 + scale) + shift).astype(BF)
    qkva[...] += mm(attn_in, grad_qkv, 0, 0)
    grad_in = mm(grad_qkv, w_ref[...], 1, 1)
    gin_ref[...] = grad_in.astype(BF).reshape(gin_ref.shape)
    modg_ref[0] += mm(selt, grad_in.astype(BF))
    modg_ref[1] += mm(selt, (grad_in * normed).astype(BF))

    attn_t = slab_attention(slots, order, size)
    gb1_t = jnp.concatenate([ga_ref[0, 1], ga_ref[1, 1]], axis=1)
    proja[...] += mm(attn_t, gb1_t, 1, 1)

    @pl.when(step == pl.num_programs(0) - 1)
    def _():
        qkvg_ref[...] = qkva[...].astype(BF)
        rows = d // n
        for part in range(n):
            projg_ref[place_ref[part]] = proja[part * rows : (part + 1) * rows].astype(BF)


def general_last_kernel(d, count, count_b, *refs):
    grads = refs[:count]
    branches = refs[count : count + count_b]
    (tok_ref, one_ref, after_ref, cot_ref, mask_ref, sel_ref, mod_ref) = refs[count + count_b : count + count_b + 7]
    (out_ref, grad_ref) = refs[count + count_b + 7 :]
    sel = sel_ref[...]
    masked = mask_ref[...] == 1
    tokens = tok_ref[...].astype(F32)
    grad_in = grads[0][...].astype(F32)
    for ref in grads[1:]:
        grad_in = grad_in + ref[...].astype(F32)
    normed, inverse = normalize(tokens)
    scale = mm(sel, mod_ref[:, d : 2 * d])
    back = normalize_back(grad_in * (1.0 + scale), normed, inverse)
    grad_ref[...] = jnp.where(masked, cot_ref[...].astype(F32), 0.0) + one_ref[...] + back
    branch = branches[0][...].astype(F32)
    for ref in branches[1:]:
        branch = branch + ref[...].astype(F32)
    gate = mm(sel, mod_ref[:, 5 * d : 6 * d])
    out_ref[...] = jnp.where(masked, tokens, after_ref[...] + gate * branch).astype(BF)


def params(steps=1):
    return pltpu.CompilerParams(vmem_limit_bytes=VMEM_BYTES, dimension_semantics=("arbitrary",) * steps)


def cost(flops, bytes_accessed):
    return pl.CostEstimate(flops=int(flops), bytes_accessed=int(bytes_accessed), transcendentals=0)


def whole(shape):
    return pl.BlockSpec(shape, lambda *_: (0,) * len(shape))


def matchings(frames):
    left = {f: {t: (frames * t + f) // 3 for t in range(3)} for f in range(frames)}
    rounds = []
    for _ in range(3):
        taken = {}

        def place(f, seen):
            for t, to in left[f].items():
                if to in seen:
                    continue
                seen.add(to)
                if to not in taken or place(taken[to][0], seen):
                    taken[to] = (f, t)
                    return True
            return False

        for f in range(frames):
            place(f, set())
        chosen = {f: (t, to) for to, (f, t) in taken.items()}
        for f, (t, _to) in chosen.items():
            del left[f][t]
        rounds.append(chosen)
    return rounds


def general_solution(mesh):
    F, N = mesh.shape["frame"], mesh.shape["patch"]
    C, Y = 2, 2
    X, Z = F // C, N // Y
    G = X * C * Y
    half_slots = X * Y
    grid = Mesh(mesh.devices.reshape(X, C, Z, Y), ("x", "core", "z", "y"))
    everywhere = ("x", "core", "z", "y")
    offsets = [(dc, dx, dy) for dc in range(C) for dx in range(X) for dy in range(Y)]

    def from_xy(a, dx, dy):
        if dx == 0 and dy == 0:
            return a
        pairs = [
            (x * Y + y, ((x - dx) % X) * Y + (y - dy) % Y) for x in range(X) for y in range(Y)
        ]
        return lax.ppermute(a, ("x", "y"), pairs)

    def to_xy(a, dx, dy):
        return from_xy(a, (-dx) % X, (-dy) % Y)

    def swap_core(a):
        return lax.ppermute(a, "core", [(0, 1), (1, 0)])

    def swap_y(a):
        return lax.ppermute(a, "y", [(0, 1), (1, 0)])

    def gather_slots(a):
        mine = [from_xy(a, dx, dy) for dx in range(X) for dy in range(Y)]
        return mine + [swap_core(piece) for piece in mine]

    def scatter_sum(slots):
        received = swap_core(slots[half_slots:])
        terms = []
        for slot in range(half_slots):
            total = slots[slot].astype(F32) + received[slot].astype(F32)
            terms.append(to_xy(total.astype(BF), slot // Y, slot % Y))
        return terms

    def exchange(slots):
        received = swap_core(slots[half_slots:])
        pieces = [None] * G
        for slot in range(half_slots):
            dx, dy = slot // Y, slot % Y
            pair = to_xy(jnp.stack([slots[slot], received[slot]]), dx, dy)
            source = ((-dx) % X) * Y + (-dy) % Y
            pieces[source] = pair[0]
            pieces[half_slots + source] = pair[1]
        return jnp.stack(pieces)

    def local(tokens, image_mask, sample_index, condition, ada_weight, ada_bias, qkv_weight, qkv_bias,
              proj_weight, proj_bias, fc1_weight, fc1_bias, fc2_weight, fc2_bias, cotangent):
        frames, columns, d = tokens.shape
        T = frames * columns
        S = G * T
        samples = condition.shape[0]
        rows_here = ada_weight.shape[0]
        ff = fc1_weight.shape[1]
        width = d // G
        unit = ff // (N * F)
        part_ff = Z * unit
        x_i, c_i = lax.axis_index("x"), lax.axis_index("core")
        z_i, y_i = lax.axis_index("z"), lax.axis_index("y")
        f_i = x_i * C + c_i
        p_i = z_i * Y + y_i
        g_i = f_i * Y + y_i
        parts_at = [
            (((x_i + dx) % X) * C + (c_i + dc) % C) * Y + (y_i + dy) % Y for dc, dx, dy in offsets
        ]
        parts_at = jnp.stack(parts_at).astype(jnp.int32)
        all_parts = jnp.arange(G, dtype=jnp.int32)
        part_x, part_c, part_y = all_parts // (C * Y), (all_parts // Y) % C, all_parts % Y
        place = ((part_c - c_i) % C) * half_slots + ((part_x - x_i) % X) * Y + (part_y - y_i) % Y
        place = place.astype(jnp.int32)

        def y_pair(own, other):
            got = swap_y(other)
            return jnp.where(y_i == 0, jnp.stack([own, got]), jnp.stack([got, own]))

        pair_width = Y * width
        qkv_cols = [
            lax.dynamic_slice_in_dim(qkv_weight, t * d + f_i * pair_width, pair_width, 1) for t in range(3)
        ]

        def qkv_for(which):
            return jnp.concatenate(
                [lax.dynamic_slice_in_dim(c, which * width, width, 1) for c in qkv_cols], axis=1
            )

        qkv_rows = y_pair(qkv_for(y_i), qkv_for(1 - y_i)).reshape(Y * rows_here, 3 * width)
        w_qkv = lax.all_gather(qkv_rows, "z", axis=0, tiled=True)
        half_rows = rows_here // C
        proj_half = lax.dynamic_slice_in_dim(proj_weight, c_i * half_rows, half_rows, 0)
        proj_rows = y_pair(proj_half, proj_half).reshape(Y * half_rows, d)
        proj_mine = lax.all_gather(proj_rows, "z", axis=0, tiled=True)
        proj_other = swap_core(proj_mine)
        proj_both = jnp.where(
            c_i == 0, jnp.stack([proj_mine, proj_other]), jnp.stack([proj_other, proj_mine])
        )
        proj_parts = (
            proj_both.reshape(C, N, half_rows, d).transpose(1, 0, 2, 3).reshape(G, width, d)
        )
        proj_rel = jnp.concatenate(
            [lax.dynamic_index_in_dim(proj_parts, parts_at[r], 0, keepdims=False) for r in range(G)],
            axis=0,
        )

        def fc1_for(which):
            return jnp.concatenate(
                [
                    lax.dynamic_slice_in_dim(
                        fc1_weight, (z * Y + which) * (F * unit) + f_i * unit, unit, 1
                    )
                    for z in range(Z)
                ],
                axis=1,
            )

        fc1_rows = y_pair(fc1_for(y_i), fc1_for(1 - y_i)).reshape(Y * rows_here, part_ff)
        w_fc1 = lax.all_gather(fc1_rows, "z", axis=0, tiled=True)
        fc2_rows = lax.dynamic_slice_in_dim(fc2_weight, f_i * unit, unit, 0)
        w_fc2 = lax.all_gather(fc2_rows, "z", axis=0, tiled=True)

        chunk = samples * 6 * d // (F * N)
        per_row = 6 * d // chunk
        frame_samples = samples // F
        first_row = p_i * rows_here
        cond_rows = lax.dynamic_slice_in_dim(condition, first_row, rows_here, 1).astype(F32)
        sigmoid = 1.0 / (1.0 + jnp.exp(-cond_rows))
        act_rows = (cond_rows * sigmoid).astype(BF)
        silu_slope = sigmoid * (1.0 + cond_rows * (1.0 - sigmoid))
        act_mine = lax.dynamic_slice_in_dim(act_rows, f_i * frame_samples, frame_samples, 0)
        partial_mod = mm(act_mine, ada_weight).reshape(N, chunk)
        mod_terms = lax.all_to_all(partial_mod, ("z", "y"), 0, 0, tiled=True)
        bias_here = lax.dynamic_slice_in_dim(ada_bias, (p_i % per_row) * chunk, chunk, 0)
        mod_chunk = (jnp.sum(mod_terms, axis=0) + bias_here.astype(F32)).astype(BF)
        mod = lax.all_to_all(
            jnp.broadcast_to(mod_chunk, (F * N, chunk)), everywhere, 0, 0, tiled=True
        ).reshape(samples, 6 * d)

        flat_tokens = tokens.reshape(T, d)
        flat_cot = cotangent.reshape(T, d)
        mask = image_mask.reshape(T, 1)
        grad_two_own = jnp.where(mask == 1, jnp.zeros_like(flat_cot), flat_cot)
        codes = jnp.zeros((16, d), BF).at[0, :T].set(sample_index.reshape(T).astype(BF))
        token_slots = gather_slots(jnp.concatenate([flat_tokens, codes], axis=0))
        slab_tokens = jnp.concatenate([piece[:T] for piece in token_slots], axis=0)
        slab_codes = jnp.stack([piece[T, :T] for piece in token_slots]).astype(jnp.int32)
        slab_cot = jnp.concatenate(gather_slots(grad_two_own), axis=0)
        numbers = jnp.arange(samples, dtype=jnp.int32)
        selt = (slab_codes.reshape(1, S) == numbers[:, None]).astype(BF)
        sel = (slab_codes.reshape(S, 1) == numbers[None, :]).astype(BF)
        sel_own, selt_own = sel[:T], selt[:, :T]

        steps = G // 2
        TB = 2 * T
        row_block = lambda w: pl.BlockSpec((TB, w), lambda j: (j, 0))
        lane_block = lambda h: pl.BlockSpec((h, TB), lambda j: (0, j))

        bias_q = lax.dynamic_slice_in_dim(qkv_bias, g_i * width, width, 0)
        bias_v = lax.dynamic_slice_in_dim(qkv_bias, d + g_i * width, width, 0)
        bias_qkv = jnp.concatenate([bias_q, jnp.zeros_like(bias_q), bias_v]).astype(F32)[None]
        attn_t, qkv = pl.pallas_call(
            functools.partial(general_attend_kernel, d, width, columns),
            grid=(steps,),
            in_specs=[
                row_block(d),
                row_block(samples),
                whole((samples, 6 * d)),
                whole((d, 3 * width)),
                whole((1, 3 * width)),
            ],
            out_specs=[lane_block(width), row_block(3 * width)],
            out_shape=[
                jax.ShapeDtypeStruct((width, S), BF),
                jax.ShapeDtypeStruct((S, 3 * width), BF),
            ],
            compiler_params=params(),
            cost_estimate=cost(2 * S * d * 3 * width * 2, 8e6),
            name="attend",
        )(slab_tokens, sel, mod, w_qkv, bias_qkv)

        attn_slots = gather_slots(attn_t)
        order = [dy == 1 for _, _, dy in offsets]

        def slot_spec(dc, dx):
            return pl.BlockSpec(
                (width, TB),
                lambda j: (0, ((j // X + C - dc) % C) * X + (j % X + X - dx) % X),
            )

        slot_specs = [slot_spec(dc, dx) for dc, dx, _ in offsets]

        hidden_at = lambda v: jnp.concatenate(
            [
                lax.dynamic_slice_in_dim(v, (z * Y + y_i) * (F * unit) + f_i * unit, unit, 0)
                for z in range(Z)
            ]
        )
        fc1_bias_part = hidden_at(fc1_bias).astype(F32)[None]
        fc2_bias_once = jnp.where(g_i == 0, fc2_bias.astype(F32), 0.0)[None]
        slot_out = pl.BlockSpec((2, T, d), lambda j: (j, 0, 0))
        (b2_slots, gm_slots, fc1g, fc2g, fc1_bias_g, fc2_bias_g, modg_two, after_own, branch_own) = pl.pallas_call(
            functools.partial(general_mlp_kernel, d, order),
            grid=(steps,),
            in_specs=slot_specs
            + [
                row_block(d),
                row_block(d),
                row_block(samples),
                lane_block(samples),
                whole((samples, 6 * d)),
                whole((d, d)),
                whole((1, d)),
                whole((d, part_ff)),
                whole((1, part_ff)),
                whole((part_ff, d)),
                whole((1, d)),
            ],
            out_specs=[
                slot_out,
                slot_out,
                whole((d, part_ff)),
                whole((part_ff, d)),
                whole((1, part_ff)),
                whole((1, d)),
                whole((3, samples, d)),
                whole((T, d)),
                whole((T, d)),
            ],
            out_shape=[
                jax.ShapeDtypeStruct((G, T, d), BF),
                jax.ShapeDtypeStruct((G, T, d), BF),
                jax.ShapeDtypeStruct((d, part_ff), BF),
                jax.ShapeDtypeStruct((part_ff, d), BF),
                jax.ShapeDtypeStruct((1, part_ff), F32),
                jax.ShapeDtypeStruct((1, d), F32),
                jax.ShapeDtypeStruct((3, samples, d), F32),
                jax.ShapeDtypeStruct((T, d), F32),
                jax.ShapeDtypeStruct((T, d), F32),
            ],
            scratch_shapes=[pltpu.VMEM((d, part_ff), F32), pltpu.VMEM((part_ff, d), F32)],
            compiler_params=params(),
            cost_estimate=cost(2 * S * (d * d + 6 * d * part_ff), 3e7),
            name="mlp",
        )(
            *attn_slots,
            slab_tokens,
            slab_cot,
            sel,
            selt,
            mod,
            proj_rel,
            proj_bias.astype(F32)[None],
            w_fc1,
            fc1_bias_part,
            w_fc2,
            fc2_bias_once,
        )

        fc1_z = lax.psum_scatter(fc1g, "z", scatter_dimension=0, tiled=True)
        fc2_z = lax.psum_scatter(fc2g, "z", scatter_dimension=0, tiled=True)
        gm_terms = scatter_sum(gm_slots)

        ex_slots, grad_one, modg_gate, proj_bias_g = pl.pallas_call(
            functools.partial(general_middle_kernel, d, G, len(gm_terms)),
            grid_spec=pltpu.PrefetchScalarGridSpec(
                num_scalar_prefetch=1,
                grid=(1,),
                in_specs=[whole((T, d))] * len(gm_terms)
                + [
                    whole((T, d)),
                    whole((T, d)),
                    whole((T, d)),
                    whole((T, samples)),
                    whole((samples, T)),
                    whole((samples, 6 * d)),
                    whole((d, d)),
                ],
                out_specs=[
                    whole((G, 2, width, T)),
                    whole((T, d)),
                    whole((samples, d)),
                    whole((1, d)),
                ],
            ),
            out_shape=[
                jax.ShapeDtypeStruct((G, 2, width, T), BF),
                jax.ShapeDtypeStruct((T, d), F32),
                jax.ShapeDtypeStruct((samples, d), F32),
                jax.ShapeDtypeStruct((1, d), F32),
            ],
            compiler_params=params(),
            cost_estimate=cost(4 * T * d * d, 8e6),
            name="middle",
        )(place, *gm_terms, after_own, branch_own, grad_two_own, sel_own, selt_own, mod, proj_rel)

        grad_attn = exchange(ex_slots)
        b2_terms = scatter_sum(b2_slots)

        slot_back = [
            pl.BlockSpec(spec.block_shape, lambda j, place, spec=spec: spec.index_map(j))
            for spec in slot_specs
        ]
        rows_b = lambda w: pl.BlockSpec((TB, w), lambda j, place: (j, 0))
        gin_slots, qkvg, projg, qkv_bias_part, modg_one = pl.pallas_call(
            functools.partial(general_attend_back_kernel, d, width, columns, order),
            grid_spec=pltpu.PrefetchScalarGridSpec(
                num_scalar_prefetch=1,
                grid=(steps,),
                in_specs=slot_back
                + [
                    pl.BlockSpec((2, 2, width, T), lambda j, place: (j, 0, 0, 0)),
                    rows_b(d),
                    rows_b(samples),
                    pl.BlockSpec((samples, TB), lambda j, place: (0, j)),
                    whole((samples, 6 * d)),
                    whole((d, 3 * width)),
                    rows_b(3 * width),
                ],
                out_specs=[
                    pl.BlockSpec((2, T, d), lambda j, place: (j, 0, 0)),
                    whole((d, 3 * width)),
                    whole((G, width, width)),
                    whole((1, 3 * width)),
                    whole((2, samples, d)),
                ],
                scratch_shapes=[
                    pltpu.VMEM((d, 3 * width), F32),
                    pltpu.VMEM((d, width), F32),
                ],
            ),
            out_shape=[
                jax.ShapeDtypeStruct((G, T, d), BF),
                jax.ShapeDtypeStruct((d, 3 * width), BF),
                jax.ShapeDtypeStruct((G, width, width), BF),
                jax.ShapeDtypeStruct((1, 3 * width), F32),
                jax.ShapeDtypeStruct((2, samples, d), F32),
            ],
            compiler_params=params(),
            cost_estimate=cost(2 * S * d * 8 * width, 1.2e7),
            name="attend_back",
        )(parts_at, *attn_slots, grad_attn, slab_tokens, sel, selt, mod, w_qkv, qkv)

        gin_terms = scatter_sum(gin_slots)

        bias_total = 2 * d + d + ff + d
        biases = jnp.zeros((bias_total,), F32)
        put = lax.dynamic_update_slice_in_dim
        biases = put(biases, qkv_bias_part[0, :width], g_i * width, 0)
        biases = put(biases, qkv_bias_part[0, 2 * width :], d + g_i * width, 0)
        biases = put(biases, proj_bias_g[0], 2 * d, 0)
        for z in range(Z):
            biases = put(
                biases,
                fc1_bias_g[0, z * unit : (z + 1) * unit],
                3 * d + (z * Y + y_i) * (F * unit) + f_i * unit,
                0,
            )
        biases = put(biases, jnp.where(g_i == 0, fc2_bias_g[0], 0.0), 3 * d + ff, 0)
        mod_sums = jnp.concatenate(
            [modg_one[0], modg_one[1], modg_gate, modg_two[0], modg_two[1], modg_two[2]], axis=1
        )
        to_sum = jnp.concatenate(
            [mod_sums.reshape(F * N, chunk), biases.reshape(F * N, bias_total // (F * N))], axis=1
        ).astype(BF)
        terms = lax.all_to_all(to_sum, everywhere, 0, 0, tiled=True)
        summed = jnp.sum(terms.astype(F32), axis=0).astype(BF)
        total = lax.all_to_all(
            jnp.broadcast_to(summed, (F * N, summed.shape[0])), everywhere, 0, 0, tiled=True
        )
        mod_grad = total[:, :chunk].reshape(samples, 6 * d)
        bias_grad = total[:, chunk:].reshape(bias_total).astype(F32)
        ada_bias_grad = jnp.sum(mod_grad.astype(F32), axis=0)
        ada_weight_grad = mm(act_rows, mod_grad, 0, 0)
        condition_grad = mm(mod_grad, ada_weight, 1, 1) * silu_slope

        def y_join(rows):
            kept = lax.dynamic_index_in_dim(rows, y_i, 0, keepdims=False)
            got = swap_y(lax.dynamic_index_in_dim(rows, 1 - y_i, 0, keepdims=False))
            return jnp.where(y_i == 0, jnp.stack([kept, got]), jnp.stack([got, kept]))

        attn_g = jnp.concatenate([qkvg, projg.reshape(d, width)], axis=1)
        attn_z = lax.psum_scatter(attn_g, "z", scatter_dimension=0, tiled=True)
        attn_y = y_join(attn_z.reshape(Y, rows_here, 4 * width))
        blocks = jnp.stack(
            [
                jnp.concatenate([attn_y[y, :, t * width : (t + 1) * width] for y in range(Y)], axis=1)
                for t in range(4)
            ]
        )
        proj_weight_grad = blocks[3].astype(F32)
        moved = [None] * 3
        spots = jnp.zeros((3, F), jnp.int32)
        for turn, chosen in enumerate(matchings(F)):
            picks = jnp.array([chosen[f][0] for f in range(F)], jnp.int32)
            block = lax.dynamic_index_in_dim(blocks, picks[f_i], 0, keepdims=False)
            pairs = [(f, chosen[f][1]) for f in range(F)]
            if any(a != b for a, b in pairs):
                block = lax.ppermute(block, ("x", "core"), pairs)
            moved[turn] = block
            for f in range(F):
                t, to = chosen[f]
                spots = spots.at[(F * t + f) % 3, to].set(turn)
        moved = jnp.stack(moved)
        qkv_weight_grad = jnp.concatenate(
            [
                lax.dynamic_index_in_dim(moved, spots[k, f_i], 0, keepdims=False)
                for k in range(3)
            ],
            axis=1,
        ).astype(F32)

        fc1_y = y_join(fc1_z.reshape(Y, rows_here, part_ff))
        per_frame = Z // F
        fc1_send = fc1_y.reshape(Y, rows_here, F, per_frame, unit).transpose(2, 1, 3, 0, 4)
        fc1_got = lax.all_to_all(fc1_send, ("x", "core"), 0, 0, tiled=True)
        fc1_weight_grad = (
            fc1_got.transpose(1, 2, 3, 0, 4).reshape(rows_here, ff // F).astype(F32)
        )
        fc2_send = fc2_z.reshape(unit, F, d // F).transpose(1, 0, 2)
        fc2_got = lax.all_to_all(fc2_send, ("x", "core"), 0, 0, tiled=True)
        fc2_weight_grad = fc2_got.reshape(F * unit, d // F).astype(F32)

        result, input_grad = pl.pallas_call(
            functools.partial(general_last_kernel, d, len(gin_terms), len(b2_terms)),
            out_shape=[jax.ShapeDtypeStruct((T, d), BF), jax.ShapeDtypeStruct((T, d), F32)],
            compiler_params=pltpu.CompilerParams(vmem_limit_bytes=VMEM_BYTES),
            cost_estimate=cost(1e6, 5e6),
            name="last",
        )(*gin_terms, *b2_terms, flat_tokens, grad_one, after_own, flat_cot, mask, sel_own, mod)

        shape = (frames, columns, d)
        return (
            result.reshape(shape),
            input_grad.reshape(shape),
            condition_grad,
            ada_weight_grad,
            ada_bias_grad,
            qkv_weight_grad,
            bias_grad[: 2 * d],
            proj_weight_grad,
            bias_grad[2 * d : 3 * d],
            fc1_weight_grad,
            bias_grad[3 * d : 3 * d + ff],
            fc2_weight_grad,
            bias_grad[3 * d + ff :],
        )

    frame, patch = ("x", "core"), ("z", "y")
    every = ("x", "core", "z", "y")
    token_spec = P(None, every, None)
    number_spec = P(None, every)
    row_spec = P(patch, None)
    both_spec = P(patch, frame)
    return jax.shard_map(
        local,
        mesh=grid,
        in_specs=(
            token_spec, number_spec, number_spec, P(), row_spec, P(), row_spec, P(), row_spec, P(), row_spec, P(),
            row_spec, P(), token_spec,
        ),
        out_specs=(
            token_spec, token_spec, P(None, patch), row_spec, P(), both_spec, P(), both_spec, P(), both_spec, P(),
            both_spec, P(),
        ),
        check_vma=False,
    )


def takes(microseconds):
    return pl.CostEstimate(flops=1000, bytes_accessed=1000, transcendentals=0)


def wide(lanes):
    return -(-lanes // 128) * 128


def row_of(values):
    return jnp.concatenate([values[k : k + 1] for k in range(values.shape[0])], axis=1)


def put_row(ref, row):
    for k in range(ref.shape[0]):
        ref[k : k + 1] = row[:, k * 128 : (k + 1) * 128]


def pick(index, options):
    total = jnp.where(index == 0, options[0], 0.0)
    for k in range(1, len(options)):
        total = total + jnp.where(index == k, options[k], 0.0)
    return total


def spread(values, index, n):
    return jnp.concatenate([jnp.where(index == k, values, 0.0) for k in range(n)], axis=1)


def at_rows(index, rows):
    return pl.ds(pl.multiple_of(index * rows, rows), rows)


def prepare_kernel(d, place, cond_ref, ada_ref, qkv_ref, fc1_ref, proj_ref, fc2_ref, tok_ref, cot_ref, num_ref, mask_ref,
                   part_ref, act_ref, slope_ref, qkv_mine, fc1_mine, send_out, fc2_out, tok_out, act_all):
    rows = ada_ref.shape[0]
    cols = 2 * rows
    for ref in (qkv_mine, fc1_mine, send_out, fc2_out):
        ref[...] = jnp.zeros_like(ref)
    act_ref[...] = jnp.zeros_like(act_ref)
    slope_ref[...] = jnp.zeros_like(slope_ref)
    for f in range(4):

        @pl.when(place[AT_F] == f)
        def _():
            fc2_out[:, d : d + cols] = proj_ref[:, f * cols : (f + 1) * cols]
            for y in range(2):
                for q_out, at_q, f_out, want in ((qkv_mine, 0, fc1_mine, y), (send_out, wide(4 * rows), send_out, 1 - y)):

                    @pl.when(place[AT_Y] == want)
                    def _():
                        for t in range(3):
                            at = t * d + (2 * f + y) * rows
                            q_out[:, at_q + t * rows : at_q + (t + 1) * rows] = qkv_ref[:, at : at + rows]
                        for z in range(4):
                            at = ((z * 2 + y) * 4 + f) * rows
                            f_out[:, z * rows : (z + 1) * rows] = fc1_ref[:, at : at + rows]

    fc2_out[:, :d] = fc2_ref[at_rows(place[AT_F], rows)]
    row = lax.broadcasted_iota(jnp.int32, (d, rows), 0)
    col = lax.broadcasted_iota(jnp.int32, (d, rows), 1)
    cond = mm(cond_ref[...], (row == col + place[AT_P] * rows).astype(BF))
    sigmoid = 1.0 / (1.0 + jnp.exp(-cond))
    act = cond * sigmoid
    act_ref[:, :rows] = act.astype(BF)
    slope_ref[:, :rows] = sigmoid * (1.0 + cond * (1.0 - sigmoid))
    act_all[...] = act
    mine = act_all[at_rows(place[AT_F], 8)].astype(BF)
    for block in range(8):
        if block < 6:
            part_ref[block] = mm(mine, ada_ref[:, block * d : (block + 1) * d]).astype(BF)
        else:
            part_ref[block] = jnp.zeros(part_ref.shape[1:], BF)
    size = tok_ref.shape[0]
    columns, frames = num_ref.shape

    def token_row(ref):
        lane = lax.broadcasted_iota(jnp.int32, (frames, size), 1)
        frame = lax.broadcasted_iota(jnp.int32, (frames, size), 0)
        wide = mm(ref[...].astype(F32).astype(BF), (lane // columns == frame).astype(BF))
        lane = lax.broadcasted_iota(jnp.int32, (columns, size), 1)
        column = lax.broadcasted_iota(jnp.int32, (columns, size), 0)
        return jnp.sum(jnp.where(lax.rem(lane, columns) == column, wide, 0.0), axis=0, keepdims=True)

    tok_out[size : 2 * size] = tok_ref[...]
    tok_out[2 * size :] = jnp.zeros((16, d), BF)
    tok_out[2 * size :, :size] = jnp.broadcast_to(token_row(num_ref), (16, size)).astype(BF)
    masked = jnp.broadcast_to(token_row(mask_ref), (size, size)).T[:, 0:1]
    tok_out[:size] = jnp.where(masked > 0.5, 0.0, cot_ref[...].astype(F32)).astype(BF)


def mod_sum_kernel(place, terms_ref, bias_ref, out_ref):
    total = terms_ref[0].astype(F32)
    for k in range(1, terms_ref.shape[0]):
        total = total + terms_ref[k].astype(F32)
    bias = row_of(bias_ref[...].astype(F32))
    d = total.shape[1]
    total = total + pick(place[AT_P], [bias[:, k * d : (k + 1) * d] for k in range(6)])
    out_ref[...] = total.astype(BF)


def grad_sum_kernel(place, terms_ref, out_ref):
    total = terms_ref[0].astype(F32)
    for k in range(1, terms_ref.shape[0]):
        total = total + terms_ref[k].astype(F32)
    out_ref[...] = total.astype(BF)


def chunk_of(ref, place, chunk):
    at_z = lax.bitwise_xor(place[AT_Z], chunk // 2 % 4)
    return ref[chunk // 8 * 2 + chunk % 2, at_z]


def token_pair(near_ref, far_ref, size):
    near = pl.program_id(0) < pl.num_programs(0) // 2
    parts, codes = [], []
    for half in range(2):
        rows = slice(size, 2 * size)
        parts.append(jnp.where(near, near_ref[half, rows].astype(F32), far_ref[half, rows].astype(F32)))
        rows = slice(2 * size, 2 * size + 16)
        code = jnp.where(near, near_ref[half, rows, :size].astype(F32), far_ref[half, rows, :size].astype(F32))
        codes.append(code[0:1])
    return jnp.concatenate(parts, axis=0), codes


def attend_kernel(d, width, columns, place, tok_near, tok_far, w_in, modin_ref, bias_ref,
                  out_ref, qkv_ref, sel_ref, selt_ref, w_ref, mod_ref, bias_row):
    step = pl.program_id(0)
    samples = selt_ref.shape[0]
    size = out_ref.shape[1] // 2

    @pl.when(step == 0)
    def _():
        for z in range(4):
            for dy in range(2):
                patch = z * 2 + lax.bitwise_xor(place[AT_Y], dy)
                w_ref[at_rows(patch, width), :] = w_in[z, dy]
        for block in range(6):
            pieces = [chunk_of(modin_ref, place, f * 8 + block).astype(F32) for f in range(4)]
            mod_ref[block] = jnp.concatenate(pieces, axis=0).astype(BF)
        bias = row_of(bias_ref[...].astype(F32))
        bias_row[:, :width] = pick(place[AT_G], [bias[:, k * width : (k + 1) * width] for k in range(8)])
        bias_row[:, width : 2 * width] = jnp.zeros((1, width), F32)
        bias_row[:, 2 * width :] = pick(place[AT_G], [bias[:, d + k * width : d + (k + 1) * width] for k in range(8)])

    numbers = lax.broadcasted_iota(jnp.int32, (samples, size), 0).astype(F32)
    tokens, codes = token_pair(tok_near, tok_far, size)
    for half in range(2):
        rows = slice(half * size, (half + 1) * size)
        hot = (codes[half] == numbers).astype(F32)
        selt_ref[:, rows] = hot.astype(BF)
        sel_ref[rows, :samples] = hot.T.astype(BF)
    normed, _ = normalize(tokens)
    sel = sel_ref[:, : mod_ref.shape[1]]
    attn_in = (normed * (1.0 + mm(sel, mod_ref[1])) + mm(sel, mod_ref[0])).astype(BF)
    qkv = (mm(attn_in, w_ref[:, : 3 * width]) + bias_row[...]).astype(BF)
    qkv_ref[:, : 3 * width] = qkv
    same = column_mask(size, columns)
    for half in range(2):
        rows = slice(half * size, (half + 1) * size)
        parts = []
        for head in range(width // HEAD_DIM):
            q, k, v = (
                qkv[rows, t * width + head * HEAD_DIM : t * width + (head + 1) * HEAD_DIM]
                for t in range(3)
            )
            prob = softmax_prob(q, k, same)
            parts.append(mm(prob.astype(BF), v).T)
        out_ref[:, rows] = jnp.concatenate(parts, axis=0).astype(BF)


def proj_kernel(d, place, *refs):
    rows = d // 8
    pieces, (proj_all, columns) = refs[:8], refs[8:]
    for slot, ref in enumerate(pieces):
        columns[slot] = ref[...]
    for slot in range(8):
        part = place[AT_PART + slot]
        for f in range(4):
            source = place[AT_SLOT + f * 2 + lax.rem(part, 2)]
            proj_all[slot * rows : (slot + 1) * rows, f * 2 * rows : (f + 1) * 2 * rows] = columns[source, part // 2]


def mlp_kernel(d, order, place, *refs):
    n = len(order)
    slots = refs[:n]
    (tok_near, tok_far, sel_ref, selt_ref, mod_ref, proj_all, projb_ref, fc1_in, fc1b_ref, fc2_in, fc2b_ref) = refs[n : n + 11]
    (b2_own, b2_far, gm_own, gm_far, fcg_ref, fc1bg_ref, fc2bg_ref, modg_ref, after_ref, branch_ref) = refs[n + 11 : n + 21]
    (fc1a, fc2a, fc1_ref, fc2_ref, pb_row, f1_row, f2_row) = refs[n + 21 :]
    step = pl.program_id(0)
    size = sel_ref.shape[0] // 2
    rows = d // 8
    sel = sel_ref[:, : mod_ref.shape[1]]
    selt = selt_ref[...]

    @pl.when(step == 0)
    def _():
        for z in range(4):
            for dy in range(2):
                patch = z * 2 + lax.bitwise_xor(place[AT_Y], dy)
                fc1_ref[at_rows(patch, rows), :] = fc1_in[z, dy, :, : 4 * rows]
            fc2_ref[z * rows : (z + 1) * rows] = fc2_in[z, :, :d]
        pb_row[...] = row_of(projb_ref[...].astype(F32))
        f2_row[...] = jnp.where(place[AT_G] == 0, row_of(fc2b_ref[...].astype(F32)), 0.0)
        bias = row_of(fc1b_ref[...].astype(F32))
        for z in range(4):
            options = []
            for k in range(8):
                at = (z * 8 + k) * rows
                options.append(bias[:, at : at + rows])
            f1_row[:, z * rows : (z + 1) * rows] = pick(place[AT_Y] * 4 + place[AT_F], options)

    tokens, _ = token_pair(tok_near, tok_far, size)
    grad_two = jnp.where(step < pl.num_programs(0) // 2, tok_near[:, :size].astype(F32), tok_far[:, :size].astype(F32))
    grad_two = grad_two.reshape(2 * size, d)
    attn_t = slab_attention(slots, order, size)
    branch_one = mm(attn_t, proj_all[...], 0, 0) + pb_row[...]
    after_one = tokens + mm(sel, mod_ref[2]) * branch_one

    @pl.when(step == 0)
    def _():
        after_ref[...] = after_one[:size]
        branch_ref[...] = branch_one[:size]
        fc1a[...] = jnp.zeros_like(fc1a)
        fc2a[...] = jnp.zeros_like(fc2a)
        fc1bg_ref[...] = jnp.zeros_like(fc1bg_ref)
        fc2bg_ref[...] = jnp.zeros_like(fc2bg_ref)
        modg_ref[...] = jnp.zeros_like(modg_ref)

    normed, _ = normalize(after_one)
    mlp_in = (normed * (1.0 + mm(sel, mod_ref[4])) + mm(sel, mod_ref[3])).astype(BF)
    pre = mm(mlp_in, fc1_ref[...]) + f1_row[...]
    square = pre * pre
    tanh = jnp.tanh(GELU_C * pre * (1.0 + GELU_A * square))
    hidden = (0.5 * pre * (1.0 + tanh)).astype(BF)
    slope = 0.5 * (1.0 + tanh) + 0.5 * pre * (1.0 - tanh * tanh) * GELU_C * (1.0 + 3.0 * GELU_A * square)
    branch_two = mm(hidden, fc2_ref[...]) + f2_row[...]
    gb2 = (mm(sel, mod_ref[5]) * grad_two).astype(BF)
    fc2bg_ref[...] += jnp.sum(gb2.astype(F32), axis=0, keepdims=True)
    fc2a[...] += mm(hidden, gb2, 0, 0)
    grad_pre = (mm(gb2, fc2_ref[...], 1, 1) * slope).astype(BF)
    fc1bg_ref[...] += jnp.sum(grad_pre.astype(F32), axis=0, keepdims=True)
    fc1a[...] += mm(mlp_in, grad_pre, 0, 0)
    grad_in = mm(grad_pre, fc1_ref[...], 1, 1)
    modg_ref[0] += mm(selt, grad_in.astype(BF))
    modg_ref[1] += mm(selt, (grad_in * normed).astype(BF))
    modg_ref[2] += mm(selt, (grad_two * branch_two).astype(BF))
    near = step < pl.num_programs(0) // 2

    @pl.when(near)
    def _():
        b2_own[...] = branch_two.astype(BF).reshape(b2_own.shape)
        gm_own[...] = grad_in.astype(BF).reshape(gm_own.shape)

    @pl.when(jnp.logical_not(near))
    def _():
        b2_far[...] = branch_two.astype(BF).reshape(b2_far.shape)
        gm_far[...] = grad_in.astype(BF).reshape(gm_far.shape)

    @pl.when(step == pl.num_programs(0) - 1)
    def _():
        for z in range(4):
            for y in range(2):
                at = (z * 2 + y) * rows
                to = (z * 4 + y) * rows
                fcg_ref[to : to + rows, : 4 * rows] = fc1a[at : at + rows].astype(BF)
            block = fc2a[z * rows : (z + 1) * rows].astype(BF)
            to = (z * 4 + 2) * rows
            fcg_ref[to : to + rows, : 4 * rows] = block[:, : d // 2]
            fcg_ref[to + rows : to + 2 * rows, : 4 * rows] = block[:, d // 2 :]


def middle_kernel(d, count, place, *refs):
    grads = refs[:count]
    (after_ref, branch_ref, cot_ref, sel_ref, selt_ref, mod_ref, proj_ref) = refs[count : count + 7]
    ex_refs = refs[count + 7 : count + 15]
    (one_ref, modg_ref, pbias_ref, turned) = refs[count + 15 :]
    sel = sel_ref[:, : mod_ref.shape[1]]
    grad_in = grads[0][...].astype(F32)
    for ref in grads[1:]:
        grad_in = grad_in + ref[...].astype(F32)
    normed, inverse = normalize(after_ref[...])
    scale = mm(sel, mod_ref[4])
    gate = mm(sel, mod_ref[2])
    grad_one = cot_ref[...].astype(F32) + normalize_back(grad_in * (1.0 + scale), normed, inverse)
    one_ref[...] = grad_one
    modg_ref[...] = mm(selt_ref[...], (grad_one * branch_ref[...]).astype(BF))
    gb1 = (gate * grad_one).astype(BF)
    gb1_wide = gb1.astype(F32)
    pbias_ref[...] = jnp.sum(gb1_wide, axis=0, keepdims=True)
    width = d // 8
    turned[...] = gb1_wide.T
    grad_attn = mm(proj_ref[...], gb1, 1, 1)
    for slot, ref in enumerate(ex_refs):
        ref[0] = grad_attn[slot * width : (slot + 1) * width].astype(BF)
        ref[1] = turned[at_rows(place[AT_PART + slot], width)].astype(BF)


def back_kernel(d, width, columns, place, *refs):
    n = 8
    gas = refs[:n]
    (tok_near, tok_far, sel_ref, selt_ref, mod_ref, qkv_ref, w_ref, two_ref, gate_ref, pb_ref, f1b_ref, f2b_ref) = refs[n : n + 12]
    (gin_own, gin_far, gqkv_ref, in_ref, sum_ref) = refs[n + 12 : n + 17]
    (ga_all, modg, bias_row) = refs[n + 17 :]
    step = pl.program_id(0)
    size = sel_ref.shape[0] // 2

    @pl.when(step == 0)
    def _():
        bias_row[...] = jnp.zeros_like(bias_row)
        modg[...] = jnp.zeros_like(modg)
        for k, ref in enumerate(gas):
            ga_all[k] = ref[...]

    qkv = qkv_ref[:, : 3 * width]
    same = column_mask(size, columns)
    heads = width // HEAD_DIM
    halves = []
    for half in range(2):
        rows = slice(half * size, (half + 1) * size)
        grad_mixed = ga_all[2 * step + half, 0].astype(F32).T
        pieces = [None] * (3 * heads)
        for head in range(heads):
            q, k, v = (
                qkv[rows, t * width + head * HEAD_DIM : t * width + (head + 1) * HEAD_DIM]
                for t in range(3)
            )
            grad = grad_mixed[:, head * HEAD_DIM : (head + 1) * HEAD_DIM].astype(BF)
            prob = softmax_prob(q, k, same)
            grad_prob = mm(grad, v, 1, 1)
            delta = jnp.sum(prob * grad_prob, axis=-1, keepdims=True)
            grad_score = (prob * (grad_prob - delta) * SCORE_SCALE).astype(BF)
            pieces[head] = mm(grad_score, k)
            pieces[heads + head] = mm(grad_score, q, 0, 0)
            pieces[2 * heads + head] = mm(prob.astype(BF), grad, 0, 0)
        halves.append(jnp.concatenate(pieces, axis=1))
    grad_qkv = jnp.concatenate(halves, axis=0).astype(BF)
    bias_row[...] += jnp.sum(grad_qkv.astype(F32), axis=0, keepdims=True)

    tokens, _ = token_pair(tok_near, tok_far, size)
    normed, _ = normalize(tokens)
    sel = sel_ref[:, : mod_ref.shape[1]]
    selt = selt_ref[...]
    attn_in = (normed * (1.0 + mm(sel, mod_ref[1])) + mm(sel, mod_ref[0])).astype(BF)
    in_ref[...] = attn_in
    gqkv_ref[:, : 3 * width] = grad_qkv
    grad_in = mm(grad_qkv, w_ref[:, : 3 * width], 1, 1)
    modg[0] += mm(selt, grad_in.astype(BF))
    modg[1] += mm(selt, (grad_in * normed).astype(BF))
    near = step < pl.num_programs(0) // 2

    @pl.when(near)
    def _():
        gin_own[...] = grad_in.astype(BF).reshape(gin_own.shape)

    @pl.when(jnp.logical_not(near))
    def _():
        gin_far[...] = grad_in.astype(BF).reshape(gin_far.shape)

    @pl.when(step == pl.num_programs(0) - 1)
    def _():
        blocks = [modg[0], modg[1], gate_ref[...], two_ref[0], two_ref[1], two_ref[2]]
        for k, block in enumerate(blocks):
            for group in range(4):
                sum_ref[k * 4 + group] = block[group * 8 : (group + 1) * 8].astype(BF)
        part = place[AT_G]
        rows = [
            spread(bias_row[:, :width], part, 8),
            spread(bias_row[:, 2 * width :], part, 8),
            pb_ref[...],
        ]
        at = place[AT_Y] * 4 + place[AT_F]
        rows += [spread(f1b_ref[:, z * width : (z + 1) * width], at, 8) for z in range(4)]
        rows.append(jnp.where(part == 0, f2b_ref[...], 0.0))
        sum_ref[24] = jnp.concatenate(rows, axis=0).astype(BF)
        for k in range(25, 32):
            sum_ref[k] = jnp.zeros(sum_ref.shape[1:], BF)


def weights_kernel(d, width, order, place, *refs):
    n = len(order)
    slots, gas = refs[:n], refs[n : 2 * n]
    (gqkv_ref, in_ref, grad_ref, qkva, proja, ga_all) = refs[2 * n :]
    step = pl.program_id(0)
    size = in_ref.shape[0] // 2

    @pl.when(step == 0)
    def _():
        qkva[...] = jnp.zeros_like(qkva)
        proja[...] = jnp.zeros_like(proja)
        for k, ref in enumerate(gas):
            ga_all[k] = ref[1]

    qkva[...] += mm(in_ref[...], gqkv_ref[:, : 3 * width], 0, 0)
    attn_t = slab_attention(slots, order, size)
    gb1_t = jnp.concatenate([ga_all[2 * step], ga_all[2 * step + 1]], axis=1)
    proja[...] += mm(attn_t, gb1_t, 1, 1)

    @pl.when(step == pl.num_programs(0) - 1)
    def _():
        grad_ref[:, : 3 * width] = qkva[...].astype(BF)
        grad_ref[:, 4 * width :] = jnp.zeros((d, grad_ref.shape[1] - 4 * width), BF)
        for slot in range(n):
            grad_ref[at_rows(place[AT_PART + slot], width), 3 * width : 4 * width] = proja[slot * width : (slot + 1) * width].astype(BF)


def ada_kernel(d, place, total_ref, act_ref, slope_ref, w_ref, wg_ref, cond_ref, ada_ref, qkv_ref, proj_ref, fc1_ref, fc2_ref):
    rows = wg_ref.shape[0]
    act = act_ref[:, :rows]
    cond = jnp.zeros(cond_ref.shape, F32)
    sums = []
    for block in range(6):
        grads = jnp.concatenate([chunk_of(total_ref, place, block * 4 + k).astype(F32) for k in range(4)], axis=0)
        cols = slice(block * d, (block + 1) * d)
        sums.append(jnp.sum(grads, axis=0, keepdims=True))
        grads = grads.astype(BF)
        wg_ref[:, cols] = mm(act, grads, 0, 0)
        cond = cond + mm(grads, w_ref[:, cols], 1, 1)
    cond_ref[...] = cond * slope_ref[:, :rows]
    put_row(ada_ref, jnp.concatenate(sums, axis=1))
    biases = chunk_of(total_ref, place, 24).astype(F32)
    rows = [biases[k : k + 1] for k in range(8)]
    put_row(qkv_ref, jnp.concatenate(rows[:2], axis=1))
    put_row(proj_ref, rows[2])
    put_row(fc1_ref, jnp.concatenate(rows[3:7], axis=1))
    put_row(fc2_ref, rows[7])


def mlp_split_kernel(rows, place, in_ref, *outs):
    cols = 2 * rows
    outs, full = outs[:8], outs[8]
    full[...] = jnp.zeros_like(full)
    for f in range(4):
        for y in range(2):
            slot = place[AT_SLOT + f * 2 + y]
            full[slot, :, :rows] = in_ref[y * rows : (y + 1) * rows, f * rows : (f + 1) * rows]
            part = in_ref[(2 + f // 2) * rows : (3 + f // 2) * rows, f % 2 * cols : (f % 2 + 1) * cols]
            full[slot, :, rows : 3 * rows] = jnp.where(place[AT_Y] == y, part.astype(F32), 0.0).astype(BF)
    for slot, out in enumerate(outs):
        out[...] = full[slot, :, : out.shape[1]]


def collect(full, refs):
    for slot, ref in enumerate(refs):
        full[slot, :, : ref.shape[1]] = ref[...]


def mlp_join_kernel(rows, place, *refs):
    (fc1_ref, fc2_ref, full) = refs[8:]
    collect(full, refs[:8])
    for f in range(4):
        for y in range(2):
            at = (y * 4 + f) * rows
            fc1_ref[:, at : at + rows] = full[place[AT_SLOT + f * 2 + y], :, :rows].astype(F32)
        fc2_ref[:, f * rows : (f + 1) * rows] = full[place[AT_SLOT + f * 2 + place[AT_Y]], :, rows : 3 * rows].astype(F32).T


def attn_split_kernel(rows, place, in_ref, *outs):
    outs, full = outs[:8], outs[8]
    full[...] = jnp.zeros_like(full)
    for part in range(8):

        @pl.when(place[AT_G] == part)
        def _():
            for y in range(2):
                block = in_ref[y * rows : (y + 1) * rows]
                for t in range(3):
                    to = (8 * t + part) // 6
                    full[place[AT_SLOT + to * 2 + y], :, :rows] = block[:, t * rows : (t + 1) * rows]
                full[place[AT_SLOT + part // 2 * 2 + y], :, rows : 2 * rows] = block[:, 3 * rows : 4 * rows]

    for slot, out in enumerate(outs):
        out[...] = full[slot, :, : out.shape[1]]


def attn_join_kernel(rows, place, *refs):
    (qkv_ref, proj_ref, full) = refs[8:]
    collect(full, refs[:8])
    for y in range(2):
        proj_ref[:, y * rows : (y + 1) * rows] = full[place[AT_SLOT + place[AT_F] * 2 + y], :, rows : 2 * rows].astype(F32)
    for to in range(4):

        @pl.when(place[AT_F] == to)
        def _():
            for k in range(6):
                slot = place[AT_SLOT + (6 * to + k) % 8]
                qkv_ref[:, k * rows : (k + 1) * rows] = full[slot, :, :rows].astype(F32)


def output_kernel(place, b2_0, b2_1, b2_2, b2_3, tok_ref, after_ref, mask_ref, sel_ref, mod_ref, out_ref):
    branch = b2_0[...].astype(F32)
    for ref in (b2_1, b2_2, b2_3):
        branch = branch + ref[...].astype(F32)
    gate = mm(sel_ref[:, : mod_ref.shape[1]], mod_ref[5])
    tokens = tok_ref[...].astype(F32)
    out_ref[...] = jnp.where(mask_ref[...] == 1, tokens, after_ref[...] + gate * branch).astype(BF)


def input_grad_kernel(place, gin_0, gin_1, gin_2, gin_3, tok_ref, one_ref, cot_ref, mask_ref, sel_ref, mod_ref, grad_ref):
    grad_in = gin_0[...].astype(F32)
    for ref in (gin_1, gin_2, gin_3):
        grad_in = grad_in + ref[...].astype(F32)
    normed, inverse = normalize(tok_ref[...].astype(F32))
    scale = mm(sel_ref[:, : mod_ref.shape[1]], mod_ref[1])
    back = normalize_back(grad_in * (1.0 + scale), normed, inverse)
    grad_ref[...] = jnp.where(mask_ref[...] == 1, cot_ref[...].astype(F32), 0.0) + one_ref[...] + back


def slab_solution(mesh):
    names = ("x", "core", "z", "y")
    grid = Mesh(mesh.devices.reshape(2, 2, 4, 2), names)
    offsets = [(dc, dx, dy) for dc in range(2) for dx in range(2) for dy in range(2)]
    order = [dy == 1 for _, _, dy in offsets]
    group = ("x", "core", "y")
    table = [[0] * TABLE for _ in range(32)]
    for device, row in enumerate(table):
        x, c, z, y = device >> 4, (device >> 3) & 1, (device >> 1) & 3, device & 1
        f = x * 2 + c
        row[AT_F], row[AT_Y], row[AT_Z], row[AT_P], row[AT_G] = f, y, z, device & 7, f * 2 + y
        for slot, (dc, dx, dy) in enumerate(offsets):
            part = ((x ^ dx) * 2 + (c ^ dc)) * 2 + (y ^ dy)
            row[AT_PART + slot] = part
            row[AT_SLOT + part] = slot
        for piece in range(8):
            row[AT_SHARD + piece] = (z ^ (piece >> 1)) * 2 + (y ^ (piece & 1))
        for patch in range(8):
            row[AT_PIECE + patch] = ((patch & 1) ^ y) * 4 + (patch >> 1)

    def swap(a, axes):
        n = 2 ** len(axes)
        return lax.ppermute(a, axes, [(k, n - 1 - k) for k in range(n)])

    def from_z(a, apart):
        return lax.ppermute(a, ("z",), [(z, z ^ apart) for z in range(4)])

    def over(a, dx, dy):
        axes = (("x",) if dx else ()) + (("y",) if dy else ())
        return swap(a, axes) if axes else a

    def gather_near(a):
        return [over(a, dx, dy) for dx in range(2) for dy in range(2)]

    def gather_slots(a):
        mine = gather_near(a)
        return mine + [swap(piece, ("core",)) for piece in mine]

    def over_z(a):
        return [a] + [from_z(a, apart) for apart in (1, 2, 3)]

    def to_slab(a):
        return lax.all_to_all(jnp.broadcast_to(a, (8, *a.shape)), group, 0, 0, tiled=True)

    def core_sum(own, far):
        received = swap(far, ("core",))
        return [(own[slot].astype(F32) + received[slot].astype(F32)).astype(BF) for slot in range(4)]

    def scatter_sum(own, far):
        return [over(total, slot // 2, slot % 2) for slot, total in enumerate(core_sum(own, far))]

    def exchange(slots):
        moved = []
        for slot, offset in zip(slots, offsets):
            axes = tuple(axis for axis, apart in zip(("x", "core", "y"), (offset[1], offset[0], offset[2])) if apart)
            moved.append(swap(slot, axes) if axes else slot)
        return moved

    def local(tokens, image_mask, sample_index, condition, ada_weight, ada_bias, qkv_weight, qkv_bias,
              proj_weight, proj_bias, fc1_weight, fc1_bias, fc2_weight, fc2_bias, cotangent):
        frames, columns, d = tokens.shape
        T = frames * columns
        S = 8 * T
        TB = 2 * T
        samples = condition.shape[0]
        rows = ada_weight.shape[0]
        ff = fc1_weight.shape[1]
        width = d // 8
        part_ff = ff // 8
        cols = 2 * width
        me = lax.axis_index(names).astype(jnp.uint32)
        place = lax.dynamic_slice(jnp.array(table, jnp.int32), (me, jnp.uint32(0)), (1, TABLE)).reshape(TABLE)

        def shaped(shape, dtype=F32):
            return jax.ShapeDtypeStruct(shape, dtype)

        def rows_at(w):
            return pl.BlockSpec((TB, w), lambda j, *_: (j, 0))

        def lanes_at(h):
            return pl.BlockSpec((h, TB), lambda j, *_: (0, j))

        token_specs = [
            pl.BlockSpec((2, 2 * T + 16, d), lambda j, *_: (jnp.minimum(j, 1), 0, 0)),
            pl.BlockSpec((2, 2 * T + 16, d), lambda j, *_: (jnp.maximum(j - 2, 0), 0, 0)),
        ]

        def call(name, us, kernel, arrays, outs, steps=1, ins=None, specs=None, scratch=()):
            return pl.pallas_call(
                kernel,
                grid_spec=pltpu.PrefetchScalarGridSpec(
                    num_scalar_prefetch=1,
                    grid=(steps,),
                    in_specs=ins or [whole(array.shape) for array in arrays],
                    out_specs=specs or [whole(out.shape) for out in outs],
                    scratch_shapes=list(scratch),
                ),
                out_shape=outs,
                compiler_params=params(),
                cost_estimate=takes(us),
                name=name,
            )(place, *arrays)

        def lines(bias):
            return bias.reshape(-1, 128)

        flat_tokens = tokens.reshape(T, d)
        flat_cot = cotangent.reshape(T, d)
        mask = image_mask.reshape(T, 1)

        (partial_mod, act_rows, silu_slope, qkv_mine, fc1_mine, send, fc2_rows, slab_rows) = call(
            "prepare",
            6,
            functools.partial(prepare_kernel, d),
            [condition, ada_weight, qkv_weight, fc1_weight, proj_weight, fc2_weight, flat_tokens, flat_cot, sample_index.T, image_mask.T],
            [
                shaped((8, 8, d), BF),
                shaped((samples, wide(rows)), BF),
                shaped((samples, wide(rows))),
                shaped((rows, wide(3 * width)), BF),
                shaped((rows, wide(part_ff)), BF),
                shaped((rows, wide(part_ff) + wide(3 * width)), BF),
                shaped((rows, wide(d + cols)), BF),
                shaped((2 * T + 16, d), BF),
            ],
            scratch=[pltpu.VMEM((samples, rows), F32)],
        )

        fc2_in = lax.all_gather(fc2_rows, "z", axis=0)
        mod_terms = lax.all_to_all(partial_mod, ("z", "y"), 0, 0, tiled=True)
        got = swap(send, ("y",))
        qkv_pair = jnp.stack([qkv_mine, got[:, wide(part_ff) :]])
        fc1_pair = jnp.stack([fc1_mine, got[:, : wide(part_ff)]])
        mod_terms, qkv_pair, fc1_pair, slab_rows = lax.optimization_barrier((mod_terms, qkv_pair, fc1_pair, slab_rows))
        qkv_pair, fc2_in = lax.optimization_barrier((qkv_pair, fc2_in))
        qkv_in = lax.all_gather(qkv_pair, "z", axis=0)
        (mod_chunk,) = call(
            "mod_sum",
            2,
            mod_sum_kernel,
            [mod_terms, lines(ada_bias)],
            [shaped((8, d), BF)],
        )
        chunks = over_z(mod_chunk)
        tok_mine = gather_near(slab_rows)
        chunks, tok_mine = lax.optimization_barrier((chunks, tok_mine))
        mod_in = to_slab(jnp.stack(chunks))
        tok_near = jnp.stack(tok_mine)
        tok_far = swap(tok_near, ("core",))
        proj_slots = gather_slots(fc2_in[:, :, d : d + cols])
        (proj_all,) = call(
            "proj",
            3,
            functools.partial(proj_kernel, d),
            proj_slots,
            [shaped((d, d), BF)],
            scratch=[pltpu.VMEM((8, 4, rows, cols), BF)],
        )
        mod_in, tok_near, tok_far, qkv_in, fc1_pair, proj_all = lax.optimization_barrier(
            (mod_in, tok_near, tok_far, qkv_in, fc1_pair, proj_all)
        )
        fc1_in = lax.all_gather(fc1_pair, "z", axis=0)
        attn_t, qkv, sel, selt, w_qkv, mod = call(
            "attend",
            13,
            functools.partial(attend_kernel, d, width, columns),
            [tok_near, tok_far, qkv_in, mod_in, lines(qkv_bias)],
            [
                shaped((width, S), BF),
                shaped((S, wide(3 * width)), BF),
                shaped((S, 128), BF),
                shaped((samples, S), BF),
                shaped((d, wide(3 * width)), BF),
                shaped((6, samples, d), BF),
            ],
            steps=4,
            ins=token_specs
            + [whole(array.shape) for array in (qkv_in, mod_in, lines(qkv_bias))],
            specs=[
                lanes_at(width),
                rows_at(wide(3 * width)),
                rows_at(128),
                lanes_at(samples),
                whole((d, wide(3 * width))),
                whole((6, samples, d)),
            ],
            scratch=[pltpu.VMEM((1, 3 * width), F32)],
        )
        attn_slots = gather_slots(attn_t)

        def slot_spec(dc, dx):
            return pl.BlockSpec((width, TB), lambda j, *_: (0, lax.bitwise_xor(j, dc * 2 + dx)))

        slot_specs = [slot_spec(dc, dx) for dc, dx, _ in offsets]
        own_out = pl.BlockSpec((2, T, d), lambda j, *_: (jnp.minimum(j, 1), 0, 0))
        far_out = pl.BlockSpec((2, T, d), lambda j, *_: (jnp.maximum(j - 2, 0), 0, 0))
        half_shape = shaped((4, T, d), BF)

        mlp_rest = [mod, proj_all, lines(proj_bias), fc1_in, lines(fc1_bias), fc2_in, lines(fc2_bias)]
        (b2_own, b2_far, gm_own, gm_far, fcg, fc1_bias_g, fc2_bias_g, modg_two, after_own, branch_own) = call(
            "mlp",
            32,
            functools.partial(mlp_kernel, d, order),
            [*attn_slots, tok_near, tok_far, sel, selt, *mlp_rest],
            [
                half_shape,
                half_shape,
                half_shape,
                half_shape,
                shaped((16 * rows, wide(part_ff)), BF),
                shaped((1, part_ff)),
                shaped((1, d)),
                shaped((3, samples, d)),
                shaped((T, d)),
                shaped((T, d)),
            ],
            steps=4,
            ins=slot_specs
            + token_specs
            + [rows_at(128), lanes_at(samples)]
            + [whole(array.shape) for array in mlp_rest],
            specs=[
                own_out,
                far_out,
                own_out,
                far_out,
                whole((16 * rows, wide(part_ff))),
                whole((1, part_ff)),
                whole((1, d)),
                whole((3, samples, d)),
                whole((T, d)),
                whole((T, d)),
            ],
            scratch=[
                pltpu.VMEM((d, part_ff), F32),
                pltpu.VMEM((part_ff, d), F32),
                pltpu.VMEM((d, part_ff), BF),
                pltpu.VMEM((part_ff, d), BF),
                pltpu.VMEM((1, d), F32),
                pltpu.VMEM((1, part_ff), F32),
                pltpu.VMEM((1, d), F32),
            ],
        )

        fc_z = lax.psum_scatter(fcg, "z", scatter_dimension=0, tiled=True)
        gm_terms = scatter_sum(gm_own, gm_far)

        *ex_slots, grad_one, modg_gate, proj_bias_g = call(
            "middle",
            6,
            functools.partial(middle_kernel, d, len(gm_terms)),
            [*gm_terms, after_own, branch_own, slab_rows, sel, selt, mod, proj_all],
            [shaped((2, width, T), BF)] * 8 + [shaped((T, d)), shaped((samples, d)), shaped((1, d))],
            ins=[whole((T, d))] * (len(gm_terms) + 3)
            + [whole((T, 128)), whole((samples, T)), whole(mod.shape), whole((d, d))],
            scratch=[pltpu.VMEM((d, T), F32)],
        )
        grad_attn = exchange(ex_slots)
        b2_sums = core_sum(b2_own, b2_far)
        grad_attn, b2_sums = lax.optimization_barrier((grad_attn, b2_sums))
        b2_terms = [over(total, slot // 2, slot % 2) for slot, total in enumerate(b2_sums)]

        back_rest = [w_qkv, modg_two, modg_gate, proj_bias_g, fc1_bias_g, fc2_bias_g]
        gin_own, gin_far, grad_qkv, attn_in, to_sum = call(
            "back",
            22,
            functools.partial(back_kernel, d, width, columns),
            [*grad_attn, tok_near, tok_far, sel, selt, mod, qkv, *back_rest],
            [half_shape, half_shape, shaped((S, wide(3 * width)), BF), shaped((S, d), BF), shaped((32, 8, d), BF)],
            steps=4,
            ins=[whole((2, width, T))] * 8
            + token_specs
            + [rows_at(128), lanes_at(samples), whole(mod.shape), rows_at(wide(3 * width))]
            + [whole(array.shape) for array in back_rest],
            specs=[own_out, far_out, rows_at(wide(3 * width)), rows_at(d), whole((32, 8, d))],
            scratch=[
                pltpu.VMEM((8, 2, width, T), BF),
                pltpu.VMEM((2, samples, d), F32),
                pltpu.VMEM((1, 3 * width), F32),
            ],
        )
        gin_own, gin_far, grad_qkv, attn_in, to_sum, b2_terms = lax.optimization_barrier(
            (gin_own, gin_far, grad_qkv, attn_in, to_sum, b2_terms)
        )
        (attn_g,) = call(
            "weights",
            8,
            functools.partial(weights_kernel, d, width, order),
            [*attn_slots, *grad_attn, grad_qkv, attn_in],
            [shaped((d, wide(4 * width)), BF)],
            steps=4,
            ins=slot_specs + [whole((2, width, T))] * 8 + [rows_at(wide(3 * width)), rows_at(d)],
            specs=[whole((d, wide(4 * width)))],
            scratch=[
                pltpu.VMEM((d, 3 * width), F32),
                pltpu.VMEM((d, width), F32),
                pltpu.VMEM((8, width, T), BF),
            ],
        )
        terms = lax.all_to_all(to_sum, names, 0, 0, tiled=True)
        own_specs = [whole((T, 1)), whole((T, 128)), whole(mod.shape)]
        (result,) = call(
            "output",
            3,
            output_kernel,
            [*b2_terms, flat_tokens, after_own, mask, sel, mod],
            [shaped((T, d), BF)],
            ins=[whole((T, d))] * 6 + own_specs,
        )
        def split(name, kernel, summed, lanes):
            return call(
                name,
                3,
                functools.partial(kernel, rows),
                [summed],
                [shaped((rows, n), BF) for n in lanes],
                scratch=[pltpu.VMEM((8, rows, max(lanes)), BF)],
            )

        def join(name, kernel, pieces, outs):
            return call(
                name,
                3,
                functools.partial(kernel, rows),
                pieces,
                outs,
                scratch=[pltpu.VMEM((8, rows, max(piece.shape[1] for piece in pieces)), BF)],
            )

        attn_g, fc_z, terms, result = lax.optimization_barrier((attn_g, fc_z, terms, result))
        attn_z = lax.psum_scatter(attn_g, "z", scatter_dimension=0, tiled=True)
        gin_terms = scatter_sum(gin_own, gin_far)

        (sums,) = call("grad_sum", 2, grad_sum_kernel, [terms], [shaped((8, d), BF)])
        total = to_slab(jnp.stack(over_z(sums)))

        (ada_weight_grad, condition_grad, ada_bias_grad, qkv_bias_grad, proj_bias_grad, fc1_bias_grad, fc2_bias_grad) = call(
            "ada",
            5,
            functools.partial(ada_kernel, d),
            [total, act_rows, silu_slope, ada_weight],
            [shaped((rows, 6 * d)), shaped((samples, rows))]
            + [shaped((n // 128, 128)) for n in (6 * d, 2 * d, d, ff, d)],
        )

        mlp_send = split("mlp_split", mlp_split_kernel, fc_z, [wide(rows if dy else 3 * rows) for _, _, dy in offsets])
        mlp_got = exchange(mlp_send)
        attn_z, ada_weight_grad = lax.optimization_barrier((attn_z, ada_weight_grad))
        attn_send = split("attn_split", attn_split_kernel, attn_z, [wide(rows if dc or dx else 2 * rows) for dc, dx, _ in offsets])
        attn_got = exchange(attn_send)
        gin_terms = lax.optimization_barrier((gin_terms, attn_send[0]))[0]
        mlp_got = lax.optimization_barrier((mlp_got, attn_send[0]))[0]
        fc1_weight_grad, fc2_weight_grad = join(
            "mlp_join", mlp_join_kernel, mlp_got, [shaped((rows, ff // 4)), shaped((d // 4, 4 * rows))]
        )
        (input_grad,) = call(
            "input_grad",
            3,
            input_grad_kernel,
            [*gin_terms, flat_tokens, grad_one, flat_cot, mask, sel, mod],
            [shaped((T, d))],
            ins=[whole((T, d))] * 7 + own_specs,
        )

        qkv_weight_grad, proj_weight_grad = join(
            "attn_join", attn_join_kernel, attn_got, [shaped((rows, 3 * d // 4)), shaped((rows, d // 4))]
        )

        shape = (frames, columns, d)
        return (
            result.reshape(shape),
            input_grad.reshape(shape),
            condition_grad,
            ada_weight_grad,
            ada_bias_grad.reshape(-1),
            qkv_weight_grad,
            qkv_bias_grad.reshape(-1),
            proj_weight_grad,
            proj_bias_grad.reshape(-1),
            fc1_weight_grad,
            fc1_bias_grad.reshape(-1),
            fc2_weight_grad.T,
            fc2_bias_grad.reshape(-1),
        )

    frame, patch = ("x", "core"), ("z", "y")
    token_spec, number_spec = P(None, names, None), P(None, names)
    row_spec, both_spec = P(patch, None), P(patch, frame)
    return jax.shard_map(
        local,
        mesh=grid,
        in_specs=(
            token_spec, number_spec, number_spec, P(), row_spec, P(), row_spec, P(), row_spec, P(), row_spec, P(),
            row_spec, P(), token_spec,
        ),
        out_specs=(
            token_spec, token_spec, P(None, patch), row_spec, P(), both_spec, P(), both_spec, P(), both_spec, P(),
            both_spec, P(),
        ),
        check_vma=False,
    )


def solution(mesh):
    if (mesh.shape["frame"], mesh.shape["patch"]) == (4, 8):
        return slab_solution(mesh)
    return general_solution(mesh)
```

profile of v0, /device:TPU:0, one launch (start us, length us, event | category | flops | bytes accessed | tf_op | source)
XLA Modules:
  0.0 324.1 jit_solution(8247438157399172930)
XLA Ops:
  8.5 5.8 %prepare.1 = (bf16[8,8,1152]{2,1,0:T(8,128)(2,1)}, bf16[32,256]{1,0:T(8,128)(2,1)}, f32[32,256]{1,0:T(8,128)}, bf16[144,512]{1,0:T(8,128)(2,1)}, bf16[144,640]{1...) custom-call(s32[40]{0:T(128)} %dynamic-slice_bitcast_fusion.place, ...), custom_call_target="tpu_custom_call" | custom-call | flops 1000 | bytes 1000 | tf_op jit(solution)/shard_map/prepare/pallas_call | solution.py:1362
  17.4 5.0 %all-to-all-start = ((bf16[8,8,1152]{2,1,0:T(8,128)(2,1)}), bf16[8,8,1152]{2,1,0:T(8,128)(2,1)S(1)}, u32[]{:S(2)}, u32[]{:S(2)}) async-start(bf16[8,8,1152]{2,1,0:T(8,128)(2,1)} %get-tuple-element.139), calls=%async_computation | async-start | bytes 294912 | tf_op jit(solution)/shard_map/all_to_all | solution.py:1403
  47.2 11.6 %collective-permute-done.6 = bf16[272,1152]{1,0:T(8,128)(2,1)S(1)} collective-permute-done((bf16[272,1152]{1,0:T(8,128)(2,1)S(1)}, bf16[272,1152]{1,0:T(8,128)(2,1)S(1)}, u32[]{:S(2)}, u32[]{:S(2)}) %collective-permute-start.6) | collective-permute-done | bytes 626720 | tf_op jit(solution)/shard_map/ppermute | solution.py:1296
  66.3 3.5 %all-to-all-start.1 = ((bf16[8,4,8,1152]{3,2,1,0:T(8,128)(2,1)}), bf16[8,4,8,1152]{3,2,1,0:T(8,128)(2,1)S(1)}, u32[]{:S(2)}, u32[]{:S(2)}) async-start(bf16[8,4,8,1152]{3,2,1,0:T(8,128)(2,1)} %broadcast_in_dim.6), calls=%async_computation.1 | async-start | bytes 1179648 | tf_op jit(solution)/shard_map/all_to_all | solution.py:1316
  70.3 5.9 %collective-permute-done.8.refs_1_ = bf16[4,144,288]{2,1,0:T(8,128)(2,1)} collective-permute-done((bf16[4,144,288]{2,1,0:T(8,128)(2,1)}, bf16[4,144,288]{2,1,0:T(8,128)(2,1)}, u32[]{:S(2)}, u32[]{:S(2)}) %collective-permute-start.8) | collective-permute-done | bytes 331808 | tf_op jit(solution)/shard_map/ppermute | solution.py:1296
  76.7 9.6 %collective-permute-done.10.refs_3_ = bf16[4,144,288]{2,1,0:T(8,128)(2,1)} collective-permute-done((bf16[4,144,288]{2,1,0:T(8,128)(2,1)}, bf16[4,144,288]{2,1,0:T(8,128)(2,1)}, u32[]{:S(2)}, u32[]{:S(2)}) %collective-permute-start.10) | collective-permute-done | bytes 331808 | tf_op jit(solution)/shard_map/ppermute | solution.py:1296
  89.1 5.4 %proj.1.refs_13_.refs_10_ = bf16[1152,1152]{1,0:T(8,128)(2,1)} custom-call(s32[40]{0:T(128)} %dynamic-slice_bitcast_fusion.place, bf16[4,144,288]{2,1,0:T(8,128)(2,1)} %slice.83.refs_0_, bf16[4,144,288]{2,1,0:T(8,128)(2,1)} %collective-permute-done.8.refs_1_, bf16[4,144,288]{2,1,0:T(8,128)(2,1)} %collective-permute-done.9.refs_2_, ...), custom_call_target="tpu_custom_call" | custom-call | flops 1000 | bytes 1000 | tf_op jit(solution)/shard_map/proj/pallas_call | solution.py:1362
  95.3 12.8 %attend.1 = (bf16[144,1024]{1,0:T(8,128)(2,1)}, bf16[1024,512]{1,0:T(8,128)(2,1)}, bf16[1024,128]{1,0:T(8,128)(2,1)}, bf16[32,1024]{1,0:T(8,128)(2,1)}, bf16[115...) custom-call(s32[40]{0:T(128)} %dynamic-slice_bitcast_fusion.place, bf16[4,272,1152]{2,1,0:T(8,128)(2,1)} %copy-done, ...), custom_call_target="tpu_custom_call" | custom-call | flops 1000 | bytes 1000 | tf_op jit(solution)/shard_map/attend/pallas_call | solution.py:1362
  111.7 5.8 %collective-permute-done.15.refs_1_ = bf16[144,1024]{1,0:T(8,128)(2,1)S(1)} collective-permute-done((bf16[144,1024]{1,0:T(8,128)(2,1)}, bf16[144,1024]{1,0:T(8,128)(2,1)S(1)}, u32[]{:S(2)}, u32[]{:S(2)}) %collective-permute-start.15) | collective-permute-done | bytes 294944 | tf_op jit(solution)/shard_map/ppermute | solution.py:1296
  119.6 5.4 %collective-permute-done.17.refs_3_ = bf16[144,1024]{1,0:T(8,128)(2,1)S(1)} collective-permute-done((bf16[144,1024]{1,0:T(8,128)(2,1)}, bf16[144,1024]{1,0:T(8,128)(2,1)S(1)}, u32[]{:S(2)}, u32[]{:S(2)}) %collective-permute-start.17) | collective-permute-done | bytes 294944 | tf_op jit(solution)/shard_map/ppermute | solution.py:1296
  126.6 3.6 %all-gather.11.cloned.1.call-done = bf16[8,144,640]{2,1,0:T(8,128)(2,1)} async-done(((bf16[2,144,640]{2,1,0:T(8,128)(2,1)}), bf16[8,144,640]{2,1,0:T(8,128)(2,1)}) %all-gather.11.cloned.1.call-update) | async-done | bytes 1474576 | tf_op jit(solution)/shard_map/all_gather | solution.py:1435
  130.2 31.6 %mlp.1 = (bf16[4,128,1152]{2,1,0:T(8,128)(2,1)}, bf16[4,128,1152]{2,1,0:T(8,128)(2,1)}, bf16[4,128,1152]{2,1,0:T(8,128)(2,1)}, bf16[4,128,1152]{2,1,0:T(8,128)(2...) custom-call(s32[40]{0:T(128)} %dynamic-slice_bitcast_fusion.place, ...), custom_call_target="tpu_custom_call" | custom-call | flops 1000 | bytes 1000 | tf_op jit(solution)/shard_map/mlp/pallas_call | solution.py:1362
  169.4 5.6 %collective-permute-done.23.refs_1_ = bf16[128,1152]{1,0:T(8,128)(2,1)S(1)} collective-permute-done((bf16[128,1152]{1,0:T(8,128)(2,1)S(1)}, bf16[128,1152]{1,0:T(8,128)(2,1)S(1)}, u32[]{:S(2)}, u32[]{:S(2)}) %collective-permute-start.23) | collective-permute-done | bytes 294944 | tf_op jit(solution)/shard_map/ppermute | solution.py:1296
  177.3 5.2 %collective-permute-done.25.refs_3_ = bf16[128,1152]{1,0:T(8,128)(2,1)S(1)} collective-permute-done((bf16[128,1152]{1,0:T(8,128)(2,1)S(1)}, bf16[128,1152]{1,0:T(8,128)(2,1)S(1)}, u32[]{:S(2)}, u32[]{:S(2)}) %collective-permute-start.25) | collective-permute-done | bytes 294944 | tf_op jit(solution)/shard_map/ppermute | solution.py:1296
  183.2 6.1 %middle.1 = (bf16[2,144,128]{2,1,0:T(8,128)(2,1)}, bf16[2,144,128]{2,1,0:T(8,128)(2,1)}, bf16[2,144,128]{2,1,0:T(8,128)(2,1)}, bf16[2,144,128]{2,1,0:T(8,128)(2,...) custom-call(s32[40]{0:T(128)} %dynamic-slice_bitcast_fusion.place, ...), custom_call_target="tpu_custom_call" | custom-call | flops 1000 | bytes 1000 | tf_op jit(solution)/shard_map/middle/pallas_call | solution.py:1362
  205.2 19.0 %back.1 = (bf16[4,128,1152]{2,1,0:T(8,128)(2,1)}, bf16[4,128,1152]{2,1,0:T(8,128)(2,1)}, bf16[1024,512]{1,0:T(8,128)(2,1)}, bf16[1024,1152]{1,0:T(8,128)(2,1)}, bf16[32,8,1152]{2,1,0:T(8,128)(2,1)}) custom-call(s32[40]{0:T(128)} %dynamic-slice_bitcast_fusion.place, bf16[2,144,128]{2,1,0:T(8,128)(2,1)} %get-tuple-element.183.refs_0_.refs_8_, ...), custom_call_target="tpu_custom_call" | custom-call | flops 1000 | bytes 1000 | tf_op jit(solution)/shard_map/back/pallas_call | solution.py:1362
  231.1 7.9 %weights.1 = bf16[1152,640]{1,0:T(8,128)(2,1)} custom-call(s32[40]{0:T(128)} %dynamic-slice_bitcast_fusion.place, bf16[144,1024]{1,0:T(8,128)(2,1)} %get-tuple-element.163.refs_0_, bf16[144,1024]{1,0:T(8,128)(2,1)} %copy-done.5, bf16[144,1024]{1,0:T(8,128)(2,1)} %copy-done.6, bf16[144,1024]{1,0:T(8,128)(2,1)} %copy-done.7, bf16[144,1024]{1,0:T(8,128)(2,1)} %copy-done.8, ...), custom_call_target="tpu_custom_call" | custom-call | flops 1000 | bytes 1000 | tf_op jit(solution)/shard_map/weights/pallas_call | solution.py:1362
  239.0 5.7 %all-to-all-done.2.terms_ref = bf16[32,8,1152]{2,1,0:T(8,128)(2,1)S(1)} async-done(((bf16[32,8,1152]{2,1,0:T(8,128)(2,1)}), bf16[32,8,1152]{2,1,0:T(8,128)(2,1)S(1)}, u32[]{:S(2)}, u32[]{:S(2)}) %all-to-all-start.2) | async-done | bytes 589856 | tf_op jit(solution)/shard_map/all_to_all | solution.py:1573
  257.2 3.5 %all-to-all-start.3 = ((bf16[8,4,8,1152]{3,2,1,0:T(8,128)(2,1)}), bf16[8,4,8,1152]{3,2,1,0:T(8,128)(2,1)S(1)}, u32[]{:S(2)}, u32[]{:S(2)}) async-start(bf16[8,4,8,1152]{3,2,1,0:T(8,128)(2,1)} %broadcast_in_dim.7), calls=%async_computation.5 | async-start | bytes 1179648 | tf_op jit(solution)/shard_map/all_to_all | solution.py:1316
  271.9 5.1 %collective-permute-done.38.gin_1 = bf16[128,1152]{1,0:T(8,128)(2,1)S(1)} collective-permute-done((bf16[128,1152]{1,0:T(8,128)(2,1)S(1)}, bf16[128,1152]{1,0:T(8,128)(2,1)S(1)}, u32[]{:S(2)}, u32[]{:S(2)}) %collective-permute-start.38) | collective-permute-done | bytes 294944 | tf_op jit(solution)/shard_map/ppermute | solution.py:1296
  278.5 5.9 %collective-permute-done.40.gin_3 = bf16[128,1152]{1,0:T(8,128)(2,1)S(1)} collective-permute-done((bf16[128,1152]{1,0:T(8,128)(2,1)S(1)}, bf16[128,1152]{1,0:T(8,128)(2,1)S(1)}, u32[]{:S(2)}, u32[]{:S(2)}) %collective-permute-start.40) | collective-permute-done | bytes 294944 | tf_op jit(solution)/shard_map/ppermute | solution.py:1296
  289.4 5.7 %ada.1 = (f32[144,6912]{1,0:T(8,128)}, f32[32,144]{1,0:T(8,128)}, f32[54,128]{1,0:T(8,128)}, f32[18,128]{1,0:T(8,128)}, f32[9,128]{1,0:T(8,128)}, /*index=5*/f32[36,128]{1,0:T(8,128)}, f32[9,128]{1,0:T(8,128)}) custom-call(s32[40]{0:T(128)} %dynamic-slice_bitcast_fusion.place, bf16[8,4,8,1152]{3,2,1,0:T(8,128)(2,1)} %copy-done.4, ...), custom_call_target="tpu_custom_call" | custom-call | flops 1000 | bytes 1000 | tf_op jit(solution)/shard_map/ada/pallas_call | solution.py:1362
  305.3 3.9 %input_grad.1 = f32[128,1152]{1,0:T(8,128)} custom-call(s32[40]{0:T(128)} %dynamic-slice_bitcast_fusion.place, bf16[128,1152]{1,0:T(8,128)(2,1)} %get-tuple-element.225.gin_0, bf16[128,1152]{1,0:T(8,128)(2,1)} %copy-done.26, bf16[128,1152]{1,0:T(8,128)(2,1)} %copy-done.27, bf16[128,1152]{1,0:T(8,128)(2,1)} %copy-done.28, bf16[128,1152]{1,0:T(8,128)(2,1)} %bitcast.68, ...), custom_call_target="tpu_custom_call" | custom-call | flops 1000 | bytes 1000 | tf_op jit(solution)/shard_map/input_grad/pallas_call | solution.py:1362
  309.2 4.0 %mlp_join.1 = (f32[144,1152]{1,0:T(8,128)}, f32[288,576]{1,0:T(8,128)}) custom-call(s32[40]{0:T(128)} %dynamic-slice_bitcast_fusion.place, bf16[144,512]{1,0:T(8,128)(2,1)} %get-tuple-element.253.refs_0_, bf16[144,256]{1,0:T(8,128)(2,1)} %copy-done.42, bf16[144,512]{1,0:T(8,128)(2,1)} %copy-done.37, bf16[144,256]{1,0:T(8,128)(2,1)} %copy-done.43, ...), custom_call_target="tpu_custom_call" | custom-call | flops 1000 | bytes 1000 | tf_op jit(solution)/shard_map/mlp_join/pallas_call | solution.py:1362
  (257 shorter events, 126.1 us)
Async XLA Ops:
  7.2 52.7 %all-gather.7.cloned.1.call-start = ((), (), s32[]{:S(2)}) async-start(), calls=%async_computation.8 | async-start | bytes 2211840 | tf_op jit(solution)/shard_map/all_gather | solution.py:1402
  22.4 72.1 %all-gather.9.cloned.1.call-start = ((), (), s32[]{:S(2)}) async-start(), calls=%async_computation.9 | async-start | bytes 1474560 | tf_op jit(solution)/shard_map/all_gather | solution.py:1409
  29.9 17.1 %collective-permute-start.4 = (bf16[272,1152]{1,0:T(8,128)(2,1)S(1)}, bf16[272,1152]{1,0:T(8,128)(2,1)S(1)}, u32[]{:S(2)}, u32[]{:S(2)}) collective-permute-start(bf16[272,1152]{1,0:T(8,128)(2,1)S(1)} %copy-done.1), channel_id=1, source_target_pairs={{0,1},{1,0},{2,3},{3,2},{4,5},{5,4},{6,7},{7,6},{8,9},{9,8},{10,11... | collective-permute-start | bytes 1880072 | tf_op jit(solution)/shard_map/ppermute | solution.py:1296
  30.2 17.1 %collective-permute-start.5 = (bf16[272,1152]{1,0:T(8,128)(2,1)S(1)}, bf16[272,1152]{1,0:T(8,128)(2,1)S(1)}, u32[]{:S(2)}, u32[]{:S(2)}) collective-permute-start(bf16[272,1152]{1,0:T(8,128)(2,1)S(1)} %copy-done.1), channel_id=1, source_target_pairs={{0,16},{16,0},{1,17},{17,1},{2,18},{18,2},{3,19},{19,3},{4,20},{20... | collective-permute-start | bytes 1880072 | tf_op jit(solution)/shard_map/ppermute | solution.py:1296
  31.9 27.0 %collective-permute-start.6 = (bf16[272,1152]{1,0:T(8,128)(2,1)S(1)}, bf16[272,1152]{1,0:T(8,128)(2,1)S(1)}, u32[]{:S(2)}, u32[]{:S(2)}) collective-permute-start(bf16[272,1152]{1,0:T(8,128)(2,1)S(1)} %copy-done.1), channel_id=1, source_target_pairs={{0,17},{1,16},{16,1},{17,0},{2,19},{3,18},{18,3},{19,2},{4,21},{5,... | collective-permute-start | bytes 1880072 | tf_op jit(solution)/shard_map/ppermute | solution.py:1296
  59.2 35.3 %collective-permute-start.7 = (bf16[4,272,1152]{2,1,0:T(8,128)(2,1)S(1)}, bf16[4,272,1152]{2,1,0:T(8,128)(2,1)}, u32[]{:S(2)}, u32[]{:S(2)}) collective-permute-start(bf16[4,272,1152]{2,1,0:T(8,128)(2,1)S(1)} %pad_maximum_fusion.tok_near.refs_8_), channel_id=1, source_target_pairs={{0,8},{8,0},{1,9},{9,1},{2,10},{10,2},{3,11},{11,3},{4,12},{12,4},... | collective-permute-start | bytes 7520264 | tf_op jit(solution)/shard_map/ppermute | solution.py:1296
  64.7 21.6 %collective-permute-start.10 = (bf16[4,144,288]{2,1,0:T(8,128)(2,1)}, bf16[4,144,288]{2,1,0:T(8,128)(2,1)}, u32[]{:S(2)}, u32[]{:S(2)}) collective-permute-start(bf16[4,144,288]{2,1,0:T(8,128)(2,1)} %slice.83.refs_0_), channel_id=1, source_target_pairs={{0,17},{1,16},{16,1},{17,0},{2,19},{3,18},{18,3},{19,2},{4,21},{5,... | collective-permute-start | bytes 995336 | tf_op jit(solution)/shard_map/ppermute | solution.py:1296
  66.3 28.2 %all-to-all-start.1 = ((bf16[8,4,8,1152]{3,2,1,0:T(8,128)(2,1)}), bf16[8,4,8,1152]{3,2,1,0:T(8,128)(2,1)S(1)}, u32[]{:S(2)}, u32[]{:S(2)}) async-start(bf16[8,4,8,1152]{3,2,1,0:T(8,128)(2,1)} %broadcast_in_dim.6), calls=%async_computation.1 | async-start | bytes 1179648 | tf_op jit(solution)/shard_map/all_to_all | solution.py:1316
  69.8 60.3 %all-gather.11.cloned.1.call-start = ((), (), s32[]{:S(2)}) async-start(), calls=%async_computation.10 | async-start | bytes 1843200 | tf_op jit(solution)/shard_map/all_gather | solution.py:1435
  69.9 16.4 %collective-permute-start.11 = (bf16[4,144,288]{2,1,0:T(8,128)(2,1)}, bf16[4,144,288]{2,1,0:T(8,128)(2,1)S(1)}, u32[]{:S(2)}, u32[]{:S(2)}) collective-permute-start(bf16[4,144,288]{2,1,0:T(8,128)(2,1)} %slice.83.refs_0_), channel_id=1, source_target_pairs={{0,8},{8,0},{1,9},{9,1},{2,10},{10,2},{3,11},{11,3},{4,12},{12,4},... | collective-permute-start | bytes 995336 | tf_op jit(solution)/shard_map/ppermute | solution.py:1296
  94.6 150.1 %reduce-scatter.3.cloned.1.call-start = ((), (), s32[]{:S(2)}) async-start(), calls=%async_computation.6 | async-start | bytes 3686400 | tf_op jit(solution)/shard_map/reduce_scatter | solution.py:1518
  163.0 29.8 %collective-permute-start.33 = (bf16[4,128,1152]{2,1,0:T(8,128)(2,1)S(1)}, bf16[4,128,1152]{2,1,0:T(8,128)(2,1)S(1)}, u32[]{:S(2)}, u32[]{:S(2)}) collective-permute-start(bf16[4,128,1152]{2,1,0:T(8,128)(2,1)S(1)} %copy-done.54), channel_id=1, source_target_pairs={{0,8},{8,0},{1,9},{9,1},{2,10},{10,2},{3,11},{11,3},{4,12},{12,4},... | collective-permute-start | bytes 3538952 | tf_op jit(solution)/shard_map/ppermute | solution.py:1296
  201.7 22.6 %collective-permute-start.34 = (bf16[128,1152]{1,0:T(8,128)(2,1)S(1)}, bf16[128,1152]{1,0:T(8,128)(2,1)S(1)}, u32[]{:S(2)}, u32[]{:S(2)}) collective-permute-start(bf16[128,1152]{1,0:T(8,128)(2,1)S(1)} %get-tuple-element.204), channel_id=1, source_target_pairs={{0,1},{1,0},{2,3},{3,2},{4,5},{5,4},{6,7},{7,6},{8,9},{9,8},{10,11... | collective-permute-start | bytes 884744 | tf_op jit(solution)/shard_map/ppermute | solution.py:1296
  201.7 22.6 %collective-permute-start.35 = (bf16[128,1152]{1,0:T(8,128)(2,1)S(1)}, bf16[128,1152]{1,0:T(8,128)(2,1)S(1)}, u32[]{:S(2)}, u32[]{:S(2)}) collective-permute-start(bf16[128,1152]{1,0:T(8,128)(2,1)S(1)} %get-tuple-element.205), channel_id=1, source_target_pairs={{0,16},{16,0},{1,17},{17,1},{2,18},{18,2},{3,19},{19,3},{4,20},{20... | collective-permute-start | bytes 884744 | tf_op jit(solution)/shard_map/ppermute | solution.py:1296
  203.6 20.7 %collective-permute-start.36 = (bf16[128,1152]{1,0:T(8,128)(2,1)S(1)}, bf16[128,1152]{1,0:T(8,128)(2,1)S(1)}, u32[]{:S(2)}, u32[]{:S(2)}) collective-permute-start(bf16[128,1152]{1,0:T(8,128)(2,1)S(1)} %get-tuple-element.206), channel_id=1, source_target_pairs={{0,17},{1,16},{16,1},{17,0},{2,19},{3,18},{18,3},{19,2},{4,21},{5,... | collective-permute-start | bytes 884744 | tf_op jit(solution)/shard_map/ppermute | solution.py:1296
  224.3 20.4 %all-to-all-start.2 = ((bf16[32,8,1152]{2,1,0:T(8,128)(2,1)}), bf16[32,8,1152]{2,1,0:T(8,128)(2,1)S(1)}, u32[]{:S(2)}, u32[]{:S(2)}) async-start(bf16[32,8,1152]{2,1,0:T(8,128)(2,1)} %get-tuple-element.210), calls=%async_computation.3 | async-start | bytes 1179648 | tf_op jit(solution)/shard_map/all_to_all | solution.py:1573
  226.9 68.2 %reduce-scatter.5.cloned.1.call-start = ((), (), s32[]{:S(2)}) async-start(), calls=%async_computation.7 | async-start | bytes 1843200 | tf_op jit(solution)/shard_map/reduce_scatter | solution.py:1604
  244.7 16.0 %collective-permute-start.37 = (bf16[4,128,1152]{2,1,0:T(8,128)(2,1)}, bf16[4,128,1152]{2,1,0:T(8,128)(2,1)S(1)}, u32[]{:S(2)}, u32[]{:S(2)}) collective-permute-start(bf16[4,128,1152]{2,1,0:T(8,128)(2,1)} %get-tuple-element.217), channel_id=1, source_target_pairs={{0,8},{8,0},{1,9},{9,1},{2,10},{10,2},{3,11},{11,3},{4,12},{12,4},... | collective-permute-start | bytes 3538952 | tf_op jit(solution)/shard_map/ppermute | solution.py:1296
  257.2 31.4 %all-to-all-start.3 = ((bf16[8,4,8,1152]{3,2,1,0:T(8,128)(2,1)}), bf16[8,4,8,1152]{3,2,1,0:T(8,128)(2,1)S(1)}, u32[]{:S(2)}, u32[]{:S(2)}) async-start(bf16[8,4,8,1152]{3,2,1,0:T(8,128)(2,1)} %broadcast_in_dim.7), calls=%async_computation.5 | async-start | bytes 1179648 | tf_op jit(solution)/shard_map/all_to_all | solution.py:1316
  265.1 19.2 %collective-permute-start.40 = (bf16[128,1152]{1,0:T(8,128)(2,1)S(1)}, bf16[128,1152]{1,0:T(8,128)(2,1)S(1)}, u32[]{:S(2)}, u32[]{:S(2)}) collective-permute-start(bf16[128,1152]{1,0:T(8,128)(2,1)S(1)} %get-tuple-element.265), channel_id=1, source_target_pairs={{0,17},{1,16},{16,1},{17,0},{2,19},{3,18},{18,3},{19,2},{4,21},{5,... | collective-permute-start | bytes 884744 | tf_op jit(solution)/shard_map/ppermute | solution.py:1296
  268.5 17.5 %collective-permute-start.51 = (bf16[144,256]{1,0:T(8,128)(2,1)}, bf16[144,256]{1,0:T(8,128)(2,1)S(1)}, u32[]{:S(2)}, u32[]{:S(2)}) collective-permute-start(bf16[144,256]{1,0:T(8,128)(2,1)} %get-tuple-element.246), channel_id=1, source_target_pairs={{0,1},{1,0},{2,3},{3,2},{4,5},{5,4},{6,7},{7,6},{8,9},{9,8},{10,11... | collective-permute-start | bytes 221192 | tf_op jit(solution)/shard_map/ppermute | solution.py:1296
  277.0 23.3 %collective-permute-start.52 = (bf16[144,512]{1,0:T(8,128)(2,1)}, bf16[144,512]{1,0:T(8,128)(2,1)S(1)}, u32[]{:S(2)}, u32[]{:S(2)}) collective-permute-start(bf16[144,512]{1,0:T(8,128)(2,1)} %get-tuple-element.247), channel_id=1, source_target_pairs={{0,16},{16,0},{1,17},{17,1},{2,18},{18,2},{3,19},{19,3},{4,20},{20... | collective-permute-start | bytes 442376 | tf_op jit(solution)/shard_map/ppermute | solution.py:1296
  278.5 23.4 %collective-permute-start.54 = (bf16[144,512]{1,0:T(8,128)(2,1)}, bf16[144,512]{1,0:T(8,128)(2,1)S(1)}, u32[]{:S(2)}, u32[]{:S(2)}) collective-permute-start(bf16[144,512]{1,0:T(8,128)(2,1)} %get-tuple-element.249), channel_id=1, source_target_pairs={{0,8},{8,0},{1,9},{9,1},{2,10},{10,2},{3,11},{11,3},{4,12},{12,4},... | collective-permute-start | bytes 442376 | tf_op jit(solution)/shard_map/ppermute | solution.py:1296
  284.4 17.6 %collective-permute-start.56 = (bf16[144,512]{1,0:T(8,128)(2,1)}, bf16[144,512]{1,0:T(8,128)(2,1)S(1)}, u32[]{:S(2)}, u32[]{:S(2)}) collective-permute-start(bf16[144,512]{1,0:T(8,128)(2,1)} %get-tuple-element.251), channel_id=1, source_target_pairs={{0,24},{8,16},{16,8},{24,0},{1,25},{9,17},{17,9},{25,1},{2,26},{10... | collective-permute-start | bytes 442376 | tf_op jit(solution)/shard_map/ppermute | solution.py:1296
  (98 other events, 786.8 us)
Sparse Core Ops, SparseCore 0:
  17.5 42.3 all-gather.6
  62.0 29.1 all-gather.8
  94.7 35.4 all-gather.10
  161.9 56.0 reduce-scatter.2
  244.8 32.1 reduce-scatter.4
where the time goes:
time: 326 us; the launch traced here: 324 us
  Pallas kernels  120 us (37%)
  waiting for transfers between devices  102 us (31%)
  starting transfers between devices  70.3 us (22%)
  between operations  14.4 us (4%)
  local copies, waits for them, and re-layouts  11.9 us (4%)
  other arithmetic  5.68 us (2%)
    pallas_call x16, Pallas kernels, call(): pl.pallas_call(kernel, grid_spec=pltpu.PrefetchScalarGridSpec(num_scalar_...  120 us
    ppermute x52, waiting for transfers between devices, swap(): return lax.ppermute(a, axes, [(k, n - 1 - k) for k in range(n)])  80.7 us
    ppermute x52, starting transfers between devices, swap(): return lax.ppermute(a, axes, [(k, n - 1 - k) for k in range(n)])  45.1 us
    ppermute x6, starting transfers between devices, from_z(): return lax.ppermute(a, ('z',), [(z, z ^ apart) for z in range(4)])  10 us
    ppermute x6, waiting for transfers between devices, from_z(): return lax.ppermute(a, ('z',), [(z, z ^ apart) for z in range(4)])  8.98 us
    all_to_all x2, starting transfers between devices, to_slab(): lax.all_to_all(jnp.broadcast_to(a, (8, *a.shape)), group, 0, 0, tiled=True)  7.08 us
  transfers between devices with their start and end apart: 67, of which 30 were waited for; matrix products, arithmetic and copies ran while one was open for 3% of the time, Pallas kernels for 24%

commit v1 on v0

--- a/solution.py
+++ b/solution.py
@@ -1191,38 +1191,27 @@
     put_row(fc2_ref, rows[7])
 
 
-def mlp_split_kernel(rows, place, in_ref, *outs):
+def mlp_split_kernel(rows, place, in_ref, out_ref):
     cols = 2 * rows
-    outs, full = outs[:8], outs[8]
-    full[...] = jnp.zeros_like(full)
+    out_ref[:, :, 3 * rows :] = jnp.zeros((8, rows, out_ref.shape[2] - 3 * rows), BF)
     for f in range(4):
         for y in range(2):
-            slot = place[AT_SLOT + f * 2 + y]
-            full[slot, :, :rows] = in_ref[y * rows : (y + 1) * rows, f * rows : (f + 1) * rows]
-            part = in_ref[(2 + f // 2) * rows : (3 + f // 2) * rows, f % 2 * cols : (f % 2 + 1) * cols]
-            full[slot, :, rows : 3 * rows] = jnp.where(place[AT_Y] == y, part.astype(F32), 0.0).astype(BF)
-    for slot, out in enumerate(outs):
-        out[...] = full[slot, :, : out.shape[1]]
-
-
-def collect(full, refs):
-    for slot, ref in enumerate(refs):
-        full[slot, :, : ref.shape[1]] = ref[...]
-
-
-def mlp_join_kernel(rows, place, *refs):
-    (fc1_ref, fc2_ref, full) = refs[8:]
-    collect(full, refs[:8])
+            out_ref[f * 2 + y, :, :rows] = in_ref[y * rows : (y + 1) * rows, f * rows : (f + 1) * rows]
+            out_ref[f * 2 + y, :, rows : 3 * rows] = in_ref[
+                (2 + f // 2) * rows : (3 + f // 2) * rows, f % 2 * cols : (f % 2 + 1) * cols
+            ]
+
+
+def mlp_join_kernel(rows, place, got_ref, fc1_ref, fc2_ref):
     for f in range(4):
         for y in range(2):
             at = (y * 4 + f) * rows
-            fc1_ref[:, at : at + rows] = full[place[AT_SLOT + f * 2 + y], :, :rows].astype(F32)
-        fc2_ref[:, f * rows : (f + 1) * rows] = full[place[AT_SLOT + f * 2 + place[AT_Y]], :, rows : 3 * rows].astype(F32).T
-
-
-def attn_split_kernel(rows, place, in_ref, *outs):
-    outs, full = outs[:8], outs[8]
-    full[...] = jnp.zeros_like(full)
+            fc1_ref[:, at : at + rows] = got_ref[f * 2 + y, :, :rows].astype(F32)
+        fc2_ref[:, f * rows : (f + 1) * rows] = got_ref[f * 2 + place[AT_Y], :, rows : 3 * rows].astype(F32).T
+
+
+def attn_split_kernel(rows, place, in_ref, out_ref):
+    out_ref[...] = jnp.zeros_like(out_ref)
     for part in range(8):
 
         @pl.when(place[AT_G] == part)
@@ -1230,26 +1219,19 @@
             for y in range(2):
                 block = in_ref[y * rows : (y + 1) * rows]
                 for t in range(3):
-                    to = (8 * t + part) // 6
-                    full[place[AT_SLOT + to * 2 + y], :, :rows] = block[:, t * rows : (t + 1) * rows]
-                full[place[AT_SLOT + part // 2 * 2 + y], :, rows : 2 * rows] = block[:, 3 * rows : 4 * rows]
-
-    for slot, out in enumerate(outs):
-        out[...] = full[slot, :, : out.shape[1]]
-
-
-def attn_join_kernel(rows, place, *refs):
-    (qkv_ref, proj_ref, full) = refs[8:]
-    collect(full, refs[:8])
+                    out_ref[(8 * t + part) // 6 * 2 + y, :, :rows] = block[:, t * rows : (t + 1) * rows]
+                out_ref[part // 2 * 2 + y, :, rows : 2 * rows] = block[:, 3 * rows : 4 * rows]
+
+
+def attn_join_kernel(rows, place, got_ref, qkv_ref, proj_ref):
     for y in range(2):
-        proj_ref[:, y * rows : (y + 1) * rows] = full[place[AT_SLOT + place[AT_F] * 2 + y], :, rows : 2 * rows].astype(F32)
+        proj_ref[:, y * rows : (y + 1) * rows] = got_ref[place[AT_F] * 2 + y, :, rows : 2 * rows].astype(F32)
     for to in range(4):
 
         @pl.when(place[AT_F] == to)
         def _():
             for k in range(6):
-                slot = place[AT_SLOT + (6 * to + k) % 8]
-                qkv_ref[:, k * rows : (k + 1) * rows] = full[slot, :, :rows].astype(F32)
+                qkv_ref[:, k * rows : (k + 1) * rows] = got_ref[(6 * to + k) % 8, :, :rows].astype(F32)
 
 
 def output_kernel(place, b2_0, b2_1, b2_2, b2_3, tok_ref, after_ref, mask_ref, sel_ref, mod_ref, out_ref):
@@ -1555,6 +1537,7 @@
         gin_own, gin_far, grad_qkv, attn_in, to_sum, b2_terms = lax.optimization_barrier(
             (gin_own, gin_far, grad_qkv, attn_in, to_sum, b2_terms)
         )
+        gin_terms = scatter_sum(gin_own, gin_far)
         (attn_g,) = call(
             "weights",
             8,
@@ -1571,6 +1554,26 @@
             ],
         )
         terms = lax.all_to_all(to_sum, names, 0, 0, tiled=True)
+        attn_g, terms, fc_z, gin_terms = lax.optimization_barrier((attn_g, terms, fc_z, gin_terms))
+        (mlp_send,) = call(
+            "mlp_split", 3, functools.partial(mlp_split_kernel, rows), [fc_z], [shaped((8, rows, wide(3 * rows)), BF)]
+        )
+        mlp_got = lax.all_to_all(mlp_send, group, 0, 0, tiled=True)
+        attn_z = lax.psum_scatter(attn_g, "z", scatter_dimension=0, tiled=True)
+
+        (sums,) = call("grad_sum", 2, grad_sum_kernel, [terms], [shaped((8, d), BF)])
+        sums, mlp_got = lax.optimization_barrier((over_z(sums), mlp_got))
+        total = to_slab(jnp.stack(sums))
+
+        (ada_weight_grad, condition_grad, ada_bias_grad, qkv_bias_grad, proj_bias_grad, fc1_bias_grad, fc2_bias_grad) = call(
+            "ada",
+            5,
+            functools.partial(ada_kernel, d),
+            [total, act_rows, silu_slope, ada_weight],
+            [shaped((rows, 6 * d)), shaped((samples, rows))]
+            + [shaped((n // 128, 128)) for n in (6 * d, 2 * d, d, ff, d)],
+        )
+
         own_specs = [whole((T, 1)), whole((T, 128)), whole(mod.shape)]
         (result,) = call(
             "output",
@@ -1580,52 +1583,20 @@
             [shaped((T, d), BF)],
             ins=[whole((T, d))] * 6 + own_specs,
         )
-        def split(name, kernel, summed, lanes):
-            return call(
-                name,
-                3,
-                functools.partial(kernel, rows),
-                [summed],
-                [shaped((rows, n), BF) for n in lanes],
-                scratch=[pltpu.VMEM((8, rows, max(lanes)), BF)],
-            )
-
-        def join(name, kernel, pieces, outs):
-            return call(
-                name,
-                3,
-                functools.partial(kernel, rows),
-                pieces,
-                outs,
-                scratch=[pltpu.VMEM((8, rows, max(piece.shape[1] for piece in pieces)), BF)],
-            )
-
-        attn_g, fc_z, terms, result = lax.optimization_barrier((attn_g, fc_z, terms, result))
-        attn_z = lax.psum_scatter(attn_g, "z", scatter_dimension=0, tiled=True)
-        gin_terms = scatter_sum(gin_own, gin_far)
-
-        (sums,) = call("grad_sum", 2, grad_sum_kernel, [terms], [shaped((8, d), BF)])
-        total = to_slab(jnp.stack(over_z(sums)))
-
-        (ada_weight_grad, condition_grad, ada_bias_grad, qkv_bias_grad, proj_bias_grad, fc1_bias_grad, fc2_bias_grad) = call(
-            "ada",
-            5,
-            functools.partial(ada_kernel, d),
-            [total, act_rows, silu_slope, ada_weight],
-            [shaped((rows, 6 * d)), shaped((samples, rows))]
-            + [shaped((n // 128, 128)) for n in (6 * d, 2 * d, d, ff, d)],
-        )
-
-        mlp_send = split("mlp_split", mlp_split_kernel, fc_z, [wide(rows if dy else 3 * rows) for _, _, dy in offsets])
-        mlp_got = exchange(mlp_send)
-        attn_z, ada_weight_grad = lax.optimization_barrier((attn_z, ada_weight_grad))
-        attn_send = split("attn_split", attn_split_kernel, attn_z, [wide(rows if dc or dx else 2 * rows) for dc, dx, _ in offsets])
-        attn_got = exchange(attn_send)
-        gin_terms = lax.optimization_barrier((gin_terms, attn_send[0]))[0]
-        mlp_got = lax.optimization_barrier((mlp_got, attn_send[0]))[0]
-        fc1_weight_grad, fc2_weight_grad = join(
-            "mlp_join", mlp_join_kernel, mlp_got, [shaped((rows, ff // 4)), shaped((d // 4, 4 * rows))]
-        )
+        attn_z, result = lax.optimization_barrier((attn_z, result))
+        (attn_send,) = call(
+            "attn_split", 3, functools.partial(attn_split_kernel, rows), [attn_z], [shaped((8, rows, wide(2 * rows)), BF)]
+        )
+        attn_got = lax.all_to_all(attn_send, group, 0, 0, tiled=True)
+        mlp_got = lax.optimization_barrier((mlp_got, attn_send))[0]
+        fc1_weight_grad, fc2_weight_grad = call(
+            "mlp_join",
+            3,
+            functools.partial(mlp_join_kernel, rows),
+            [mlp_got],
+            [shaped((rows, ff // 4)), shaped((d // 4, 4 * rows))],
+        )
+        gin_terms = lax.optimization_barrier((gin_terms, attn_send))[0]
         (input_grad,) = call(
             "input_grad",
             3,
@@ -1634,9 +1605,12 @@
             [shaped((T, d))],
             ins=[whole((T, d))] * 7 + own_specs,
         )
-
-        qkv_weight_grad, proj_weight_grad = join(
-            "attn_join", attn_join_kernel, attn_got, [shaped((rows, 3 * d // 4)), shaped((rows, d // 4))]
+        qkv_weight_grad, proj_weight_grad = call(
+            "attn_join",
+            3,
+            functools.partial(attn_join_kernel, rows),
+            [attn_got],
+            [shaped((rows, 3 * d // 4)), shaped((rows, d // 4))],
         )
 
         shape = (frames, columns, d)

time: 326 us -> 317 us (0.972)
  starting transfers between devices: 70.3 us -> 65 us
    ppermute x52 -> x38, starting transfers between devices: 45.1 us -> 32.7 us  [swap(): return lax.ppermute(a, axes, [(k, n - 1 - k) for k in range(n)])]
    ppermute x52 -> x38, waiting for transfers between devices: 80.7 us -> 71.3 us  [swap(): return lax.ppermute(a, axes, [(k, n - 1 - k) for k in range(n)])]
    all_to_all x0 -> x2, starting transfers between devices: none -> 7.22 us  [the longest x1 3.64 us: local(): attn_got = lax.all_to_all(attn_send, group, 0, 0, tiled=True)]
  transfers between devices with their start and end apart: 67 -> 55, of which waited for: 30 -> 31; matrix products, arithmetic and copies ran while one was open for 3% -> 3% of each run, Pallas kernels for 24% -> 25%
where the time goes in v1:
time: 317 us; the launch traced here: 316 us
  Pallas kernels  120 us (38%)
  waiting for transfers between devices  99.8 us (31%)
  starting transfers between devices  65 us (21%)
  between operations  14.3 us (5%)
  local copies, waits for them, and re-layouts  11 us (3%)
  other arithmetic  5.81 us (2%)
    pallas_call x16, Pallas kernels, call(): pl.pallas_call(kernel, grid_spec=pltpu.PrefetchScalarGridSpec(num_scalar_...  120 us
    ppermute x38, waiting for transfers between devices, swap(): return lax.ppermute(a, axes, [(k, n - 1 - k) for k in range(n)])  71.3 us
    ppermute x38, starting transfers between devices, swap(): return lax.ppermute(a, axes, [(k, n - 1 - k) for k in range(n)])  32.7 us
    ppermute x6, waiting for transfers between devices, from_z(): return lax.ppermute(a, ('z',), [(z, z ^ apart) for z in range(4)])  11.5 us
    ppermute x6, starting transfers between devices, from_z(): return lax.ppermute(a, ('z',), [(z, z ^ apart) for z in range(4)])  10 us
    all_to_all x2, starting transfers between devices, to_slab(): lax.all_to_all(jnp.broadcast_to(a, (8, *a.shape)), group, 0, 0, tiled=True)  7.08 us
  transfers between devices with their start and end apart: 55, of which 31 were waited for; matrix products, arithmetic and copies ran while one was open for 3% of the time, Pallas kernels for 25%

profile of v1, /device:TPU:0, one launch (start us, length us, event | category | flops | bytes accessed | tf_op | source)
XLA Modules:
  0.0 315.7 jit_solution(8217862982263189595)
XLA Ops:
  8.5 5.8 %prepare.1 = (bf16[8,8,1152]{2,1,0:T(8,128)(2,1)}, bf16[32,256]{1,0:T(8,128)(2,1)}, f32[32,256]{1,0:T(8,128)}, bf16[144,512]{1,0:T(8,128)(2,1)}, bf16[144,640]{1...) custom-call(s32[40]{0:T(128)} %dynamic-slice_bitcast_fusion.place, ...), custom_call_target="tpu_custom_call" | custom-call | flops 1000 | bytes 1000 | tf_op jit(solution)/shard_map/prepare/pallas_call | solution.py:1344
  17.4 5.0 %all-to-all-start = ((bf16[8,8,1152]{2,1,0:T(8,128)(2,1)}), bf16[8,8,1152]{2,1,0:T(8,128)(2,1)S(1)}, u32[]{:S(2)}, u32[]{:S(2)}) async-start(bf16[8,8,1152]{2,1,0:T(8,128)(2,1)} %get-tuple-element.124), calls=%async_computation | async-start | bytes 294912 | tf_op jit(solution)/shard_map/all_to_all | solution.py:1385
  47.2 11.6 %collective-permute-done.6 = bf16[272,1152]{1,0:T(8,128)(2,1)S(1)} collective-permute-done((bf16[272,1152]{1,0:T(8,128)(2,1)S(1)}, bf16[272,1152]{1,0:T(8,128)(2,1)S(1)}, u32[]{:S(2)}, u32[]{:S(2)}) %collective-permute-start.6) | collective-permute-done | bytes 626720 | tf_op jit(solution)/shard_map/ppermute | solution.py:1278
  66.3 3.5 %all-to-all-start.1 = ((bf16[8,4,8,1152]{3,2,1,0:T(8,128)(2,1)}), bf16[8,4,8,1152]{3,2,1,0:T(8,128)(2,1)S(1)}, u32[]{:S(2)}, u32[]{:S(2)}) async-start(bf16[8,4,8,1152]{3,2,1,0:T(8,128)(2,1)} %broadcast_in_dim.6), calls=%async_computation.1 | async-start | bytes 1179648 | tf_op jit(solution)/shard_map/all_to_all | solution.py:1298
  70.2 5.9 %collective-permute-done.8.refs_1_ = bf16[4,144,288]{2,1,0:T(8,128)(2,1)} collective-permute-done((bf16[4,144,288]{2,1,0:T(8,128)(2,1)}, bf16[4,144,288]{2,1,0:T(8,128)(2,1)}, u32[]{:S(2)}, u32[]{:S(2)}) %collective-permute-start.8) | collective-permute-done | bytes 331808 | tf_op jit(solution)/shard_map/ppermute | solution.py:1278
  76.7 9.6 %collective-permute-done.10.refs_3_ = bf16[4,144,288]{2,1,0:T(8,128)(2,1)} collective-permute-done((bf16[4,144,288]{2,1,0:T(8,128)(2,1)}, bf16[4,144,288]{2,1,0:T(8,128)(2,1)}, u32[]{:S(2)}, u32[]{:S(2)}) %collective-permute-start.10) | collective-permute-done | bytes 331808 | tf_op jit(solution)/shard_map/ppermute | solution.py:1278
  89.1 5.4 %proj.1.refs_13_.refs_10_ = bf16[1152,1152]{1,0:T(8,128)(2,1)} custom-call(s32[40]{0:T(128)} %dynamic-slice_bitcast_fusion.place, bf16[4,144,288]{2,1,0:T(8,128)(2,1)} %slice.83.refs_0_, bf16[4,144,288]{2,1,0:T(8,128)(2,1)} %collective-permute-done.8.refs_1_, bf16[4,144,288]{2,1,0:T(8,128)(2,1)} %collective-permute-done.9.refs_2_, ...), custom_call_target="tpu_custom_call" | custom-call | flops 1000 | bytes 1000 | tf_op jit(solution)/shard_map/proj/pallas_call | solution.py:1344
  95.3 12.8 %attend.1 = (bf16[144,1024]{1,0:T(8,128)(2,1)}, bf16[1024,512]{1,0:T(8,128)(2,1)}, bf16[1024,128]{1,0:T(8,128)(2,1)}, bf16[32,1024]{1,0:T(8,128)(2,1)}, bf16[115...) custom-call(s32[40]{0:T(128)} %dynamic-slice_bitcast_fusion.place, bf16[4,272,1152]{2,1,0:T(8,128)(2,1)} %copy-done, ...), custom_call_target="tpu_custom_call" | custom-call | flops 1000 | bytes 1000 | tf_op jit(solution)/shard_map/attend/pallas_call | solution.py:1344
  111.7 5.8 %collective-permute-done.15.refs_1_ = bf16[144,1024]{1,0:T(8,128)(2,1)S(1)} collective-permute-done((bf16[144,1024]{1,0:T(8,128)(2,1)}, bf16[144,1024]{1,0:T(8,128)(2,1)S(1)}, u32[]{:S(2)}, u32[]{:S(2)}) %collective-permute-start.15) | collective-permute-done | bytes 294944 | tf_op jit(solution)/shard_map/ppermute | solution.py:1278
  119.6 5.4 %collective-permute-done.17.refs_3_ = bf16[144,1024]{1,0:T(8,128)(2,1)S(1)} collective-permute-done((bf16[144,1024]{1,0:T(8,128)(2,1)}, bf16[144,1024]{1,0:T(8,128)(2,1)S(1)}, u32[]{:S(2)}, u32[]{:S(2)}) %collective-permute-start.17) | collective-permute-done | bytes 294944 | tf_op jit(solution)/shard_map/ppermute | solution.py:1278
  126.6 3.6 %all-gather.11.cloned.1.call-done = bf16[8,144,640]{2,1,0:T(8,128)(2,1)} async-done(((bf16[2,144,640]{2,1,0:T(8,128)(2,1)}), bf16[8,144,640]{2,1,0:T(8,128)(2,1)}) %all-gather.11.cloned.1.call-update) | async-done | bytes 1474576 | tf_op jit(solution)/shard_map/all_gather | solution.py:1417
  130.2 31.6 %mlp.1 = (bf16[4,128,1152]{2,1,0:T(8,128)(2,1)}, bf16[4,128,1152]{2,1,0:T(8,128)(2,1)}, bf16[4,128,1152]{2,1,0:T(8,128)(2,1)}, bf16[4,128,1152]{2,1,0:T(8,128)(2...) custom-call(s32[40]{0:T(128)} %dynamic-slice_bitcast_fusion.place, ...), custom_call_target="tpu_custom_call" | custom-call | flops 1000 | bytes 1000 | tf_op jit(solution)/shard_map/mlp/pallas_call | solution.py:1344
  169.4 5.6 %collective-permute-done.23.refs_1_ = bf16[128,1152]{1,0:T(8,128)(2,1)S(1)} collective-permute-done((bf16[128,1152]{1,0:T(8,128)(2,1)S(1)}, bf16[128,1152]{1,0:T(8,128)(2,1)S(1)}, u32[]{:S(2)}, u32[]{:S(2)}) %collective-permute-start.23) | collective-permute-done | bytes 294944 | tf_op jit(solution)/shard_map/ppermute | solution.py:1278
  177.3 5.2 %collective-permute-done.25.refs_3_ = bf16[128,1152]{1,0:T(8,128)(2,1)S(1)} collective-permute-done((bf16[128,1152]{1,0:T(8,128)(2,1)S(1)}, bf16[128,1152]{1,0:T(8,128)(2,1)S(1)}, u32[]{:S(2)}, u32[]{:S(2)}) %collective-permute-start.25) | collective-permute-done | bytes 294944 | tf_op jit(solution)/shard_map/ppermute | solution.py:1278
  183.2 6.1 %middle.1 = (bf16[2,144,128]{2,1,0:T(8,128)(2,1)}, bf16[2,144,128]{2,1,0:T(8,128)(2,1)}, bf16[2,144,128]{2,1,0:T(8,128)(2,1)}, bf16[2,144,128]{2,1,0:T(8,128)(2,...) custom-call(s32[40]{0:T(128)} %dynamic-slice_bitcast_fusion.place, ...), custom_call_target="tpu_custom_call" | custom-call | flops 1000 | bytes 1000 | tf_op jit(solution)/shard_map/middle/pallas_call | solution.py:1344
  205.2 19.0 %back.1 = (bf16[4,128,1152]{2,1,0:T(8,128)(2,1)}, bf16[4,128,1152]{2,1,0:T(8,128)(2,1)}, bf16[1024,512]{1,0:T(8,128)(2,1)}, bf16[1024,1152]{1,0:T(8,128)(2,1)}, bf16[32,8,1152]{2,1,0:T(8,128)(2,1)}) custom-call(s32[40]{0:T(128)} %dynamic-slice_bitcast_fusion.place, bf16[2,144,128]{2,1,0:T(8,128)(2,1)} %get-tuple-element.168.refs_0_.refs_8_, ...), custom_call_target="tpu_custom_call" | custom-call | flops 1000 | bytes 1000 | tf_op jit(solution)/shard_map/back/pallas_call | solution.py:1344
  232.9 7.9 %weights.1 = bf16[1152,640]{1,0:T(8,128)(2,1)} custom-call(s32[40]{0:T(128)} %dynamic-slice_bitcast_fusion.place, bf16[144,1024]{1,0:T(8,128)(2,1)} %get-tuple-element.148.refs_0_, bf16[144,1024]{1,0:T(8,128)(2,1)} %copy-done.7, bf16[144,1024]{1,0:T(8,128)(2,1)} %copy-done.8, bf16[144,1024]{1,0:T(8,128)(2,1)} %copy-done.9, bf16[144,1024]{1,0:T(8,128)(2,1)} %copy-done.10, ...), custom_call_target="tpu_custom_call" | custom-call | flops 1000 | bytes 1000 | tf_op jit(solution)/shard_map/weights/pallas_call | solution.py:1344
  240.8 5.0 %all-to-all-done.2.terms_ref = bf16[32,8,1152]{2,1,0:T(8,128)(2,1)S(1)} async-done(((bf16[32,8,1152]{2,1,0:T(8,128)(2,1)}), bf16[32,8,1152]{2,1,0:T(8,128)(2,1)S(1)}, u32[]{:S(2)}, u32[]{:S(2)}) %all-to-all-start.2) | async-done | bytes 589856 | tf_op jit(solution)/shard_map/all_to_all | solution.py:1556
  245.9 4.9 %collective-permute-done.40.gin_3 = bf16[128,1152]{1,0:T(8,128)(2,1)S(1)} collective-permute-done((bf16[128,1152]{1,0:T(8,128)(2,1)S(1)}, bf16[128,1152]{1,0:T(8,128)(2,1)S(1)}, u32[]{:S(2)}, u32[]{:S(2)}) %collective-permute-start.40) | collective-permute-done | bytes 294944 | tf_op jit(solution)/shard_map/ppermute | solution.py:1278
  254.0 3.6 %all-to-all-start.3 = ((bf16[8,144,512]{2,1,0:T(8,128)(2,1)}), bf16[8,144,512]{2,1,0:T(8,128)(2,1)S(1)}, u32[]{:S(2)}, u32[]{:S(2)}) async-start(bf16[8,144,512]{2,1,0:T(8,128)(2,1)} %mlp_split.1), calls=%async_computation.5 | async-start | bytes 2359296 | tf_op jit(solution)/shard_map/all_to_all | solution.py:1561
  288.2 3.6 %all-to-all-start.5 = ((bf16[8,144,384]{2,1,0:T(8,128)(2,1)}), bf16[8,144,384]{2,1,0:T(8,128)(2,1)S(1)}, u32[]{:S(2)}, u32[]{:S(2)}) async-start(bf16[8,144,384]{2,1,0:T(8,128)(2,1)} %attn_split.1), calls=%async_computation.7 | async-start | bytes 1769472 | tf_op jit(solution)/shard_map/all_to_all | solution.py:1590
  291.8 5.7 %ada.1 = (f32[144,6912]{1,0:T(8,128)}, f32[32,144]{1,0:T(8,128)}, f32[54,128]{1,0:T(8,128)}, f32[18,128]{1,0:T(8,128)}, f32[9,128]{1,0:T(8,128)}, /*index=5*/f32[36,128]{1,0:T(8,128)}, f32[9,128]{1,0:T(8,128)}) custom-call(s32[40]{0:T(128)} %dynamic-slice_bitcast_fusion.place, bf16[8,4,8,1152]{3,2,1,0:T(8,128)(2,1)} %copy-done.6, ...), custom_call_target="tpu_custom_call" | custom-call | flops 1000 | bytes 1000 | tf_op jit(solution)/shard_map/ada/pallas_call | solution.py:1344
  297.5 3.9 %mlp_join.1 = (f32[144,1152]{1,0:T(8,128)}, f32[288,576]{1,0:T(8,128)}) custom-call(s32[40]{0:T(128)} %dynamic-slice_bitcast_fusion.place, bf16[8,144,512]{2,1,0:T(8,128)(2,1)} %copy-done.1), custom_call_target="tpu_custom_call" | custom-call | flops 1000 | bytes 1000 | tf_op jit(solution)/shard_map/mlp_join/pallas_call | solution.py:1344
  301.4 3.9 %input_grad.1 = f32[128,1152]{1,0:T(8,128)} custom-call(s32[40]{0:T(128)} %dynamic-slice_bitcast_fusion.place, bf16[128,1152]{1,0:T(8,128)(2,1)} %get-tuple-element.209.gin_0, bf16[128,1152]{1,0:T(8,128)(2,1)} %copy-done.28, bf16[128,1152]{1,0:T(8,128)(2,1)} %copy-done.29, bf16[128,1152]{1,0:T(8,128)(2,1)} %copy-done.30, bf16[128,1152]{1,0:T(8,128)(2,1)} %bitcast.68, ...), custom_call_target="tpu_custom_call" | custom-call | flops 1000 | bytes 1000 | tf_op jit(solution)/shard_map/input_grad/pallas_call | solution.py:1344
  (209 shorter events, 121.0 us)
Async XLA Ops:
  7.2 52.7 %all-gather.7.cloned.1.call-start = ((), (), s32[]{:S(2)}) async-start(), calls=%async_computation.10 | async-start | bytes 2211840 | tf_op jit(solution)/shard_map/all_gather | solution.py:1384
  22.4 72.2 %all-gather.9.cloned.1.call-start = ((), (), s32[]{:S(2)}) async-start(), calls=%async_computation.11 | async-start | bytes 1474560 | tf_op jit(solution)/shard_map/all_gather | solution.py:1391
  29.9 17.1 %collective-permute-start.4 = (bf16[272,1152]{1,0:T(8,128)(2,1)S(1)}, bf16[272,1152]{1,0:T(8,128)(2,1)S(1)}, u32[]{:S(2)}, u32[]{:S(2)}) collective-permute-start(bf16[272,1152]{1,0:T(8,128)(2,1)S(1)} %copy-done.3), channel_id=1, source_target_pairs={{0,1},{1,0},{2,3},{3,2},{4,5},{5,4},{6,7},{7,6},{8,9},{9,8},{10,11... | collective-permute-start | bytes 1880072 | tf_op jit(solution)/shard_map/ppermute | solution.py:1278
  30.1 17.1 %collective-permute-start.5 = (bf16[272,1152]{1,0:T(8,128)(2,1)S(1)}, bf16[272,1152]{1,0:T(8,128)(2,1)S(1)}, u32[]{:S(2)}, u32[]{:S(2)}) collective-permute-start(bf16[272,1152]{1,0:T(8,128)(2,1)S(1)} %copy-done.3), channel_id=1, source_target_pairs={{0,16},{16,0},{1,17},{17,1},{2,18},{18,2},{3,19},{19,3},{4,20},{20... | collective-permute-start | bytes 1880072 | tf_op jit(solution)/shard_map/ppermute | solution.py:1278
  31.8 27.0 %collective-permute-start.6 = (bf16[272,1152]{1,0:T(8,128)(2,1)S(1)}, bf16[272,1152]{1,0:T(8,128)(2,1)S(1)}, u32[]{:S(2)}, u32[]{:S(2)}) collective-permute-start(bf16[272,1152]{1,0:T(8,128)(2,1)S(1)} %copy-done.3), channel_id=1, source_target_pairs={{0,17},{1,16},{16,1},{17,0},{2,19},{3,18},{18,3},{19,2},{4,21},{5,... | collective-permute-start | bytes 1880072 | tf_op jit(solution)/shard_map/ppermute | solution.py:1278
  59.2 35.3 %collective-permute-start.7 = (bf16[4,272,1152]{2,1,0:T(8,128)(2,1)S(1)}, bf16[4,272,1152]{2,1,0:T(8,128)(2,1)}, u32[]{:S(2)}, u32[]{:S(2)}) collective-permute-start(bf16[4,272,1152]{2,1,0:T(8,128)(2,1)S(1)} %pad_maximum_fusion.tok_near.refs_8_), channel_id=1, source_target_pairs={{0,8},{8,0},{1,9},{9,1},{2,10},{10,2},{3,11},{11,3},{4,12},{12,4},... | collective-permute-start | bytes 7520264 | tf_op jit(solution)/shard_map/ppermute | solution.py:1278
  61.9 14.3 %collective-permute-start.8 = (bf16[4,144,288]{2,1,0:T(8,128)(2,1)}, bf16[4,144,288]{2,1,0:T(8,128)(2,1)}, u32[]{:S(2)}, u32[]{:S(2)}) collective-permute-start(bf16[4,144,288]{2,1,0:T(8,128)(2,1)} %slice.83.refs_0_), channel_id=1, source_target_pairs={{0,1},{1,0},{2,3},{3,2},{4,5},{5,4},{6,7},{7,6},{8,9},{9,8},{10,11... | collective-permute-start | bytes 995336 | tf_op jit(solution)/shard_map/ppermute | solution.py:1278
  64.7 21.6 %collective-permute-start.10 = (bf16[4,144,288]{2,1,0:T(8,128)(2,1)}, bf16[4,144,288]{2,1,0:T(8,128)(2,1)}, u32[]{:S(2)}, u32[]{:S(2)}) collective-permute-start(bf16[4,144,288]{2,1,0:T(8,128)(2,1)} %slice.83.refs_0_), channel_id=1, source_target_pairs={{0,17},{1,16},{16,1},{17,0},{2,19},{3,18},{18,3},{19,2},{4,21},{5,... | collective-permute-start | bytes 995336 | tf_op jit(solution)/shard_map/ppermute | solution.py:1278
  66.3 28.2 %all-to-all-start.1 = ((bf16[8,4,8,1152]{3,2,1,0:T(8,128)(2,1)}), bf16[8,4,8,1152]{3,2,1,0:T(8,128)(2,1)S(1)}, u32[]{:S(2)}, u32[]{:S(2)}) async-start(bf16[8,4,8,1152]{3,2,1,0:T(8,128)(2,1)} %broadcast_in_dim.6), calls=%async_computation.1 | async-start | bytes 1179648 | tf_op jit(solution)/shard_map/all_to_all | solution.py:1298
  69.8 60.3 %all-gather.11.cloned.1.call-start = ((), (), s32[]{:S(2)}) async-start(), calls=%async_computation.12 | async-start | bytes 1843200 | tf_op jit(solution)/shard_map/all_gather | solution.py:1417
  69.9 16.4 %collective-permute-start.11 = (bf16[4,144,288]{2,1,0:T(8,128)(2,1)}, bf16[4,144,288]{2,1,0:T(8,128)(2,1)S(1)}, u32[]{:S(2)}, u32[]{:S(2)}) collective-permute-start(bf16[4,144,288]{2,1,0:T(8,128)(2,1)} %slice.83.refs_0_), channel_id=1, source_target_pairs={{0,8},{8,0},{1,9},{9,1},{2,10},{10,2},{3,11},{11,3},{4,12},{12,4},... | collective-permute-start | bytes 995336 | tf_op jit(solution)/shard_map/ppermute | solution.py:1278
  94.6 156.2 %reduce-scatter.3.cloned.1.call-start = ((), (), s32[]{:S(2)}) async-start(), calls=%async_computation.8 | async-start | bytes 3686400 | tf_op jit(solution)/shard_map/reduce_scatter | solution.py:1500
  111.0 14.0 %collective-permute-start.17 = (bf16[144,1024]{1,0:T(8,128)(2,1)}, bf16[144,1024]{1,0:T(8,128)(2,1)S(1)}, u32[]{:S(2)}, u32[]{:S(2)}) collective-permute-start(bf16[144,1024]{1,0:T(8,128)(2,1)} %get-tuple-element.148.refs_0_), channel_id=1, source_target_pairs={{0,17},{1,16},{16,1},{17,0},{2,19},{3,18},{18,3},{19,2},{4,21},{5,... | collective-permute-start | bytes 884744 | tf_op jit(solution)/shard_map/ppermute | solution.py:1278
  163.0 29.8 %collective-permute-start.33 = (bf16[4,128,1152]{2,1,0:T(8,128)(2,1)S(1)}, bf16[4,128,1152]{2,1,0:T(8,128)(2,1)S(1)}, u32[]{:S(2)}, u32[]{:S(2)}) collective-permute-start(bf16[4,128,1152]{2,1,0:T(8,128)(2,1)S(1)} %copy-done.42), channel_id=1, source_target_pairs={{0,8},{8,0},{1,9},{9,1},{2,10},{10,2},{3,11},{11,3},{4,12},{12,4},... | collective-permute-start | bytes 3538952 | tf_op jit(solution)/shard_map/ppermute | solution.py:1278
  201.7 22.6 %collective-permute-start.34 = (bf16[128,1152]{1,0:T(8,128)(2,1)S(1)}, bf16[128,1152]{1,0:T(8,128)(2,1)S(1)}, u32[]{:S(2)}, u32[]{:S(2)}) collective-permute-start(bf16[128,1152]{1,0:T(8,128)(2,1)S(1)} %get-tuple-element.189), channel_id=1, source_target_pairs={{0,1},{1,0},{2,3},{3,2},{4,5},{5,4},{6,7},{7,6},{8,9},{9,8},{10,11... | collective-permute-start | bytes 884744 | tf_op jit(solution)/shard_map/ppermute | solution.py:1278
  201.7 22.6 %collective-permute-start.35 = (bf16[128,1152]{1,0:T(8,128)(2,1)S(1)}, bf16[128,1152]{1,0:T(8,128)(2,1)S(1)}, u32[]{:S(2)}, u32[]{:S(2)}) collective-permute-start(bf16[128,1152]{1,0:T(8,128)(2,1)S(1)} %get-tuple-element.190), channel_id=1, source_target_pairs={{0,16},{16,0},{1,17},{17,1},{2,18},{18,2},{3,19},{19,3},{4,20},{20... | collective-permute-start | bytes 884744 | tf_op jit(solution)/shard_map/ppermute | solution.py:1278
  203.7 20.7 %collective-permute-start.36 = (bf16[128,1152]{1,0:T(8,128)(2,1)S(1)}, bf16[128,1152]{1,0:T(8,128)(2,1)S(1)}, u32[]{:S(2)}, u32[]{:S(2)}) collective-permute-start(bf16[128,1152]{1,0:T(8,128)(2,1)S(1)} %get-tuple-element.191), channel_id=1, source_target_pairs={{0,17},{1,16},{16,1},{17,0},{2,19},{3,18},{18,3},{19,2},{4,21},{5,... | collective-permute-start | bytes 884744 | tf_op jit(solution)/shard_map/ppermute | solution.py:1278
  225.3 20.6 %all-to-all-start.2 = ((bf16[32,8,1152]{2,1,0:T(8,128)(2,1)}), bf16[32,8,1152]{2,1,0:T(8,128)(2,1)S(1)}, u32[]{:S(2)}, u32[]{:S(2)}) async-start(bf16[32,8,1152]{2,1,0:T(8,128)(2,1)} %get-tuple-element.194), calls=%async_computation.2 | async-start | bytes 1179648 | tf_op jit(solution)/shard_map/all_to_all | solution.py:1556
  227.9 57.0 %reduce-scatter.5.cloned.1.call-start = ((), (), s32[]{:S(2)}) async-start(), calls=%async_computation.9 | async-start | bytes 1843200 | tf_op jit(solution)/shard_map/reduce_scatter | solution.py:1562
  229.5 16.4 %collective-permute-start.38 = (bf16[128,1152]{1,0:T(8,128)(2,1)}, bf16[128,1152]{1,0:T(8,128)(2,1)S(1)}, u32[]{:S(2)}, u32[]{:S(2)}) collective-permute-start(bf16[128,1152]{1,0:T(8,128)(2,1)} %get-tuple-element.237), channel_id=1, source_target_pairs={{0,1},{1,0},{2,3},{3,2},{4,5},{5,4},{6,7},{7,6},{8,9},{9,8},{10,11... | collective-permute-start | bytes 884744 | tf_op jit(solution)/shard_map/ppermute | solution.py:1278
  230.8 15.1 %collective-permute-start.39 = (bf16[128,1152]{1,0:T(8,128)(2,1)S(1)}, bf16[128,1152]{1,0:T(8,128)(2,1)S(1)}, u32[]{:S(2)}, u32[]{:S(2)}) collective-permute-start(bf16[128,1152]{1,0:T(8,128)(2,1)S(1)} %get-tuple-element.236), channel_id=1, source_target_pairs={{0,16},{16,0},{1,17},{17,1},{2,18},{18,2},{3,19},{19,3},{4,20},{20... | collective-permute-start | bytes 884744 | tf_op jit(solution)/shard_map/ppermute | solution.py:1278
  232.2 18.5 %collective-permute-start.40 = (bf16[128,1152]{1,0:T(8,128)(2,1)S(1)}, bf16[128,1152]{1,0:T(8,128)(2,1)S(1)}, u32[]{:S(2)}, u32[]{:S(2)}) collective-permute-start(bf16[128,1152]{1,0:T(8,128)(2,1)S(1)} %get-tuple-element.235), channel_id=1, source_target_pairs={{0,17},{1,16},{16,1},{17,0},{2,19},{3,18},{18,3},{19,2},{4,21},{5,... | collective-permute-start | bytes 884744 | tf_op jit(solution)/shard_map/ppermute | solution.py:1278
  254.0 19.5 %all-to-all-start.3 = ((bf16[8,144,512]{2,1,0:T(8,128)(2,1)}), bf16[8,144,512]{2,1,0:T(8,128)(2,1)S(1)}, u32[]{:S(2)}, u32[]{:S(2)}) async-start(bf16[8,144,512]{2,1,0:T(8,128)(2,1)} %mlp_split.1), calls=%async_computation.5 | async-start | bytes 2359296 | tf_op jit(solution)/shard_map/all_to_all | solution.py:1561
  288.2 17.1 %all-to-all-start.5 = ((bf16[8,144,384]{2,1,0:T(8,128)(2,1)}), bf16[8,144,384]{2,1,0:T(8,128)(2,1)S(1)}, u32[]{:S(2)}, u32[]{:S(2)}) async-start(bf16[8,144,384]{2,1,0:T(8,128)(2,1)} %attn_split.1), calls=%async_computation.7 | async-start | bytes 1769472 | tf_op jit(solution)/shard_map/all_to_all | solution.py:1590
  (74 other events, 479.5 us)
Sparse Core Ops, SparseCore 0:
  17.5 42.3 all-gather.6
  62.0 29.1 all-gather.8
  94.7 35.4 all-gather.10
  161.9 56.0 reduce-scatter.2
  250.9 33.9 reduce-scatter.4

commit v2 on v1

--- a/solution.py
+++ b/solution.py
@@ -800,7 +800,7 @@
                    part_ref, act_ref, slope_ref, qkv_mine, fc1_mine, send_out, fc2_out, tok_out, act_all):
     rows = ada_ref.shape[0]
     cols = 2 * rows
-    for ref in (qkv_mine, fc1_mine, send_out, fc2_out):
+    for ref in (qkv_mine, send_out, fc2_out):
         ref[...] = jnp.zeros_like(ref)
     act_ref[...] = jnp.zeros_like(act_ref)
     slope_ref[...] = jnp.zeros_like(slope_ref)
@@ -810,7 +810,7 @@
         def _():
             fc2_out[:, d : d + cols] = proj_ref[:, f * cols : (f + 1) * cols]
             for y in range(2):
-                for q_out, at_q, f_out, want in ((qkv_mine, 0, fc1_mine, y), (send_out, wide(4 * rows), send_out, 1 - y)):
+                for q_out, at_q, f_out, want in ((qkv_mine, 0, fc1_mine, y), (send_out, 512, send_out, 1 - y)):
 
                     @pl.when(place[AT_Y] == want)
                     def _():
@@ -819,7 +819,11 @@
                             q_out[:, at_q + t * rows : at_q + (t + 1) * rows] = qkv_ref[:, at : at + rows]
                         for z in range(4):
                             at = ((z * 2 + y) * 4 + f) * rows
-                            f_out[:, z * rows : (z + 1) * rows] = fc1_ref[:, at : at + rows]
+                            kept = min(rows, 512 - z * rows)
+                            f_out[:, z * rows : z * rows + kept] = fc1_ref[:, at : at + kept]
+                            if kept < rows:
+                                to = at_q + 3 * rows
+                                q_out[:, to : to + rows - kept] = fc1_ref[:, at + kept : at + rows]
 
     fc2_out[:, :d] = fc2_ref[at_rows(place[AT_F], rows)]
     row = lax.broadcasted_iota(jnp.int32, (d, rows), 0)
@@ -949,9 +953,9 @@
 def mlp_kernel(d, order, place, *refs):
     n = len(order)
     slots = refs[:n]
-    (tok_near, tok_far, sel_ref, selt_ref, mod_ref, proj_all, projb_ref, fc1_in, fc1b_ref, fc2_in, fc2b_ref) = refs[n : n + 11]
-    (b2_own, b2_far, gm_own, gm_far, fcg_ref, fc1bg_ref, fc2bg_ref, modg_ref, after_ref, branch_ref) = refs[n + 11 : n + 21]
-    (fc1a, fc2a, fc1_ref, fc2_ref, pb_row, f1_row, f2_row) = refs[n + 21 :]
+    (tok_near, tok_far, sel_ref, selt_ref, mod_ref, proj_all, projb_ref, fc1_in, fc1b_ref, fc2_in, fc2b_ref, w_ref) = refs[n : n + 12]
+    (b2_own, b2_far, gm_own, gm_far, fcg_ref, fc1bg_ref, fc2bg_ref, modg_ref, after_ref, branch_ref) = refs[n + 12 : n + 22]
+    (fc1a, fc2a, fc1_ref, fc2_ref, pb_row, f1_row, f2_row) = refs[n + 22 :]
     step = pl.program_id(0)
     size = sel_ref.shape[0] // 2
     rows = d // 8
@@ -963,8 +967,9 @@
         for z in range(4):
             for dy in range(2):
                 patch = z * 2 + lax.bitwise_xor(place[AT_Y], dy)
-                fc1_ref[at_rows(patch, rows), :] = fc1_in[z, dy, :, : 4 * rows]
+                fc1_ref[at_rows(patch, rows), :512] = fc1_in[z, dy]
             fc2_ref[z * rows : (z + 1) * rows] = fc2_in[z, :, :d]
+        fc1_ref[:, 512:] = w_ref[:, 3 * rows : 7 * rows - 512]
         pb_row[...] = row_of(projb_ref[...].astype(F32))
         f2_row[...] = jnp.where(place[AT_G] == 0, row_of(fc2b_ref[...].astype(F32)), 0.0)
         bias = row_of(fc1b_ref[...].astype(F32))
@@ -1145,7 +1150,7 @@
 def weights_kernel(d, width, order, place, *refs):
     n = len(order)
     slots, gas = refs[:n], refs[n : 2 * n]
-    (gqkv_ref, in_ref, grad_ref, qkva, proja, ga_all) = refs[2 * n :]
+    (gqkv_ref, in_ref, grad_ref, qkva, proja, ga_all, grad_all) = refs[2 * n :]
     step = pl.program_id(0)
     size = in_ref.shape[0] // 2
 
@@ -1163,10 +1168,16 @@
 
     @pl.when(step == pl.num_programs(0) - 1)
     def _():
-        grad_ref[:, : 3 * width] = qkva[...].astype(BF)
-        grad_ref[:, 4 * width :] = jnp.zeros((d, grad_ref.shape[1] - 4 * width), BF)
+        grad_all[:, : 3 * width] = qkva[...].astype(BF)
         for slot in range(n):
-            grad_ref[at_rows(place[AT_PART + slot], width), 3 * width : 4 * width] = proja[slot * width : (slot + 1) * width].astype(BF)
+            grad_all[at_rows(place[AT_PART + slot], width), 3 * width :] = proja[slot * width : (slot + 1) * width].astype(BF)
+        for z in range(4):
+            rows = slice(2 * z * width, 2 * (z + 1) * width)
+            for tile in range(4):
+                grad_ref[z, tile * 2 * width : (tile + 1) * 2 * width] = grad_all[rows, tile * 128 : (tile + 1) * 128]
+            for half in range(2):
+                rows = slice((2 * z + half) * width, (2 * z + half + 1) * width)
+                grad_ref[z, 8 * width :, half * 64 : (half + 1) * 64] = grad_all[rows, 512:]
 
 
 def ada_kernel(d, place, total_ref, act_ref, slope_ref, w_ref, wg_ref, cond_ref, ada_ref, qkv_ref, proj_ref, fc1_ref, fc2_ref):
@@ -1210,7 +1221,11 @@
         fc2_ref[:, f * rows : (f + 1) * rows] = got_ref[f * 2 + place[AT_Y], :, rows : 3 * rows].astype(F32).T
 
 
-def attn_split_kernel(rows, place, in_ref, out_ref):
+def attn_split_kernel(rows, place, packed_ref, out_ref, keep_ref, send_ref, in_ref):
+    for tile in range(4):
+        in_ref[:, tile * 128 : (tile + 1) * 128] = packed_ref[tile * 2 * rows : (tile + 1) * 2 * rows]
+    for half in range(2):
+        in_ref[half * rows : (half + 1) * rows, 512:] = packed_ref[8 * rows :, half * 64 : (half + 1) * 64]
     out_ref[...] = jnp.zeros_like(out_ref)
     for part in range(8):
 
@@ -1220,12 +1235,15 @@
                 block = in_ref[y * rows : (y + 1) * rows]
                 for t in range(3):
                     out_ref[(8 * t + part) // 6 * 2 + y, :, :rows] = block[:, t * rows : (t + 1) * rows]
-                out_ref[part // 2 * 2 + y, :, rows : 2 * rows] = block[:, 3 * rows : 4 * rows]
-
-
-def attn_join_kernel(rows, place, got_ref, qkv_ref, proj_ref):
-    for y in range(2):
-        proj_ref[:, y * rows : (y + 1) * rows] = got_ref[place[AT_F] * 2 + y, :, rows : 2 * rows].astype(F32)
+    for ref, y in ((keep_ref, place[AT_Y]), (send_ref, 1 - place[AT_Y])):
+        ref[:, :rows] = in_ref[at_rows(y, rows), 3 * rows :]
+        ref[:, rows:] = jnp.zeros((rows, ref.shape[1] - rows), BF)
+
+
+def attn_join_kernel(rows, place, got_ref, keep_ref, swap_ref, qkv_ref, proj_ref):
+    keep, swapped = keep_ref[:, :rows].astype(F32), swap_ref[:, :rows].astype(F32)
+    proj_ref[:, :rows] = jnp.where(place[AT_Y] == 0, keep, swapped)
+    proj_ref[:, rows:] = jnp.where(place[AT_Y] == 0, swapped, keep)
     for to in range(4):
 
         @pl.when(place[AT_F] == to)
@@ -1373,8 +1391,8 @@
                 shaped((samples, wide(rows)), BF),
                 shaped((samples, wide(rows))),
                 shaped((rows, wide(3 * width)), BF),
-                shaped((rows, wide(part_ff)), BF),
-                shaped((rows, wide(part_ff) + wide(3 * width)), BF),
+                shaped((rows, 512), BF),
+                shaped((rows, 512 + wide(3 * width)), BF),
                 shaped((rows, wide(d + cols)), BF),
                 shaped((2 * T + 16, d), BF),
             ],
@@ -1384,8 +1402,8 @@
         fc2_in = lax.all_gather(fc2_rows, "z", axis=0)
         mod_terms = lax.all_to_all(partial_mod, ("z", "y"), 0, 0, tiled=True)
         got = swap(send, ("y",))
-        qkv_pair = jnp.stack([qkv_mine, got[:, wide(part_ff) :]])
-        fc1_pair = jnp.stack([fc1_mine, got[:, : wide(part_ff)]])
+        qkv_pair = jnp.stack([qkv_mine, got[:, 512:]])
+        fc1_pair = jnp.stack([fc1_mine, got[:, :512]])
         mod_terms, qkv_pair, fc1_pair, slab_rows = lax.optimization_barrier((mod_terms, qkv_pair, fc1_pair, slab_rows))
         qkv_pair, fc2_in = lax.optimization_barrier((qkv_pair, fc2_in))
         qkv_in = lax.all_gather(qkv_pair, "z", axis=0)
@@ -1403,16 +1421,8 @@
         tok_near = jnp.stack(tok_mine)
         tok_far = swap(tok_near, ("core",))
         proj_slots = gather_slots(fc2_in[:, :, d : d + cols])
-        (proj_all,) = call(
-            "proj",
-            3,
-            functools.partial(proj_kernel, d),
-            proj_slots,
-            [shaped((d, d), BF)],
-            scratch=[pltpu.VMEM((8, 4, rows, cols), BF)],
-        )
-        mod_in, tok_near, tok_far, qkv_in, fc1_pair, proj_all = lax.optimization_barrier(
-            (mod_in, tok_near, tok_far, qkv_in, fc1_pair, proj_all)
+        mod_in, tok_near, tok_far, qkv_in, fc1_pair, proj_slots = lax.optimization_barrier(
+            (mod_in, tok_near, tok_far, qkv_in, fc1_pair, proj_slots)
         )
         fc1_in = lax.all_gather(fc1_pair, "z", axis=0)
         attn_t, qkv, sel, selt, w_qkv, mod = call(
@@ -1441,7 +1451,16 @@
             ],
             scratch=[pltpu.VMEM((1, 3 * width), F32)],
         )
-        attn_slots = gather_slots(attn_t)
+        (proj_all,) = call(
+            "proj",
+            3,
+            functools.partial(proj_kernel, d),
+            proj_slots,
+            [shaped((d, d), BF)],
+            scratch=[pltpu.VMEM((8, 4, rows, cols), BF)],
+        )
+        attn_mine, proj_all = lax.optimization_barrier((gather_near(attn_t), proj_all))
+        attn_slots = attn_mine + [swap(piece, ("core",)) for piece in attn_mine]
 
         def slot_spec(dc, dx):
             return pl.BlockSpec((width, TB), lambda j, *_: (0, lax.bitwise_xor(j, dc * 2 + dx)))
@@ -1451,7 +1470,7 @@
         far_out = pl.BlockSpec((2, T, d), lambda j, *_: (jnp.maximum(j - 2, 0), 0, 0))
         half_shape = shaped((4, T, d), BF)
 
-        mlp_rest = [mod, proj_all, lines(proj_bias), fc1_in, lines(fc1_bias), fc2_in, lines(fc2_bias)]
+        mlp_rest = [mod, proj_all, lines(proj_bias), fc1_in, lines(fc1_bias), fc2_in, lines(fc2_bias), w_qkv]
         (b2_own, b2_far, gm_own, gm_far, fcg, fc1_bias_g, fc2_bias_g, modg_two, after_own, branch_own) = call(
             "mlp",
             32,
@@ -1543,26 +1562,36 @@
             8,
             functools.partial(weights_kernel, d, width, order),
             [*attn_slots, *grad_attn, grad_qkv, attn_in],
-            [shaped((d, wide(4 * width)), BF)],
+            [shaped((4, 9 * width, 128), BF)],
             steps=4,
             ins=slot_specs + [whole((2, width, T))] * 8 + [rows_at(wide(3 * width)), rows_at(d)],
-            specs=[whole((d, wide(4 * width)))],
+            specs=[whole((4, 9 * width, 128))],
             scratch=[
                 pltpu.VMEM((d, 3 * width), F32),
                 pltpu.VMEM((d, width), F32),
                 pltpu.VMEM((8, width, T), BF),
+                pltpu.VMEM((d, 4 * width), BF),
             ],
         )
         terms = lax.all_to_all(to_sum, names, 0, 0, tiled=True)
-        attn_g, terms, fc_z, gin_terms = lax.optimization_barrier((attn_g, terms, fc_z, gin_terms))
         (mlp_send,) = call(
             "mlp_split", 3, functools.partial(mlp_split_kernel, rows), [fc_z], [shaped((8, rows, wide(3 * rows)), BF)]
         )
+        attn_g, terms, mlp_send, gin_terms = lax.optimization_barrier((attn_g, terms, mlp_send, gin_terms))
         mlp_got = lax.all_to_all(mlp_send, group, 0, 0, tiled=True)
-        attn_z = lax.psum_scatter(attn_g, "z", scatter_dimension=0, tiled=True)
+        attn_z = lax.psum_scatter(attn_g.reshape(36 * width, 128), "z", scatter_dimension=0, tiled=True)
 
         (sums,) = call("grad_sum", 2, grad_sum_kernel, [terms], [shaped((8, d), BF)])
-        sums, mlp_got = lax.optimization_barrier((over_z(sums), mlp_got))
+        own_specs = [whole((T, 1)), whole((T, 128)), whole(mod.shape)]
+        (input_grad,) = call(
+            "input_grad",
+            3,
+            input_grad_kernel,
+            [*gin_terms, flat_tokens, grad_one, flat_cot, mask, sel, mod],
+            [shaped((T, d))],
+            ins=[whole((T, d))] * 7 + own_specs,
+        )
+        sums, mlp_got, input_grad = lax.optimization_barrier((over_z(sums), mlp_got, input_grad))
         total = to_slab(jnp.stack(sums))
 
         (ada_weight_grad, condition_grad, ada_bias_grad, qkv_bias_grad, proj_bias_grad, fc1_bias_grad, fc2_bias_grad) = call(
@@ -1574,7 +1603,6 @@
             + [shaped((n // 128, 128)) for n in (6 * d, 2 * d, d, ff, d)],
         )
 
-        own_specs = [whole((T, 1)), whole((T, 128)), whole(mod.shape)]
         (result,) = call(
             "output",
             3,
@@ -1583,12 +1611,6 @@
             [shaped((T, d), BF)],
             ins=[whole((T, d))] * 6 + own_specs,
         )
-        attn_z, result = lax.optimization_barrier((attn_z, result))
-        (attn_send,) = call(
-            "attn_split", 3, functools.partial(attn_split_kernel, rows), [attn_z], [shaped((8, rows, wide(2 * rows)), BF)]
-        )
-        attn_got = lax.all_to_all(attn_send, group, 0, 0, tiled=True)
-        mlp_got = lax.optimization_barrier((mlp_got, attn_send))[0]
         fc1_weight_grad, fc2_weight_grad = call(
             "mlp_join",
             3,
@@ -1596,20 +1618,21 @@
             [mlp_got],
             [shaped((rows, ff // 4)), shaped((d // 4, 4 * rows))],
         )
-        gin_terms = lax.optimization_barrier((gin_terms, attn_send))[0]
-        (input_grad,) = call(
-            "input_grad",
+        attn_z, result, fc1_weight_grad = lax.optimization_barrier((attn_z, result, fc1_weight_grad))
+        attn_send, proj_keep, proj_send = call(
+            "attn_split",
             3,
-            input_grad_kernel,
-            [*gin_terms, flat_tokens, grad_one, flat_cot, mask, sel, mod],
-            [shaped((T, d))],
-            ins=[whole((T, d))] * 7 + own_specs,
-        )
+            functools.partial(attn_split_kernel, rows),
+            [attn_z],
+            [shaped((8, rows, wide(rows)), BF), shaped((rows, wide(rows)), BF), shaped((rows, wide(rows)), BF)],
+            scratch=[pltpu.VMEM((2 * rows, 4 * rows), BF)],
+        )
+        attn_got = lax.all_to_all(attn_send, group, 0, 0, tiled=True)
         qkv_weight_grad, proj_weight_grad = call(
             "attn_join",
             3,
             functools.partial(attn_join_kernel, rows),
-            [attn_got],
+            [attn_got, proj_keep, swap(proj_send, ("y",))],
             [shaped((rows, 3 * d // 4)), shaped((rows, d // 4))],
         )
 

time: 317 us -> 307 us (0.968)
  waiting for transfers between devices: 99.8 us -> 91.3 us
    all_to_all x2, waiting for transfers between devices: 0.08 us -> 4.53 us  [to_slab(): lax.all_to_all(jnp.broadcast_to(a, (8, *a.shape)), group, 0, 0, tiled=True)]
    ppermute x38 -> x39, waiting for transfers between devices: 71.3 us -> 67.5 us  [swap(): return lax.ppermute(a, axes, [(k, n - 1 - k) for k in range(n)])]
    all_gather x1, waiting for transfers between devices: 3.56 us -> 0.01 us  [local(): fc1_in = lax.all_gather(fc1_pair, 'z', axis=0)]
    ppermute x6, starting transfers between devices: 10 us -> 6.48 us  [from_z(): return lax.ppermute(a, ('z',), [(z, z ^ apart) for z in range(4)])]
    ppermute x38 -> x39, starting transfers between devices: 32.7 us -> 33.8 us  [swap(): return lax.ppermute(a, axes, [(k, n - 1 - k) for k in range(n)])]
  transfers between devices with their start and end apart: 55 -> 56, of which waited for: 31 -> 33; matrix products, arithmetic and copies ran while one was open for 3% -> 3% of each run, Pallas kernels for 25% -> 26%
where the time goes in v2:
time: 307 us; the launch traced here: 306 us
  Pallas kernels  120 us (39%)
  waiting for transfers between devices  91.3 us (30%)
  starting transfers between devices  64.3 us (21%)
  between operations  14.3 us (5%)
  local copies, waits for them, and re-layouts  11.4 us (4%)
  other arithmetic  4.41 us (1%)
    pallas_call x16, Pallas kernels, call(): pl.pallas_call(kernel, grid_spec=pltpu.PrefetchScalarGridSpec(num_scalar_...  120 us
    ppermute x39, waiting for transfers between devices, swap(): return lax.ppermute(a, axes, [(k, n - 1 - k) for k in range(n)])  67.5 us
    ppermute x39, starting transfers between devices, swap(): return lax.ppermute(a, axes, [(k, n - 1 - k) for k in range(n)])  33.8 us
    ppermute x6, waiting for transfers between devices, from_z(): return lax.ppermute(a, ('z',), [(z, z ^ apart) for z in range(4)])  9.53 us
    all_to_all x2, starting transfers between devices, to_slab(): lax.all_to_all(jnp.broadcast_to(a, (8, *a.shape)), group, 0, 0, tiled=True)  7.09 us
    ppermute x6, starting transfers between devices, from_z(): return lax.ppermute(a, ('z',), [(z, z ^ apart) for z in range(4)])  6.48 us
  transfers between devices with their start and end apart: 56, of which 33 were waited for; matrix products, arithmetic and copies ran while one was open for 3% of the time, Pallas kernels for 26%

profile of v2, /device:TPU:0, one launch (start us, length us, event | category | flops | bytes accessed | tf_op | source)
XLA Modules:
  0.0 305.8 jit_solution(12306876460265466971)
XLA Ops:
  8.4 5.8 %prepare.1 = (bf16[8,8,1152]{2,1,0:T(8,128)(2,1)}, bf16[32,256]{1,0:T(8,128)(2,1)}, f32[32,256]{1,0:T(8,128)}, bf16[144,512]{1,0:T(8,128)(2,1)}, bf16[144,512]{1...) custom-call(s32[40]{0:T(128)} %dynamic-slice_bitcast_fusion.place, ...), custom_call_target="tpu_custom_call" | custom-call | flops 1000 | bytes 1000 | tf_op jit(solution)/shard_map/prepare/pallas_call | solution.py:1362
  17.3 4.9 %all-to-all-start = ((bf16[8,8,1152]{2,1,0:T(8,128)(2,1)}), bf16[8,8,1152]{2,1,0:T(8,128)(2,1)S(1)}, u32[]{:S(2)}, u32[]{:S(2)}) async-start(bf16[8,8,1152]{2,1,0:T(8,128)(2,1)} %get-tuple-element.136), calls=%async_computation | async-start | bytes 294912 | tf_op jit(solution)/shard_map/all_to_all | solution.py:1403
  25.7 4.0 %all-to-all-done.terms_ref = bf16[8,8,1152]{2,1,0:T(8,128)(2,1)S(1)} async-done(((bf16[8,8,1152]{2,1,0:T(8,128)(2,1)}), bf16[8,8,1152]{2,1,0:T(8,128)(2,1)S(1)}, u32[]{:S(2)}, u32[]{:S(2)}) %all-to-all-start) | async-done | bytes 147488 | tf_op jit(solution)/shard_map/all_to_all | solution.py:1403
  41.5 4.8 %collective-permute-done.3 = bf16[8,1152]{1,0:T(8,128)(2,1)S(1)} collective-permute-done((bf16[8,1152]{1,0:T(8,128)(2,1)}, bf16[8,1152]{1,0:T(8,128)(2,1)S(1)}, u32[]{:S(2)}, u32[]{:S(2)}) %collective-permute-start.3) | collective-permute-done | bytes 18464 | tf_op jit(solution)/shard_map/ppermute | solution.py:1299
  47.1 11.6 %collective-permute-done.6 = bf16[272,1152]{1,0:T(8,128)(2,1)S(1)} collective-permute-done((bf16[272,1152]{1,0:T(8,128)(2,1)S(1)}, bf16[272,1152]{1,0:T(8,128)(2,1)S(1)}, u32[]{:S(2)}, u32[]{:S(2)}) %collective-permute-start.6) | collective-permute-done | bytes 626720 | tf_op jit(solution)/shard_map/ppermute | solution.py:1296
  69.9 6.3 %collective-permute-done.8.refs_1_ = bf16[4,144,288]{2,1,0:T(8,128)(2,1)} collective-permute-done((bf16[4,144,288]{2,1,0:T(8,128)(2,1)}, bf16[4,144,288]{2,1,0:T(8,128)(2,1)}, u32[]{:S(2)}, u32[]{:S(2)}) %collective-permute-start.8) | collective-permute-done | bytes 331808 | tf_op jit(solution)/shard_map/ppermute | solution.py:1296
  76.7 9.3 %collective-permute-done.10.refs_3_ = bf16[4,144,288]{2,1,0:T(8,128)(2,1)} collective-permute-done((bf16[4,144,288]{2,1,0:T(8,128)(2,1)}, bf16[4,144,288]{2,1,0:T(8,128)(2,1)}, u32[]{:S(2)}, u32[]{:S(2)}) %collective-permute-start.10) | collective-permute-done | bytes 331808 | tf_op jit(solution)/shard_map/ppermute | solution.py:1296
  86.0 4.5 %all-to-all-done.1.modin_ref = bf16[8,4,8,1152]{3,2,1,0:T(8,128)(2,1)S(1)} async-done(((bf16[8,4,8,1152]{3,2,1,0:T(8,128)(2,1)}), bf16[8,4,8,1152]{3,2,1,0:T(8,128)(2,1)S(1)}, u32[]{:S(2)}, u32[]{:S(2)}) %all-to-all-start.1) | async-done | bytes 589856 | tf_op jit(solution)/shard_map/all_to_all | solution.py:1316
  91.3 12.8 %attend.1 = (bf16[144,1024]{1,0:T(8,128)(2,1)}, bf16[1024,512]{1,0:T(8,128)(2,1)}, bf16[1024,128]{1,0:T(8,128)(2,1)}, bf16[32,1024]{1,0:T(8,128)(2,1)}, bf16[115...) custom-call(s32[40]{0:T(128)} %dynamic-slice_bitcast_fusion.place, bf16[4,272,1152]{2,1,0:T(8,128)(2,1)} %copy-done, ...), custom_call_target="tpu_custom_call" | custom-call | flops 1000 | bytes 1000 | tf_op jit(solution)/shard_map/attend/pallas_call | solution.py:1362
  107.8 5.4 %proj.1.refs_13_.refs_10_ = bf16[1152,1152]{1,0:T(8,128)(2,1)} custom-call(s32[40]{0:T(128)} %dynamic-slice_bitcast_fusion.place, bf16[4,144,288]{2,1,0:T(8,128)(2,1)} %slice.83.refs_0_, bf16[4,144,288]{2,1,0:T(8,128)(2,1)} %collective-permute-done.8.refs_1_, bf16[4,144,288]{2,1,0:T(8,128)(2,1)} %collective-permute-done.9.refs_2_, ...), custom_call_target="tpu_custom_call" | custom-call | flops 1000 | bytes 1000 | tf_op jit(solution)/shard_map/proj/pallas_call | solution.py:1362
  115.5 5.2 %collective-permute-done.17.refs_3_ = bf16[144,1024]{1,0:T(8,128)(2,1)S(1)} collective-permute-done((bf16[144,1024]{1,0:T(8,128)(2,1)}, bf16[144,1024]{1,0:T(8,128)(2,1)S(1)}, u32[]{:S(2)}, u32[]{:S(2)}) %collective-permute-start.17) | collective-permute-done | bytes 294944 | tf_op jit(solution)/shard_map/ppermute | solution.py:1296
  124.2 31.9 %mlp.1 = (bf16[4,128,1152]{2,1,0:T(8,128)(2,1)}, bf16[4,128,1152]{2,1,0:T(8,128)(2,1)}, bf16[4,128,1152]{2,1,0:T(8,128)(2,1)}, bf16[4,128,1152]{2,1,0:T(8,128)(2...) custom-call(s32[40]{0:T(128)} %dynamic-slice_bitcast_fusion.place, ...), custom_call_target="tpu_custom_call" | custom-call | flops 1000 | bytes 1000 | tf_op jit(solution)/shard_map/mlp/pallas_call | solution.py:1362
  163.8 5.6 %collective-permute-done.23.refs_1_ = bf16[128,1152]{1,0:T(8,128)(2,1)S(1)} collective-permute-done((bf16[128,1152]{1,0:T(8,128)(2,1)S(1)}, bf16[128,1152]{1,0:T(8,128)(2,1)S(1)}, u32[]{:S(2)}, u32[]{:S(2)}) %collective-permute-start.23) | collective-permute-done | bytes 294944 | tf_op jit(solution)/shard_map/ppermute | solution.py:1296
  170.7 6.1 %collective-permute-done.25.refs_3_ = bf16[128,1152]{1,0:T(8,128)(2,1)S(1)} collective-permute-done((bf16[128,1152]{1,0:T(8,128)(2,1)S(1)}, bf16[128,1152]{1,0:T(8,128)(2,1)S(1)}, u32[]{:S(2)}, u32[]{:S(2)}) %collective-permute-start.25) | collective-permute-done | bytes 294944 | tf_op jit(solution)/shard_map/ppermute | solution.py:1296
  177.5 6.1 %middle.1 = (bf16[2,144,128]{2,1,0:T(8,128)(2,1)}, bf16[2,144,128]{2,1,0:T(8,128)(2,1)}, bf16[2,144,128]{2,1,0:T(8,128)(2,1)}, bf16[2,144,128]{2,1,0:T(8,128)(2,...) custom-call(s32[40]{0:T(128)} %dynamic-slice_bitcast_fusion.place, ...), custom_call_target="tpu_custom_call" | custom-call | flops 1000 | bytes 1000 | tf_op jit(solution)/shard_map/middle/pallas_call | solution.py:1362
  198.1 19.1 %back.1 = (bf16[4,128,1152]{2,1,0:T(8,128)(2,1)}, bf16[4,128,1152]{2,1,0:T(8,128)(2,1)}, bf16[1024,512]{1,0:T(8,128)(2,1)}, bf16[1024,1152]{1,0:T(8,128)(2,1)}, bf16[32,8,1152]{2,1,0:T(8,128)(2,1)}) custom-call(s32[40]{0:T(128)} %dynamic-slice_bitcast_fusion.place, bf16[2,144,128]{2,1,0:T(8,128)(2,1)} %get-tuple-element.193.refs_0_.refs_8_, ...), custom_call_target="tpu_custom_call" | custom-call | flops 1000 | bytes 1000 | tf_op jit(solution)/shard_map/back/pallas_call | solution.py:1362
  218.3 3.8 %all-to-all-start.2 = ((bf16[32,8,1152]{2,1,0:T(8,128)(2,1)}), bf16[32,8,1152]{2,1,0:T(8,128)(2,1)S(1)}, u32[]{:S(2)}, u32[]{:S(2)}) async-start(bf16[32,8,1152]{2,1,0:T(8,128)(2,1)} %get-tuple-element.218), calls=%async_computation.2 | async-start | bytes 1179648 | tf_op jit(solution)/shard_map/all_to_all | solution.py:1576
  226.7 8.0 %weights.1 = bf16[4,1296,128]{2,1,0:T(8,128)(2,1)} custom-call(s32[40]{0:T(128)} %dynamic-slice_bitcast_fusion.place, bf16[144,1024]{1,0:T(8,128)(2,1)} %get-tuple-element.169.refs_0_, bf16[144,1024]{1,0:T(8,128)(2,1)} %copy-done.11, bf16[144,1024]{1,0:T(8,128)(2,1)} %copy-done.12, bf16[144,1024]{1,0:T(8,128)(2,1)} %copy-done.13, ...), custom_call_target="tpu_custom_call" | custom-call | flops 1000 | bytes 1000 | tf_op jit(solution)/shard_map/weights/pallas_call | solution.py:1362
  240.0 4.9 %collective-permute-done.40.gin_3 = bf16[128,1152]{1,0:T(8,128)(2,1)S(1)} collective-permute-done((bf16[128,1152]{1,0:T(8,128)(2,1)S(1)}, bf16[128,1152]{1,0:T(8,128)(2,1)S(1)}, u32[]{:S(2)}, u32[]{:S(2)}) %collective-permute-start.40) | collective-permute-done | bytes 294944 | tf_op jit(solution)/shard_map/ppermute | solution.py:1296
  245.7 3.6 %all-to-all-start.3 = ((bf16[8,144,512]{2,1,0:T(8,128)(2,1)}), bf16[8,144,512]{2,1,0:T(8,128)(2,1)S(1)}, u32[]{:S(2)}, u32[]{:S(2)}) async-start(bf16[8,144,512]{2,1,0:T(8,128)(2,1)} %mlp_split.1), calls=%async_computation.5 | async-start | bytes 2359296 | tf_op jit(solution)/shard_map/all_to_all | solution.py:1581
  256.9 4.0 %input_grad.1 = f32[128,1152]{1,0:T(8,128)} custom-call(s32[40]{0:T(128)} %dynamic-slice_bitcast_fusion.place, bf16[128,1152]{1,0:T(8,128)(2,1)} %get-tuple-element.229.gin_0, bf16[128,1152]{1,0:T(8,128)(2,1)} %copy-done.25, bf16[128,1152]{1,0:T(8,128)(2,1)} %copy-done.26, bf16[128,1152]{1,0:T(8,128)(2,1)} %copy-done.27, bf16[128,1152]{1,0:T(8,128)(2,1)} %bitcast.69, ...), custom_call_target="tpu_custom_call" | custom-call | flops 1000 | bytes 1000 | tf_op jit(solution)/shard_map/input_grad/pallas_call | solution.py:1362
  273.1 3.9 %mlp_join.1 = (f32[144,1152]{1,0:T(8,128)}, f32[288,576]{1,0:T(8,128)}) custom-call(s32[40]{0:T(128)} %dynamic-slice_bitcast_fusion.place, bf16[8,144,512]{2,1,0:T(8,128)(2,1)} %copy-done.1), custom_call_target="tpu_custom_call" | custom-call | flops 1000 | bytes 1000 | tf_op jit(solution)/shard_map/mlp_join/pallas_call | solution.py:1362
  280.1 4.3 %all-to-all-start.5 = ((bf16[8,144,256]{2,1,0:T(8,128)(2,1)}), bf16[8,144,256]{2,1,0:T(8,128)(2,1)S(1)}, u32[]{:S(2)}, u32[]{:S(2)}) async-start(bf16[8,144,256]{2,1,0:T(8,128)(2,1)} %get-tuple-element.248), calls=%async_computation.7 | async-start | bytes 1179648 | tf_op jit(solution)/shard_map/all_to_all | solution.py:1630
  286.5 5.7 %ada.1 = (f32[144,6912]{1,0:T(8,128)}, f32[32,144]{1,0:T(8,128)}, f32[54,128]{1,0:T(8,128)}, f32[18,128]{1,0:T(8,128)}, f32[9,128]{1,0:T(8,128)}, /*index=5*/f32[36,128]{1,0:T(8,128)}, f32[9,128]{1,0:T(8,128)}) custom-call(s32[40]{0:T(128)} %dynamic-slice_bitcast_fusion.place, bf16[8,4,8,1152]{3,2,1,0:T(8,128)(2,1)} %copy-done.6, ...), custom_call_target="tpu_custom_call" | custom-call | flops 1000 | bytes 1000 | tf_op jit(solution)/shard_map/ada/pallas_call | solution.py:1362
  (209 shorter events, 110.0 us)
Async XLA Ops:
  7.2 52.2 %all-gather.7.cloned.1.call-start = ((), (), s32[]{:S(2)}) async-start(), calls=%async_computation.10 | async-start | bytes 2211840 | tf_op jit(solution)/shard_map/all_gather | solution.py:1402
  22.2 68.4 %all-gather.9.cloned.1.call-start = ((), (), s32[]{:S(2)}) async-start(), calls=%async_computation.11 | async-start | bytes 1474560 | tf_op jit(solution)/shard_map/all_gather | solution.py:1409
  29.7 16.6 %collective-permute-start.4 = (bf16[272,1152]{1,0:T(8,128)(2,1)S(1)}, bf16[272,1152]{1,0:T(8,128)(2,1)S(1)}, u32[]{:S(2)}, u32[]{:S(2)}) collective-permute-start(bf16[272,1152]{1,0:T(8,128)(2,1)S(1)} %copy-done.2), channel_id=1, source_target_pairs={{0,1},{1,0},{2,3},{3,2},{4,5},{5,4},{6,7},{7,6},{8,9},{9,8},{10,11... | collective-permute-start | bytes 1880072 | tf_op jit(solution)/shard_map/ppermute | solution.py:1296
  30.0 17.1 %collective-permute-start.5 = (bf16[272,1152]{1,0:T(8,128)(2,1)S(1)}, bf16[272,1152]{1,0:T(8,128)(2,1)S(1)}, u32[]{:S(2)}, u32[]{:S(2)}) collective-permute-start(bf16[272,1152]{1,0:T(8,128)(2,1)S(1)} %copy-done.2), channel_id=1, source_target_pairs={{0,16},{16,0},{1,17},{17,1},{2,18},{18,2},{3,19},{19,3},{4,20},{20... | collective-permute-start | bytes 1880072 | tf_op jit(solution)/shard_map/ppermute | solution.py:1296
  31.6 27.1 %collective-permute-start.6 = (bf16[272,1152]{1,0:T(8,128)(2,1)S(1)}, bf16[272,1152]{1,0:T(8,128)(2,1)S(1)}, u32[]{:S(2)}, u32[]{:S(2)}) collective-permute-start(bf16[272,1152]{1,0:T(8,128)(2,1)S(1)} %copy-done.2), channel_id=1, source_target_pairs={{0,17},{1,16},{16,1},{17,0},{2,19},{3,18},{18,3},{19,2},{4,21},{5,... | collective-permute-start | bytes 1880072 | tf_op jit(solution)/shard_map/ppermute | solution.py:1296
  59.1 31.5 %collective-permute-start.7 = (bf16[4,272,1152]{2,1,0:T(8,128)(2,1)S(1)}, bf16[4,272,1152]{2,1,0:T(8,128)(2,1)}, u32[]{:S(2)}, u32[]{:S(2)}) collective-permute-start(bf16[4,272,1152]{2,1,0:T(8,128)(2,1)S(1)} %pad_maximum_fusion.tok_near.refs_8_), channel_id=1, source_target_pairs={{0,8},{8,0},{1,9},{9,1},{2,10},{10,2},{3,11},{11,3},{4,12},{12,4},... | collective-permute-start | bytes 7520264 | tf_op jit(solution)/shard_map/ppermute | solution.py:1296
  61.6 14.6 %collective-permute-start.8 = (bf16[4,144,288]{2,1,0:T(8,128)(2,1)}, bf16[4,144,288]{2,1,0:T(8,128)(2,1)}, u32[]{:S(2)}, u32[]{:S(2)}) collective-permute-start(bf16[4,144,288]{2,1,0:T(8,128)(2,1)} %slice.83.refs_0_), channel_id=1, source_target_pairs={{0,1},{1,0},{2,3},{3,2},{4,5},{5,4},{6,7},{7,6},{8,9},{9,8},{10,11... | collective-permute-start | bytes 995336 | tf_op jit(solution)/shard_map/ppermute | solution.py:1296
  64.3 21.7 %collective-permute-start.10 = (bf16[4,144,288]{2,1,0:T(8,128)(2,1)}, bf16[4,144,288]{2,1,0:T(8,128)(2,1)}, u32[]{:S(2)}, u32[]{:S(2)}) collective-permute-start(bf16[4,144,288]{2,1,0:T(8,128)(2,1)} %slice.83.refs_0_), channel_id=1, source_target_pairs={{0,17},{1,16},{16,1},{17,0},{2,19},{3,18},{18,3},{19,2},{4,21},{5,... | collective-permute-start | bytes 995336 | tf_op jit(solution)/shard_map/ppermute | solution.py:1296
  66.0 24.5 %all-to-all-start.1 = ((bf16[8,4,8,1152]{3,2,1,0:T(8,128)(2,1)}), bf16[8,4,8,1152]{3,2,1,0:T(8,128)(2,1)S(1)}, u32[]{:S(2)}, u32[]{:S(2)}) async-start(bf16[8,4,8,1152]{3,2,1,0:T(8,128)(2,1)} %broadcast_in_dim.6), calls=%async_computation.1 | async-start | bytes 1179648 | tf_op jit(solution)/shard_map/all_to_all | solution.py:1316
  69.5 54.0 %all-gather.11.cloned.1.call-start = ((), (), s32[]{:S(2)}) async-start(), calls=%async_computation.12 | async-start | bytes 1474560 | tf_op jit(solution)/shard_map/all_gather | solution.py:1427
  69.6 20.9 %collective-permute-start.11 = (bf16[4,144,288]{2,1,0:T(8,128)(2,1)}, bf16[4,144,288]{2,1,0:T(8,128)(2,1)}, u32[]{:S(2)}, u32[]{:S(2)}) collective-permute-start(bf16[4,144,288]{2,1,0:T(8,128)(2,1)} %slice.83.refs_0_), channel_id=1, source_target_pairs={{0,8},{8,0},{1,9},{9,1},{2,10},{10,2},{3,11},{11,3},{4,12},{12,4},... | collective-permute-start | bytes 995336 | tf_op jit(solution)/shard_map/ppermute | solution.py:1296
  90.7 144.1 %reduce-scatter.3.cloned.1.call-start = ((), (), s32[]{:S(2)}) async-start(), calls=%async_computation.8 | async-start | bytes 3686400 | tf_op jit(solution)/shard_map/reduce_scatter | solution.py:1519
  157.4 29.8 %collective-permute-start.33 = (bf16[4,128,1152]{2,1,0:T(8,128)(2,1)S(1)}, bf16[4,128,1152]{2,1,0:T(8,128)(2,1)S(1)}, u32[]{:S(2)}, u32[]{:S(2)}) collective-permute-start(bf16[4,128,1152]{2,1,0:T(8,128)(2,1)S(1)} %copy-done.41), channel_id=1, source_target_pairs={{0,8},{8,0},{1,9},{9,1},{2,10},{10,2},{3,11},{11,3},{4,12},{12,4},... | collective-permute-start | bytes 3538952 | tf_op jit(solution)/shard_map/ppermute | solution.py:1296
  162.3 14.5 %collective-permute-start.25 = (bf16[128,1152]{1,0:T(8,128)(2,1)S(1)}, bf16[128,1152]{1,0:T(8,128)(2,1)S(1)}, u32[]{:S(2)}, u32[]{:S(2)}) collective-permute-start(bf16[128,1152]{1,0:T(8,128)(2,1)S(1)} %get-tuple-element.267), channel_id=1, source_target_pairs={{0,17},{1,16},{16,1},{17,0},{2,19},{3,18},{18,3},{19,2},{4,21},{5,... | collective-permute-start | bytes 884744 | tf_op jit(solution)/shard_map/ppermute | solution.py:1296
  194.3 22.8 %collective-permute-start.34 = (bf16[128,1152]{1,0:T(8,128)(2,1)S(1)}, bf16[128,1152]{1,0:T(8,128)(2,1)S(1)}, u32[]{:S(2)}, u32[]{:S(2)}) collective-permute-start(bf16[128,1152]{1,0:T(8,128)(2,1)S(1)} %get-tuple-element.213), channel_id=1, source_target_pairs={{0,1},{1,0},{2,3},{3,2},{4,5},{5,4},{6,7},{7,6},{8,9},{9,8},{10,11... | collective-permute-start | bytes 884744 | tf_op jit(solution)/shard_map/ppermute | solution.py:1296
  196.6 20.6 %collective-permute-start.35 = (bf16[128,1152]{1,0:T(8,128)(2,1)S(1)}, bf16[128,1152]{1,0:T(8,128)(2,1)S(1)}, u32[]{:S(2)}, u32[]{:S(2)}) collective-permute-start(bf16[128,1152]{1,0:T(8,128)(2,1)S(1)} %get-tuple-element.214), channel_id=1, source_target_pairs={{0,16},{16,0},{1,17},{17,1},{2,18},{18,2},{3,19},{19,3},{4,20},{20... | collective-permute-start | bytes 884744 | tf_op jit(solution)/shard_map/ppermute | solution.py:1296
  197.6 19.7 %collective-permute-start.36 = (bf16[128,1152]{1,0:T(8,128)(2,1)S(1)}, bf16[128,1152]{1,0:T(8,128)(2,1)S(1)}, u32[]{:S(2)}, u32[]{:S(2)}) collective-permute-start(bf16[128,1152]{1,0:T(8,128)(2,1)S(1)} %get-tuple-element.215), channel_id=1, source_target_pairs={{0,17},{1,16},{16,1},{17,0},{2,19},{3,18},{18,3},{19,2},{4,21},{5,... | collective-permute-start | bytes 884744 | tf_op jit(solution)/shard_map/ppermute | solution.py:1296
  218.3 21.7 %all-to-all-start.2 = ((bf16[32,8,1152]{2,1,0:T(8,128)(2,1)}), bf16[32,8,1152]{2,1,0:T(8,128)(2,1)S(1)}, u32[]{:S(2)}, u32[]{:S(2)}) async-start(bf16[32,8,1152]{2,1,0:T(8,128)(2,1)} %get-tuple-element.218), calls=%async_computation.2 | async-start | bytes 1179648 | tf_op jit(solution)/shard_map/all_to_all | solution.py:1576
  222.1 54.9 %reduce-scatter.5.cloned.1.call-start = ((), (), s32[]{:S(2)}) async-start(), calls=%async_computation.9 | async-start | bytes 1658880 | tf_op jit(solution)/shard_map/reduce_scatter | solution.py:1582
  223.2 16.8 %collective-permute-start.38 = (bf16[128,1152]{1,0:T(8,128)(2,1)}, bf16[128,1152]{1,0:T(8,128)(2,1)S(1)}, u32[]{:S(2)}, u32[]{:S(2)}) collective-permute-start(bf16[128,1152]{1,0:T(8,128)(2,1)} %get-tuple-element.261), channel_id=1, source_target_pairs={{0,1},{1,0},{2,3},{3,2},{4,5},{5,4},{6,7},{7,6},{8,9},{9,8},{10,11... | collective-permute-start | bytes 884744 | tf_op jit(solution)/shard_map/ppermute | solution.py:1296
  225.0 15.0 %collective-permute-start.39 = (bf16[128,1152]{1,0:T(8,128)(2,1)S(1)}, bf16[128,1152]{1,0:T(8,128)(2,1)S(1)}, u32[]{:S(2)}, u32[]{:S(2)}) collective-permute-start(bf16[128,1152]{1,0:T(8,128)(2,1)S(1)} %get-tuple-element.260), channel_id=1, source_target_pairs={{0,16},{16,0},{1,17},{17,1},{2,18},{18,2},{3,19},{19,3},{4,20},{20... | collective-permute-start | bytes 884744 | tf_op jit(solution)/shard_map/ppermute | solution.py:1296
  226.5 18.5 %collective-permute-start.40 = (bf16[128,1152]{1,0:T(8,128)(2,1)S(1)}, bf16[128,1152]{1,0:T(8,128)(2,1)S(1)}, u32[]{:S(2)}, u32[]{:S(2)}) collective-permute-start(bf16[128,1152]{1,0:T(8,128)(2,1)S(1)} %get-tuple-element.259), channel_id=1, source_target_pairs={{0,17},{1,16},{16,1},{17,0},{2,19},{3,18},{18,3},{19,2},{4,21},{5,... | collective-permute-start | bytes 884744 | tf_op jit(solution)/shard_map/ppermute | solution.py:1296
  245.7 19.4 %all-to-all-start.3 = ((bf16[8,144,512]{2,1,0:T(8,128)(2,1)}), bf16[8,144,512]{2,1,0:T(8,128)(2,1)S(1)}, u32[]{:S(2)}, u32[]{:S(2)}) async-start(bf16[8,144,512]{2,1,0:T(8,128)(2,1)} %mlp_split.1), calls=%async_computation.5 | async-start | bytes 2359296 | tf_op jit(solution)/shard_map/all_to_all | solution.py:1581
  280.1 15.4 %all-to-all-start.5 = ((bf16[8,144,256]{2,1,0:T(8,128)(2,1)}), bf16[8,144,256]{2,1,0:T(8,128)(2,1)S(1)}, u32[]{:S(2)}, u32[]{:S(2)}) async-start(bf16[8,144,256]{2,1,0:T(8,128)(2,1)} %get-tuple-element.248), calls=%async_computation.7 | async-start | bytes 1179648 | tf_op jit(solution)/shard_map/all_to_all | solution.py:1630
  (75 other events, 458.0 us)
Sparse Core Ops, SparseCore 0:
  14.4 44.9 all-gather.6
  61.6 29.0 all-gather.8
  92.8 29.1 all-gather.10
  156.3 56.0 reduce-scatter.2
  245.1 31.7 reduce-scatter.4

commit v3 on v2

--- a/solution.py
+++ b/solution.py
@@ -796,9 +796,12 @@
     return pl.ds(pl.multiple_of(index * rows, rows), rows)
 
 
-def prepare_kernel(d, place, cond_ref, ada_ref, qkv_ref, fc1_ref, proj_ref, fc2_ref, tok_ref, cot_ref, num_ref, mask_ref,
+def prepare_kernel(d, cond_ref, ada_ref, qkv_ref, fc1_ref, proj_ref, fc2_ref, tok_ref, cot_ref, num_ref, mask_ref,
                    part_ref, act_ref, slope_ref, qkv_mine, fc1_mine, send_out, fc2_out, tok_out, act_all):
     rows = ada_ref.shape[0]
+    frame = lax.axis_index("x") * 2 + lax.axis_index("core")
+    at_y = lax.axis_index("y")
+    patch = lax.axis_index("z") * 2 + at_y
     cols = 2 * rows
     for ref in (qkv_mine, send_out, fc2_out):
         ref[...] = jnp.zeros_like(ref)
@@ -806,13 +809,13 @@
     slope_ref[...] = jnp.zeros_like(slope_ref)
     for f in range(4):
 
-        @pl.when(place[AT_F] == f)
+        @pl.when(frame == f)
         def _():
             fc2_out[:, d : d + cols] = proj_ref[:, f * cols : (f + 1) * cols]
             for y in range(2):
                 for q_out, at_q, f_out, want in ((qkv_mine, 0, fc1_mine, y), (send_out, 512, send_out, 1 - y)):
 
-                    @pl.when(place[AT_Y] == want)
+                    @pl.when(at_y == want)
                     def _():
                         for t in range(3):
                             at = t * d + (2 * f + y) * rows
@@ -825,16 +828,16 @@
                                 to = at_q + 3 * rows
                                 q_out[:, to : to + rows - kept] = fc1_ref[:, at + kept : at + rows]
 
-    fc2_out[:, :d] = fc2_ref[at_rows(place[AT_F], rows)]
+    fc2_out[:, :d] = fc2_ref[at_rows(frame, rows)]
     row = lax.broadcasted_iota(jnp.int32, (d, rows), 0)
     col = lax.broadcasted_iota(jnp.int32, (d, rows), 1)
-    cond = mm(cond_ref[...], (row == col + place[AT_P] * rows).astype(BF))
+    cond = mm(cond_ref[...], (row == col + patch * rows).astype(BF))
     sigmoid = 1.0 / (1.0 + jnp.exp(-cond))
     act = cond * sigmoid
     act_ref[:, :rows] = act.astype(BF)
     slope_ref[:, :rows] = sigmoid * (1.0 + cond * (1.0 - sigmoid))
     act_all[...] = act
-    mine = act_all[at_rows(place[AT_F], 8)].astype(BF)
+    mine = act_all[at_rows(frame, 8)].astype(BF)
     for block in range(8):
         if block < 6:
             part_ref[block] = mm(mine, ada_ref[:, block * d : (block + 1) * d]).astype(BF)
@@ -1381,12 +1384,9 @@
         flat_cot = cotangent.reshape(T, d)
         mask = image_mask.reshape(T, 1)
 
-        (partial_mod, act_rows, silu_slope, qkv_mine, fc1_mine, send, fc2_rows, slab_rows) = call(
-            "prepare",
-            6,
+        (partial_mod, act_rows, silu_slope, qkv_mine, fc1_mine, send, fc2_rows, slab_rows) = pl.pallas_call(
             functools.partial(prepare_kernel, d),
-            [condition, ada_weight, qkv_weight, fc1_weight, proj_weight, fc2_weight, flat_tokens, flat_cot, sample_index.T, image_mask.T],
-            [
+            out_shape=[
                 shaped((8, 8, d), BF),
                 shaped((samples, wide(rows)), BF),
                 shaped((samples, wide(rows))),
@@ -1396,15 +1396,19 @@
                 shaped((rows, wide(d + cols)), BF),
                 shaped((2 * T + 16, d), BF),
             ],
-            scratch=[pltpu.VMEM((samples, rows), F32)],
-        )
+            scratch_shapes=[pltpu.VMEM((samples, rows), F32)],
+            compiler_params=pltpu.CompilerParams(vmem_limit_bytes=VMEM_BYTES),
+            cost_estimate=takes(6),
+            name="prepare",
+        )(*[condition, ada_weight, qkv_weight, fc1_weight, proj_weight, fc2_weight, flat_tokens, flat_cot, sample_index.T, image_mask.T])
 
         fc2_in = lax.all_gather(fc2_rows, "z", axis=0)
         mod_terms = lax.all_to_all(partial_mod, ("z", "y"), 0, 0, tiled=True)
         got = swap(send, ("y",))
         qkv_pair = jnp.stack([qkv_mine, got[:, 512:]])
         fc1_pair = jnp.stack([fc1_mine, got[:, :512]])
-        mod_terms, qkv_pair, fc1_pair, slab_rows = lax.optimization_barrier((mod_terms, qkv_pair, fc1_pair, slab_rows))
+        qkv_pair, fc1_pair, slab_rows = lax.optimization_barrier((qkv_pair, fc1_pair, slab_rows))
+        mod_terms, qkv_pair, fc1_pair = lax.optimization_barrier((mod_terms, qkv_pair, fc1_pair))
         qkv_pair, fc2_in = lax.optimization_barrier((qkv_pair, fc2_in))
         qkv_in = lax.all_gather(qkv_pair, "z", axis=0)
         (mod_chunk,) = call(

time: 307 us -> 320 us (1.042)
  starting transfers between devices: 64.3 us -> 73.1 us
    all_to_all x1, waiting for transfers between devices: 3.95 us -> 19.6 us  [local(): mod_terms = lax.all_to_all(partial_mod, ('z', 'y'), 0, 0, tiled=True)]
    ppermute x39, waiting for transfers between devices: 67.5 us -> 58.7 us  [swap(): return lax.ppermute(a, axes, [(k, n - 1 - k) for k in range(n)])]
    ppermute x6, waiting for transfers between devices: 9.53 us -> 3.12 us  [from_z(): return lax.ppermute(a, ('z',), [(z, z ^ apart) for z in range(4)])]
    pallas_call x16 -> x15, Pallas kernels: 120 us -> 114 us  [call(): pl.pallas_call(kernel, grid_spec=pltpu.PrefetchScalarGridSpec(num_scalar_...]
    ppermute x6, starting transfers between devices: 6.48 us -> 11.9 us  [from_z(): return lax.ppermute(a, ('z',), [(z, z ^ apart) for z in range(4)])]
    pallas_call x0 -> x1, Pallas kernels: none -> 5.16 us  [local(): pl.pallas_call(functools.partial(prepare_kernel, d), out_shape=[shaped((8...]
    unnamed x87 -> x89, local copies, waits for them, and re-layouts: 5.48 us -> 7.31 us
  transfers between devices with their start and end apart: 56 -> 56, of which waited for: 33 -> 27; matrix products, arithmetic and copies ran while one was open for 3% -> 4% of each run, Pallas kernels for 26% -> 25%
where the time goes in v3:
time: 320 us; the launch traced here: 319 us
  Pallas kernels  119 us (37%)
  waiting for transfers between devices  92.1 us (29%)
  starting transfers between devices  73.1 us (23%)
  between operations  14.3 us (4%)
  local copies, waits for them, and re-layouts  13.3 us (4%)
  other arithmetic  6.85 us (2%)
    pallas_call x15, Pallas kernels, call(): pl.pallas_call(kernel, grid_spec=pltpu.PrefetchScalarGridSpec(num_scalar_...  114 us
    ppermute x39, waiting for transfers between devices, swap(): return lax.ppermute(a, axes, [(k, n - 1 - k) for k in range(n)])  58.7 us
    ppermute x39, starting transfers between devices, swap(): return lax.ppermute(a, axes, [(k, n - 1 - k) for k in range(n)])  35 us
    all_to_all x1, waiting for transfers between devices, local(): mod_terms = lax.all_to_all(partial_mod, ('z', 'y'), 0, 0, tiled=True)  19.6 us
    ppermute x6, starting transfers between devices, from_z(): return lax.ppermute(a, ('z',), [(z, z ^ apart) for z in range(4)])  11.9 us
    unnamed x89, local copies, waits for them, and re-layouts  7.31 us
    all_to_all x2, starting transfers between devices, to_slab(): lax.all_to_all(jnp.broadcast_to(a, (8, *a.shape)), group, 0, 0, tiled=True)  7.14 us
  transfers between devices with their start and end apart: 56, of which 27 were waited for; matrix products, arithmetic and copies ran while one was open for 4% of the time, Pallas kernels for 25%

profile of v3, /device:TPU:0, one launch (start us, length us, event | category | flops | bytes accessed | tf_op | source)
XLA Modules:
  0.0 319.0 jit_solution(8313415949318031067)
XLA Ops:
  7.2 5.2 %prepare.1 = (bf16[8,8,1152]{2,1,0:T(8,128)(2,1)}, bf16[32,256]{1,0:T(8,128)(2,1)}, f32[32,256]{1,0:T(8,128)}, bf16[144,512]{1,0:T(8,128)(2,1)}, bf16[144,512]{1...) custom-call(bf16[32,1152]{1,0:T(8,128)(2,1)} %cond_ref.1, ...), custom_call_target="tpu_custom_call" | custom-call | flops 1000 | bytes 1000 | tf_op jit(solution)/shard_map/prepare/pallas_call | solution.py:1387
  15.4 7.3 %collective-permute-done = bf16[144,1024]{1,0:T(8,128)(2,1)S(1)} collective-permute-done((bf16[144,1024]{1,0:T(8,128)(2,1)}, bf16[144,1024]{1,0:T(8,128)(2,1)S(1)}, u32[]{:S(2)}, u32[]{:S(2)}) %collective-permute-start) | collective-permute-done | bytes 294944 | tf_op jit(solution)/shard_map/ppermute | solution.py:1299
  28.1 6.1 %all-to-all-start = ((bf16[8,8,1152]{2,1,0:T(8,128)(2,1)}), bf16[8,8,1152]{2,1,0:T(8,128)(2,1)S(1)}, u32[]{:S(2)}, u32[]{:S(2)}) async-start(bf16[8,8,1152]{2,1,0:T(8,128)(2,1)} %get-tuple-element.138), calls=%async_computation | async-start | bytes 294912 | tf_op jit(solution)/shard_map/all_to_all | solution.py:1406
  35.5 19.6 %all-to-all-done.terms_ref = bf16[8,8,1152]{2,1,0:T(8,128)(2,1)S(1)} async-done(((bf16[8,8,1152]{2,1,0:T(8,128)(2,1)}), bf16[8,8,1152]{2,1,0:T(8,128)(2,1)S(1)}, u32[]{:S(2)}, u32[]{:S(2)}) %all-to-all-start) | async-done | bytes 147488 | tf_op jit(solution)/shard_map/all_to_all | solution.py:1406
  77.6 3.6 %all-to-all-start.1 = ((bf16[8,4,8,1152]{3,2,1,0:T(8,128)(2,1)}), bf16[8,4,8,1152]{3,2,1,0:T(8,128)(2,1)S(1)}, u32[]{:S(2)}, u32[]{:S(2)}) async-start(bf16[8,4,8,1152]{3,2,1,0:T(8,128)(2,1)} %broadcast_in_dim.6), calls=%async_computation.1 | async-start | bytes 1179648 | tf_op jit(solution)/shard_map/all_to_all | solution.py:1319
  81.7 5.6 %collective-permute-done.8.refs_1_ = bf16[4,144,288]{2,1,0:T(8,128)(2,1)} collective-permute-done((bf16[4,144,288]{2,1,0:T(8,128)(2,1)}, bf16[4,144,288]{2,1,0:T(8,128)(2,1)}, u32[]{:S(2)}, u32[]{:S(2)}) %collective-permute-start.8) | collective-permute-done | bytes 331808 | tf_op jit(solution)/shard_map/ppermute | solution.py:1299
  88.1 9.5 %collective-permute-done.10.refs_3_ = bf16[4,144,288]{2,1,0:T(8,128)(2,1)} collective-permute-done((bf16[4,144,288]{2,1,0:T(8,128)(2,1)}, bf16[4,144,288]{2,1,0:T(8,128)(2,1)}, u32[]{:S(2)}, u32[]{:S(2)}) %collective-permute-start.10) | collective-permute-done | bytes 331808 | tf_op jit(solution)/shard_map/ppermute | solution.py:1299
  97.6 5.1 %all-to-all-done.1.modin_ref = bf16[8,4,8,1152]{3,2,1,0:T(8,128)(2,1)S(1)} async-done(((bf16[8,4,8,1152]{3,2,1,0:T(8,128)(2,1)}), bf16[8,4,8,1152]{3,2,1,0:T(8,128)(2,1)S(1)}, u32[]{:S(2)}, u32[]{:S(2)}) %all-to-all-start.1) | async-done | bytes 589856 | tf_op jit(solution)/shard_map/all_to_all | solution.py:1319
  103.6 12.8 %attend.1 = (bf16[144,1024]{1,0:T(8,128)(2,1)}, bf16[1024,512]{1,0:T(8,128)(2,1)}, bf16[1024,128]{1,0:T(8,128)(2,1)}, bf16[32,1024]{1,0:T(8,128)(2,1)}, bf16[115...) custom-call(s32[40]{0:T(128)} %dynamic-slice_bitcast_fusion.place, bf16[4,272,1152]{2,1,0:T(8,128)(2,1)} %copy-done, ...), custom_call_target="tpu_custom_call" | custom-call | flops 1000 | bytes 1000 | tf_op jit(solution)/shard_map/attend/pallas_call | solution.py:1365
  120.0 5.4 %proj.1.refs_13_.refs_10_ = bf16[1152,1152]{1,0:T(8,128)(2,1)} custom-call(s32[40]{0:T(128)} %dynamic-slice_bitcast_fusion.place, bf16[4,144,288]{2,1,0:T(8,128)(2,1)} %slice.83.refs_0_, bf16[4,144,288]{2,1,0:T(8,128)(2,1)} %collective-permute-done.8.refs_1_, bf16[4,144,288]{2,1,0:T(8,128)(2,1)} %collective-permute-done.9.refs_2_, ...), custom_call_target="tpu_custom_call" | custom-call | flops 1000 | bytes 1000 | tf_op jit(solution)/shard_map/proj/pallas_call | solution.py:1365
  127.6 4.9 %collective-permute-done.17.refs_3_ = bf16[144,1024]{1,0:T(8,128)(2,1)S(1)} collective-permute-done((bf16[144,1024]{1,0:T(8,128)(2,1)}, bf16[144,1024]{1,0:T(8,128)(2,1)S(1)}, u32[]{:S(2)}, u32[]{:S(2)}) %collective-permute-start.17) | collective-permute-done | bytes 294944 | tf_op jit(solution)/shard_map/ppermute | solution.py:1299
  136.1 31.8 %mlp.1 = (bf16[4,128,1152]{2,1,0:T(8,128)(2,1)}, bf16[4,128,1152]{2,1,0:T(8,128)(2,1)}, bf16[4,128,1152]{2,1,0:T(8,128)(2,1)}, bf16[4,128,1152]{2,1,0:T(8,128)(2...) custom-call(s32[40]{0:T(128)} %dynamic-slice_bitcast_fusion.place, ...), custom_call_target="tpu_custom_call" | custom-call | flops 1000 | bytes 1000 | tf_op jit(solution)/shard_map/mlp/pallas_call | solution.py:1365
  175.6 5.6 %collective-permute-done.23.refs_1_ = bf16[128,1152]{1,0:T(8,128)(2,1)S(1)} collective-permute-done((bf16[128,1152]{1,0:T(8,128)(2,1)S(1)}, bf16[128,1152]{1,0:T(8,128)(2,1)S(1)}, u32[]{:S(2)}, u32[]{:S(2)}) %collective-permute-start.23) | collective-permute-done | bytes 294944 | tf_op jit(solution)/shard_map/ppermute | solution.py:1299
  182.8 5.9 %collective-permute-done.25.refs_3_ = bf16[128,1152]{1,0:T(8,128)(2,1)S(1)} collective-permute-done((bf16[128,1152]{1,0:T(8,128)(2,1)S(1)}, bf16[128,1152]{1,0:T(8,128)(2,1)S(1)}, u32[]{:S(2)}, u32[]{:S(2)}) %collective-permute-start.25) | collective-permute-done | bytes 294944 | tf_op jit(solution)/shard_map/ppermute | solution.py:1299
  189.4 6.1 %middle.1 = (bf16[2,144,128]{2,1,0:T(8,128)(2,1)}, bf16[2,144,128]{2,1,0:T(8,128)(2,1)}, bf16[2,144,128]{2,1,0:T(8,128)(2,1)}, bf16[2,144,128]{2,1,0:T(8,128)(2,...) custom-call(s32[40]{0:T(128)} %dynamic-slice_bitcast_fusion.place, ...), custom_call_target="tpu_custom_call" | custom-call | flops 1000 | bytes 1000 | tf_op jit(solution)/shard_map/middle/pallas_call | solution.py:1365
  210.0 19.1 %back.1 = (bf16[4,128,1152]{2,1,0:T(8,128)(2,1)}, bf16[4,128,1152]{2,1,0:T(8,128)(2,1)}, bf16[1024,512]{1,0:T(8,128)(2,1)}, bf16[1024,1152]{1,0:T(8,128)(2,1)}, bf16[32,8,1152]{2,1,0:T(8,128)(2,1)}) custom-call(s32[40]{0:T(128)} %dynamic-slice_bitcast_fusion.place, bf16[2,144,128]{2,1,0:T(8,128)(2,1)} %get-tuple-element.197.refs_0_.refs_8_, ...), custom_call_target="tpu_custom_call" | custom-call | flops 1000 | bytes 1000 | tf_op jit(solution)/shard_map/back/pallas_call | solution.py:1365
  230.4 4.8 %all-to-all-start.2 = ((bf16[32,8,1152]{2,1,0:T(8,128)(2,1)}), bf16[32,8,1152]{2,1,0:T(8,128)(2,1)S(1)}, u32[]{:S(2)}, u32[]{:S(2)}) async-start(bf16[32,8,1152]{2,1,0:T(8,128)(2,1)} %get-tuple-element.222), calls=%async_computation.2 | async-start | bytes 1179648 | tf_op jit(solution)/shard_map/all_to_all | solution.py:1580
  239.9 8.0 %weights.1 = bf16[4,1296,128]{2,1,0:T(8,128)(2,1)} custom-call(s32[40]{0:T(128)} %dynamic-slice_bitcast_fusion.place, bf16[144,1024]{1,0:T(8,128)(2,1)} %get-tuple-element.173.refs_0_, bf16[144,1024]{1,0:T(8,128)(2,1)} %copy-done.11, bf16[144,1024]{1,0:T(8,128)(2,1)} %copy-done.12, bf16[144,1024]{1,0:T(8,128)(2,1)} %copy-done.13, ...), custom_call_target="tpu_custom_call" | custom-call | flops 1000 | bytes 1000 | tf_op jit(solution)/shard_map/weights/pallas_call | solution.py:1365
  253.2 4.9 %collective-permute-done.40.gin_3 = bf16[128,1152]{1,0:T(8,128)(2,1)S(1)} collective-permute-done((bf16[128,1152]{1,0:T(8,128)(2,1)S(1)}, bf16[128,1152]{1,0:T(8,128)(2,1)S(1)}, u32[]{:S(2)}, u32[]{:S(2)}) %collective-permute-start.40) | collective-permute-done | bytes 294944 | tf_op jit(solution)/shard_map/ppermute | solution.py:1299
  258.9 3.6 %all-to-all-start.3 = ((bf16[8,144,512]{2,1,0:T(8,128)(2,1)}), bf16[8,144,512]{2,1,0:T(8,128)(2,1)S(1)}, u32[]{:S(2)}, u32[]{:S(2)}) async-start(bf16[8,144,512]{2,1,0:T(8,128)(2,1)} %mlp_split.1), calls=%async_computation.5 | async-start | bytes 2359296 | tf_op jit(solution)/shard_map/all_to_all | solution.py:1585
  270.1 4.0 %input_grad.1 = f32[128,1152]{1,0:T(8,128)} custom-call(s32[40]{0:T(128)} %dynamic-slice_bitcast_fusion.place, bf16[128,1152]{1,0:T(8,128)(2,1)} %get-tuple-element.233.gin_0, bf16[128,1152]{1,0:T(8,128)(2,1)} %copy-done.28, bf16[128,1152]{1,0:T(8,128)(2,1)} %copy-done.29, bf16[128,1152]{1,0:T(8,128)(2,1)} %copy-done.30, bf16[128,1152]{1,0:T(8,128)(2,1)} %bitcast.69, ...), custom_call_target="tpu_custom_call" | custom-call | flops 1000 | bytes 1000 | tf_op jit(solution)/shard_map/input_grad/pallas_call | solution.py:1365
  286.2 3.9 %mlp_join.1 = (f32[144,1152]{1,0:T(8,128)}, f32[288,576]{1,0:T(8,128)}) custom-call(s32[40]{0:T(128)} %dynamic-slice_bitcast_fusion.place, bf16[8,144,512]{2,1,0:T(8,128)(2,1)} %copy-done.1), custom_call_target="tpu_custom_call" | custom-call | flops 1000 | bytes 1000 | tf_op jit(solution)/shard_map/mlp_join/pallas_call | solution.py:1365
  293.3 4.3 %all-to-all-start.5 = ((bf16[8,144,256]{2,1,0:T(8,128)(2,1)}), bf16[8,144,256]{2,1,0:T(8,128)(2,1)S(1)}, u32[]{:S(2)}, u32[]{:S(2)}) async-start(bf16[8,144,256]{2,1,0:T(8,128)(2,1)} %get-tuple-element.252), calls=%async_computation.7 | async-start | bytes 1179648 | tf_op jit(solution)/shard_map/all_to_all | solution.py:1634
  299.6 5.7 %ada.1 = (f32[144,6912]{1,0:T(8,128)}, f32[32,144]{1,0:T(8,128)}, f32[54,128]{1,0:T(8,128)}, f32[18,128]{1,0:T(8,128)}, f32[9,128]{1,0:T(8,128)}, /*index=5*/f32[36,128]{1,0:T(8,128)}, f32[9,128]{1,0:T(8,128)}) custom-call(s32[40]{0:T(128)} %dynamic-slice_bitcast_fusion.place, bf16[8,4,8,1152]{3,2,1,0:T(8,128)(2,1)} %copy-done.6, ...), custom_call_target="tpu_custom_call" | custom-call | flops 1000 | bytes 1000 | tf_op jit(solution)/shard_map/ada/pallas_call | solution.py:1365
  (211 shorter events, 111.8 us)
Async XLA Ops:
  7.2 63.9 %all-gather.7.cloned.1.call-start = ((), (), s32[]{:S(2)}) async-start(), calls=%async_computation.10 | async-start | bytes 2211840 | tf_op jit(solution)/shard_map/all_gather | solution.py:1405
  24.6 43.2 %collective-permute-start.4 = (bf16[272,1152]{1,0:T(8,128)(2,1)S(1)}, bf16[272,1152]{1,0:T(8,128)(2,1)S(1)}, u32[]{:S(2)}, u32[]{:S(2)}) collective-permute-start(bf16[272,1152]{1,0:T(8,128)(2,1)S(1)} %copy-done.2), channel_id=1, source_target_pairs={{0,1},{1,0},{2,3},{3,2},{4,5},{5,4},{6,7},{7,6},{8,9},{9,8},{10,11... | collective-permute-start | bytes 1880072 | tf_op jit(solution)/shard_map/ppermute | solution.py:1299
  26.4 41.5 %collective-permute-start.5 = (bf16[272,1152]{1,0:T(8,128)(2,1)S(1)}, bf16[272,1152]{1,0:T(8,128)(2,1)S(1)}, u32[]{:S(2)}, u32[]{:S(2)}) collective-permute-start(bf16[272,1152]{1,0:T(8,128)(2,1)S(1)} %copy-done.2), channel_id=1, source_target_pairs={{0,16},{16,0},{1,17},{17,1},{2,18},{18,2},{3,19},{19,3},{4,20},{20... | collective-permute-start | bytes 1880072 | tf_op jit(solution)/shard_map/ppermute | solution.py:1299
  27.9 40.0 %collective-permute-start.6 = (bf16[272,1152]{1,0:T(8,128)(2,1)S(1)}, bf16[272,1152]{1,0:T(8,128)(2,1)S(1)}, u32[]{:S(2)}, u32[]{:S(2)}) collective-permute-start(bf16[272,1152]{1,0:T(8,128)(2,1)S(1)} %copy-done.2), channel_id=1, source_target_pairs={{0,17},{1,16},{16,1},{17,0},{2,19},{3,18},{18,3},{19,2},{4,21},{5,... | collective-permute-start | bytes 1880072 | tf_op jit(solution)/shard_map/ppermute | solution.py:1299
  28.1 27.0 %all-to-all-start = ((bf16[8,8,1152]{2,1,0:T(8,128)(2,1)}), bf16[8,8,1152]{2,1,0:T(8,128)(2,1)S(1)}, u32[]{:S(2)}, u32[]{:S(2)}) async-start(bf16[8,8,1152]{2,1,0:T(8,128)(2,1)} %get-tuple-element.138), calls=%async_computation | async-start | bytes 294912 | tf_op jit(solution)/shard_map/all_to_all | solution.py:1406
  34.2 68.6 %all-gather.9.cloned.1.call-start = ((), (), s32[]{:S(2)}) async-start(), calls=%async_computation.11 | async-start | bytes 1474560 | tf_op jit(solution)/shard_map/all_gather | solution.py:1413
  71.0 31.8 %collective-permute-start.7 = (bf16[4,272,1152]{2,1,0:T(8,128)(2,1)S(1)}, bf16[4,272,1152]{2,1,0:T(8,128)(2,1)}, u32[]{:S(2)}, u32[]{:S(2)}) collective-permute-start(bf16[4,272,1152]{2,1,0:T(8,128)(2,1)S(1)} %pad_maximum_fusion.tok_near.refs_8_), channel_id=1, source_target_pairs={{0,8},{8,0},{1,9},{9,1},{2,10},{10,2},{3,11},{11,3},{4,12},{12,4},... | collective-permute-start | bytes 7520264 | tf_op jit(solution)/shard_map/ppermute | solution.py:1299
  76.1 21.5 %collective-permute-start.10 = (bf16[4,144,288]{2,1,0:T(8,128)(2,1)}, bf16[4,144,288]{2,1,0:T(8,128)(2,1)}, u32[]{:S(2)}, u32[]{:S(2)}) collective-permute-start(bf16[4,144,288]{2,1,0:T(8,128)(2,1)} %slice.83.refs_0_), channel_id=1, source_target_pairs={{0,17},{1,16},{16,1},{17,0},{2,19},{3,18},{18,3},{19,2},{4,21},{5,... | collective-permute-start | bytes 995336 | tf_op jit(solution)/shard_map/ppermute | solution.py:1299
  77.6 25.1 %all-to-all-start.1 = ((bf16[8,4,8,1152]{3,2,1,0:T(8,128)(2,1)}), bf16[8,4,8,1152]{3,2,1,0:T(8,128)(2,1)S(1)}, u32[]{:S(2)}, u32[]{:S(2)}) async-start(bf16[8,4,8,1152]{3,2,1,0:T(8,128)(2,1)} %broadcast_in_dim.6), calls=%async_computation.1 | async-start | bytes 1179648 | tf_op jit(solution)/shard_map/all_to_all | solution.py:1319
  81.2 54.1 %all-gather.11.cloned.1.call-start = ((), (), s32[]{:S(2)}) async-start(), calls=%async_computation.12 | async-start | bytes 1474560 | tf_op jit(solution)/shard_map/all_gather | solution.py:1431
  81.3 21.5 %collective-permute-start.11 = (bf16[4,144,288]{2,1,0:T(8,128)(2,1)}, bf16[4,144,288]{2,1,0:T(8,128)(2,1)}, u32[]{:S(2)}, u32[]{:S(2)}) collective-permute-start(bf16[4,144,288]{2,1,0:T(8,128)(2,1)} %slice.83.refs_0_), channel_id=1, source_target_pairs={{0,8},{8,0},{1,9},{9,1},{2,10},{10,2},{3,11},{11,3},{4,12},{12,4},... | collective-permute-start | bytes 995336 | tf_op jit(solution)/shard_map/ppermute | solution.py:1299
  87.3 15.4 %collective-permute-start.12 = (bf16[4,144,288]{2,1,0:T(8,128)(2,1)}, bf16[4,144,288]{2,1,0:T(8,128)(2,1)}, u32[]{:S(2)}, u32[]{:S(2)}) collective-permute-start(bf16[4,144,288]{2,1,0:T(8,128)(2,1)} %collective-permute-done.8.refs_1_), channel_id=1, source_target_pairs={{0,8},{8,0},{1,9},{9,1},{2,10},{10,2},{3,11},{11,3},{4,12},{12,4},... | collective-permute-start | bytes 995336 | tf_op jit(solution)/shard_map/ppermute | solution.py:1299
  102.8 145.1 %reduce-scatter.3.cloned.1.call-start = ((), (), s32[]{:S(2)}) async-start(), calls=%async_computation.8 | async-start | bytes 3686400 | tf_op jit(solution)/shard_map/reduce_scatter | solution.py:1523
  169.2 29.8 %collective-permute-start.33 = (bf16[4,128,1152]{2,1,0:T(8,128)(2,1)S(1)}, bf16[4,128,1152]{2,1,0:T(8,128)(2,1)S(1)}, u32[]{:S(2)}, u32[]{:S(2)}) collective-permute-start(bf16[4,128,1152]{2,1,0:T(8,128)(2,1)S(1)} %copy-done.42), channel_id=1, source_target_pairs={{0,8},{8,0},{1,9},{9,1},{2,10},{10,2},{3,11},{11,3},{4,12},{12,4},... | collective-permute-start | bytes 3538952 | tf_op jit(solution)/shard_map/ppermute | solution.py:1299
  206.2 22.9 %collective-permute-start.34 = (bf16[128,1152]{1,0:T(8,128)(2,1)S(1)}, bf16[128,1152]{1,0:T(8,128)(2,1)S(1)}, u32[]{:S(2)}, u32[]{:S(2)}) collective-permute-start(bf16[128,1152]{1,0:T(8,128)(2,1)S(1)} %get-tuple-element.217), channel_id=1, source_target_pairs={{0,1},{1,0},{2,3},{3,2},{4,5},{5,4},{6,7},{7,6},{8,9},{9,8},{10,11... | collective-permute-start | bytes 884744 | tf_op jit(solution)/shard_map/ppermute | solution.py:1299
  207.1 22.0 %collective-permute-start.35 = (bf16[128,1152]{1,0:T(8,128)(2,1)S(1)}, bf16[128,1152]{1,0:T(8,128)(2,1)S(1)}, u32[]{:S(2)}, u32[]{:S(2)}) collective-permute-start(bf16[128,1152]{1,0:T(8,128)(2,1)S(1)} %get-tuple-element.218), channel_id=1, source_target_pairs={{0,16},{16,0},{1,17},{17,1},{2,18},{18,2},{3,19},{19,3},{4,20},{20... | collective-permute-start | bytes 884744 | tf_op jit(solution)/shard_map/ppermute | solution.py:1299
  209.4 19.8 %collective-permute-start.36 = (bf16[128,1152]{1,0:T(8,128)(2,1)S(1)}, bf16[128,1152]{1,0:T(8,128)(2,1)S(1)}, u32[]{:S(2)}, u32[]{:S(2)}) collective-permute-start(bf16[128,1152]{1,0:T(8,128)(2,1)S(1)} %get-tuple-element.219), channel_id=1, source_target_pairs={{0,17},{1,16},{16,1},{17,0},{2,19},{3,18},{18,3},{19,2},{4,21},{5,... | collective-permute-start | bytes 884744 | tf_op jit(solution)/shard_map/ppermute | solution.py:1299
  230.4 22.8 %all-to-all-start.2 = ((bf16[32,8,1152]{2,1,0:T(8,128)(2,1)}), bf16[32,8,1152]{2,1,0:T(8,128)(2,1)S(1)}, u32[]{:S(2)}, u32[]{:S(2)}) async-start(bf16[32,8,1152]{2,1,0:T(8,128)(2,1)} %get-tuple-element.222), calls=%async_computation.2 | async-start | bytes 1179648 | tf_op jit(solution)/shard_map/all_to_all | solution.py:1580
  235.2 54.9 %reduce-scatter.5.cloned.1.call-start = ((), (), s32[]{:S(2)}) async-start(), calls=%async_computation.9 | async-start | bytes 1658880 | tf_op jit(solution)/shard_map/reduce_scatter | solution.py:1586
  236.4 16.8 %collective-permute-start.38 = (bf16[128,1152]{1,0:T(8,128)(2,1)}, bf16[128,1152]{1,0:T(8,128)(2,1)S(1)}, u32[]{:S(2)}, u32[]{:S(2)}) collective-permute-start(bf16[128,1152]{1,0:T(8,128)(2,1)} %get-tuple-element.265), channel_id=1, source_target_pairs={{0,1},{1,0},{2,3},{3,2},{4,5},{5,4},{6,7},{7,6},{8,9},{9,8},{10,11... | collective-permute-start | bytes 884744 | tf_op jit(solution)/shard_map/ppermute | solution.py:1299
  238.2 15.0 %collective-permute-start.39 = (bf16[128,1152]{1,0:T(8,128)(2,1)S(1)}, bf16[128,1152]{1,0:T(8,128)(2,1)S(1)}, u32[]{:S(2)}, u32[]{:S(2)}) collective-permute-start(bf16[128,1152]{1,0:T(8,128)(2,1)S(1)} %get-tuple-element.264), channel_id=1, source_target_pairs={{0,16},{16,0},{1,17},{17,1},{2,18},{18,2},{3,19},{19,3},{4,20},{20... | collective-permute-start | bytes 884744 | tf_op jit(solution)/shard_map/ppermute | solution.py:1299
  239.6 18.5 %collective-permute-start.40 = (bf16[128,1152]{1,0:T(8,128)(2,1)S(1)}, bf16[128,1152]{1,0:T(8,128)(2,1)S(1)}, u32[]{:S(2)}, u32[]{:S(2)}) collective-permute-start(bf16[128,1152]{1,0:T(8,128)(2,1)S(1)} %get-tuple-element.263), channel_id=1, source_target_pairs={{0,17},{1,16},{16,1},{17,0},{2,19},{3,18},{18,3},{19,2},{4,21},{5,... | collective-permute-start | bytes 884744 | tf_op jit(solution)/shard_map/ppermute | solution.py:1299
  258.9 19.4 %all-to-all-start.3 = ((bf16[8,144,512]{2,1,0:T(8,128)(2,1)}), bf16[8,144,512]{2,1,0:T(8,128)(2,1)S(1)}, u32[]{:S(2)}, u32[]{:S(2)}) async-start(bf16[8,144,512]{2,1,0:T(8,128)(2,1)} %mlp_split.1), calls=%async_computation.5 | async-start | bytes 2359296 | tf_op jit(solution)/shard_map/all_to_all | solution.py:1585
  293.3 15.4 %all-to-all-start.5 = ((bf16[8,144,256]{2,1,0:T(8,128)(2,1)}), bf16[8,144,256]{2,1,0:T(8,128)(2,1)S(1)}, u32[]{:S(2)}, u32[]{:S(2)}) async-start(bf16[8,144,256]{2,1,0:T(8,128)(2,1)} %get-tuple-element.252), calls=%async_computation.7 | async-start | bytes 1179648 | tf_op jit(solution)/shard_map/all_to_all | solution.py:1634
  (76 other events, 436.4 us)
Sparse Core Ops, SparseCore 0:
  12.5 47.0 all-gather.6
  71.2 31.4 all-gather.8
  104.3 29.6 all-gather.10
  168.1 56.8 reduce-scatter.2
  258.3 31.7 reduce-scatter.4
